TPU v7x, 256 devices: a whole 4x4x8 slice. The times are simulated.
256 devices in a mesh: gx: 16 (over x, y_lo, core), gy: 16 (over z, y_hi).
Axes of the slice: x: 4, y: 4 (y_hi: 2, y_lo: 2; y = y_hi * 2 + y_lo), z: 8, core: 2. Of those that a mesh axis runs over, the one named last changes fastest.
Arguments:
- positions: float32 [3, 16, 16, 16384], P(None, 'gx', 'gy'), may hold values from 0 to 2
- velocities: float32 [3, 16, 16, 16384], P(None, 'gx', 'gy'), may hold values from -6 to 6
- charges: float32 [16, 16, 16384], P('gx', 'gy'), may hold values from -1 to 1
- repel_root: float32 [16, 16, 16384], P('gx', 'gy'), may hold values from 0.001 to 0.01
- disperse_root: float32 [16, 16, 16384], P('gx', 'gy'), may hold values from 0.02 to 0.2
- inverse_mass: float32 [16, 16, 16384], P('gx', 'gy'), may hold values from 0.06 to 1
- move: int32 [16, 16, 128], P('gx', 'gy'), may hold values from 0 to 8, as said below
- tiles: int32 [16, 16, 2304, 2], P('gx', 'gy'), may hold values from 0 to 575
Outputs:
- new_positions: float32 [3, 16, 16, 18432], P(None, 'gx', 'gy')
- new_velocities: float32 [3, 16, 16, 18432], P(None, 'gx', 'gy')
- forces: float32 [3, 16, 16, 18432], P(None, 'gx', 'gy')
Inputs may be any that keep to these rules, and one draw needn't show every extreme that they name: `move`: on every owner at most 2 blocks carry any one code from 1 to 8, so an owner receives at most 144 blocks; in every draw some owner sends exactly 2 blocks toward a neighbour and some owner receives exactly 144.
All inputs are finite; a program needn't handle non-finite values.
Results may differ from a plain program's by a relative error of at most 0.0003.
Values sent between devices are 32-bit elements; how exact they have to be, the bound alone decides.
No kernel may reach another device: no remote copies, remote signals or barrier semaphores. Data moves between devices by JAX's collectives and lax.ppermute only.
A program may use at most 128 MiB of HBM per device.

v0:
```python
import functools

import jax
import jax.numpy as jnp
from jax import lax
from jax.experimental import pallas as pl
from jax.experimental.pallas import tpu as pltpu
from jax.sharding import PartitionSpec as P

BLOCK = 128
NB = 128
CAPACITY = 144
CELL = 2.0
TSTEP = 0.05
OFFSETS = ((0, 0), (1, 0), (-1, 0), (0, 1), (0, -1), (1, 1), (1, -1), (-1, 1), (-1, -1))
RECIP_GAP = (
    0.004694723058491945,
    5.942236423492432,
    -13.92039680480957,
    18.602458953857422,
    -16.470346450805664,
    9.659473419189453,
    -3.41253399848938,
    0.5484030246734619,
)


def passed_along(value, step_x, step_y):
    nx, ny = lax.axis_size("gx"), lax.axis_size("gy")
    if step_y == 0:
        return lax.ppermute(value, "gx", [(s, (s + step_x) % nx) for s in range(nx)])
    if step_x == 0:
        return lax.ppermute(value, "gy", [(s, (s + step_y) % ny) for s in range(ny)])
    pairs = [
        (i * ny + j, ((i + step_x) % nx) * ny + (j + step_y) % ny)
        for i in range(nx)
        for j in range(ny)
    ]
    return lax.ppermute(value, ("gx", "gy"), pairs)


def pack_kernel(move, pos, vel, chg, rep, dis, inv, stay, parcels, staying, tally):
    zero = jnp.zeros((8, BLOCK), jnp.float32)
    for f in range(10):
        for u in range(CAPACITY // 8):
            stay[f, 8 * u : 8 * u + 8, :] = zero
    for p in range(9):
        for u in range(3):
            parcels[p, 8 * u : 8 * u + 8, :] = zero
        tally[p] = 0

    def rows(k):
        at = pl.ds(k, 1)
        return [pos[d, at, :] for d in range(3)] + [vel[d, at, :] for d in range(3)] + [
            ref[at, :] for ref in (chg, rep, dis, inv)
        ]

    def one(k, kept):
        code = move[k]
        values = rows(k)
        for f in range(10):
            stay[f, pl.ds(kept, 1), :] = values[f]
        seen = tally[code]
        tally[code] = seen + 1
        slot = jnp.where(code == 0, 0, jnp.minimum(seen, 1)) * 10
        for f in range(10):
            parcels[code, pl.ds(slot + f, 1), :] = values[f]
        return kept + jnp.where(code == 0, 1, 0)

    kept = lax.fori_loop(0, NB, one, 0)
    for f in range(10):
        stay[f, pl.ds(kept, 1), :] = zero[0:1]
    staying[0] = kept
    for code in range(1, 9):
        step_x, step_y = OFFSETS[code]
        for n in range(2):
            if step_x != 0:
                parcels[code, 10 * n : 10 * n + 1, :] = parcels[code, 10 * n : 10 * n + 1, :] - step_x * CELL
            if step_y != 0:
                parcels[code, 10 * n + 1 : 10 * n + 2, :] = parcels[code, 10 * n + 1 : 10 * n + 2, :] - step_y * CELL
        parcels[code, 20:21, :] = jnp.broadcast_to(tally[code], (1, BLOCK)).astype(jnp.float32)


def arrive_kernel(staying, stay, *refs):
    parcels, coords, rest, held = refs[:8], refs[8], refs[9], refs[10]
    for f in range(10):
        held[f, 0:CAPACITY, :] = stay[f]
    counts = jnp.concatenate([p[20:21, :] for p in parcels], axis=0).astype(jnp.int32)
    at = staying[0]
    for code in range(8):
        count = counts[code, 0]
        for n in range(2):
            for f in range(10):
                held[f, pl.ds(at, 1), :] = parcels[code][10 * n + f : 10 * n + f + 1, :]
            at = at + jnp.where(count > n, 1, 0)
    for f in range(10):
        held[f, pl.ds(at, 1), :] = jnp.zeros((1, BLOCK), jnp.float32)
    for k, f in enumerate((0, 1, 2, 6, 7, 8)):
        coords[k] = held[f, 0:CAPACITY, :]
    for k, f in enumerate((3, 4, 5, 9)):
        rest[k] = held[f, 0:CAPACITY, :]


def update_kernel(home, east, north, corner, coords, rest, new_x, new_v, total):
    for d in range(3):
        force = home[d] + east[d] + north[d] + corner[d]
        fresh = rest[d] + TSTEP * rest[3] * force
        total[d] = force
        new_v[d] = fresh
        new_x[d] = coords[d] + TSTEP * fresh


def listed(b):
    return (b // 8) * 256 + (b % 8) * 16


def pair_kernel(tiles, home, east, north, corner, fh, fe, fn, fc, zone, ac0, ac1, ac2, ibuf0, ibuf1, vbuf0, vbuf1, wbuf, *, T=2, mxu=True):
    acc=(ac0,ac1,ac2)
    sub = lax.broadcasted_iota(jnp.int32,(8,128),0)
    lane = lax.broadcasted_iota(jnp.int32,(8,128),1)
    rel = lane//4 - sub//4
    for c in range(16):
        wbuf[c]=jnp.where(rel==2*c,0.0,1.0)
    wbuf[16]=jnp.ones((8,128),jnp.float32)
    for z,(ref,sx,sy) in enumerate(((home,0.,0.),(east,2.,0.),(north,0.,2.),(corner,2.,2.))):
        for f in range(6):
            v = ref[f]
            if f==0 and sx: v=v+sx
            if f==1 and sy: v=v+sy
            zone[f, pl.ds(z*CAPACITY,CAPACITY), :] = v
    zero = jnp.zeros((8,128),jnp.float32)
    def clear(k,_):
        for u in range(16):
            for d in range(3):
                acc[d][pl.ds(pl.multiple_of(k*128,128)+8*u,8),:]=zero
        return 0
    lax.fori_loop(0,(4*CAPACITY)//16,clear,0)

    def row(f,j):
        return jnp.broadcast_to(zone[f, pl.ds(j,1), :],(8,128))
    SC=jnp.where(sub==4,12.0,jnp.where(sub==5,6.0,1.0)).astype(jnp.float32)
    kk=lax.broadcasted_iota(jnp.int32,(24,768),0); nn=lax.broadcasted_iota(jnp.int32,(24,768),1)
    pick=jnp.where(kk%8==nn//128,1.0,0.0).astype(jnp.bfloat16)

    def spread(b,ibuf):
        feat = jnp.concatenate([home[f, pl.ds(b,1), :] for f in range(6)]+[jnp.zeros((2,128),jnp.float32)],axis=0)*SC
        hi=feat.astype(jnp.bfloat16).astype(jnp.float32); r=feat-hi
        mid=r.astype(jnp.bfloat16).astype(jnp.float32); lo=r-mid
        ft=jnp.concatenate([hi,mid,lo],axis=0).T.astype(jnp.bfloat16)
        out=jnp.dot(ft,pick,preferred_element_type=jnp.float32)
        for f in range(6):
            for c in range(16): ibuf[f,c]=out[8*c:8*c+8,128*f:128*f+128]

    def settle(b,vbuf):
        tots=[]
        for c in range(16):
            tot=None
            for t in range(T):
                j8=pl.multiple_of(tiles[listed(b) + (128 * t + c)]*8,8)
                v=[vbuf[d,t,c] for d in range(3)]
                for d in range(3):
                    acc[d][pl.ds(j8,8),:]=acc[d][pl.ds(j8,8),:]+v[d]
                tot=v if tot is None else [p+q for p,q in zip(tot,v)]
            tots.append(tot)
        cc=[]
        for c in range(16):
            r=[jnp.sum(tots[c][d],axis=1,keepdims=True) for d in range(3)]
            cc.append(jnp.where(lane==0,r[0],jnp.where(lane==1,r[1],r[2])))
        m=jnp.concatenate(cc,axis=0)[:, :8].T
        for d in range(3):
            fh[d,pl.ds(b,1),:]=m[d:d+1]

    def block(b,ibuf,vbuf):
        for c in range(16):
            xi,yi,zi,qi,ai,bi=[ibuf[f,c] for f in range(6)]
            for t in range(T):
                j=tiles[listed(b) + (128 * t + c)]
                dx=xi-row(0,j); dy=yi-row(1,j); dz=zi-row(2,j)
                r2=dx*dx+dy*dy+dz*dz
                w=jnp.maximum(wbuf[jnp.where(j==b,c,16)]-r2,0.0)
                s=jnp.clip(r2,0.25,1.0)
                rs=lax.rsqrt(s)
                inv=rs*rs
                cube=inv*inv*inv
                h=RECIP_GAP[-1]
                for n in range(len(RECIP_GAP)-2,-1,-1):
                    h=h*s+RECIP_GAP[n]
                g=(qi*row(3,j))*(rs-h)+cube*((ai*row(4,j))*cube-bi*row(5,j))
                g=g*(inv*(w*w))
                vbuf[0,t,c]=g*dx
                vbuf[1,t,c]=g*dy
                vbuf[2,t,c]=g*dz

    spread(0,ibuf0)
    for d in range(3):
        for t in range(T):
            for c in range(16): vbuf1[d,t,c]=zero
    def two(k,_):
        b=2*k
        settle(jnp.maximum(b-1,0),vbuf1)
        spread(b+1,ibuf1)
        block(b,ibuf0,vbuf0)
        settle(b,vbuf0)
        spread(jnp.minimum(b+2,CAPACITY-1),ibuf0)
        block(b+1,ibuf1,vbuf1)
        return 0
    lax.fori_loop(0,CAPACITY//2,two,0)
    settle(CAPACITY-1,vbuf1)
    for d in range(3):
        for z,ref in enumerate((fh,fe,fn,fc)):
            def red(k,_):
                for u in range(3):
                    k8=pl.multiple_of(k*24+8*u,8)
                    r=[acc[d][pl.ds((z*CAPACITY+k8)*8+q,8,stride=8),:] for q in range(8)]
                    r=((r[0]+r[1])+(r[2]+r[3]))+((r[4]+r[5])+(r[6]+r[7]))
                    if z==0: ref[d,pl.ds(k8,8),:]=ref[d,pl.ds(k8,8),:]-r
                    else: ref[d,pl.ds(k8,8),:]=-r
                return 0
            lax.fori_loop(0,CAPACITY//24,red,0)


VM = pl.BlockSpec(memory_space=pltpu.VMEM)
SM = pl.BlockSpec(memory_space=pltpu.SMEM)
PARAMS = pltpu.CompilerParams(vmem_limit_bytes=48 * 1024 * 1024)


def planes(count, rows=CAPACITY):
    return jax.ShapeDtypeStruct((count, rows, BLOCK), jnp.float32)


def body(positions, velocities, charges, repel_root, disperse_root, inverse_mass, move, tiles):
    stay, parcels, staying = pl.pallas_call(
        pack_kernel,
        out_shape=(planes(10), planes(9, 24), jax.ShapeDtypeStruct((1,), jnp.int32)),
        in_specs=[SM] + [VM] * 6,
        out_specs=(VM, VM, SM),
        scratch_shapes=[pltpu.SMEM((9,), jnp.int32)],
        compiler_params=PARAMS,
        name="pack",
    )(
        move.reshape(NB),
        positions.reshape(3, NB, BLOCK),
        velocities.reshape(3, NB, BLOCK),
        charges.reshape(NB, BLOCK),
        repel_root.reshape(NB, BLOCK),
        disperse_root.reshape(NB, BLOCK),
        inverse_mass.reshape(NB, BLOCK),
    )
    arrived = [passed_along(parcels[code], *OFFSETS[code]) for code in range(1, 9)]
    coords, rest = pl.pallas_call(
        arrive_kernel,
        out_shape=(planes(6), planes(4)),
        in_specs=[SM] + [VM] * 9,
        out_specs=(VM, VM),
        scratch_shapes=[pltpu.VMEM((10, CAPACITY + 8, BLOCK), jnp.float32)],
        compiler_params=PARAMS,
        name="arrive",
    )(staying, stay, *arrived)
    east = passed_along(coords, -1, 0)
    north = passed_along(coords, 0, -1)
    corner = passed_along(coords, -1, -1)
    on_home, on_east, on_north, on_corner = pl.pallas_call(
        pair_kernel,
        out_shape=(planes(3),) * 4,
        in_specs=[SM] + [VM] * 4,
        out_specs=(VM,) * 4,
        scratch_shapes=[pltpu.VMEM((6,4 * CAPACITY,128),jnp.float32)]+[pltpu.VMEM((4 * CAPACITY*8,128),jnp.float32)]*3+[pltpu.VMEM((6,16,8,128),jnp.float32)]*2+[pltpu.VMEM((3,2,16,8,128),jnp.float32)]*2+[pltpu.VMEM((17,8,128),jnp.float32)],
        compiler_params=PARAMS,
        name="pair",
    )(tiles.reshape(18, 128, 2).transpose(0, 2, 1).reshape(-1), coords, east, north, corner)
    from_east = passed_along(on_east, 1, 0)
    from_north = passed_along(on_north, 0, 1)
    from_corner = passed_along(on_corner, 1, 1)
    out = pl.pallas_call(
        update_kernel,
        out_shape=(planes(3),) * 3,
        in_specs=[VM] * 6,
        out_specs=(VM,) * 3,
        compiler_params=PARAMS,
        name="update",
    )(on_home, from_east, from_north, from_corner, coords, rest)
    return tuple(value.reshape(3, 1, 1, CAPACITY * BLOCK) for value in out)


def solution(mesh):
    vector = P(None, "gx", "gy", None)
    scalar = P("gx", "gy", None)
    return jax.shard_map(
        body,
        mesh=mesh,
        in_specs=(vector, vector) + (scalar,) * 5 + (P("gx", "gy", None, None),),
        out_specs=(vector,) * 3,
        check_vma=False,
    )
```

profile of v0, /device:TPU:0, one launch (start us, length us, event | category | flops | bytes accessed | tf_op | source)
XLA Modules:
  0.0 131.3 jit_solution(13068263355882773120)
XLA Ops:
  0.6 0.6 copy-done.6
  1.3 0.9 copy-done
  2.2 0.9 copy-done.1
  3.1 0.8 copy-done.2
  4.0 0.8 copy-done.3
  4.8 0.8 copy-done.4
  5.7 0.8 copy-done.5
  6.5 2.8 %pack.1 = (f32[10,144,128]{2,1,0:T(8,128)S(1)}, f32[9,24,128]{2,1,0:T(8,128)S(1)}, s32[1]{0:T(128)}) custom-call(s32[128]{0:T(128)S(1)} %bitcast.37, f32[3,128,128]{2,1,0:T(8,128)S(1)} %bitcast.31, f32[3,128,128]{2,1,0:T(8,128)S(1)} %bitcast.32, f32[128,128]{1,0:T(8,128)S(1)} %bitcast.33, f32[128,128]{1,0:T(8,128)S(1)} %bitcast.34, f32[128,128]{1,0:T(8,128)S(1)} %bitcast.35, ...), custom_call_target="tpu_custom_call" | custom-call | tf_op jit(solution)/shard_map/pack/pallas_call | solution.py:232
  9.3 8.3 %collective-permute-start.7 = (f32[24,128]{1,0:T(8,128)S(1)}, f32[24,128]{1,0:T(8,128)S(1)}, u32[]{:S(2)}, u32[]{:S(2)}) collective-permute-start(f32[24,128]{1,0:T(8,128)S(1)} %get-tuple-element.33), channel_id=1, source_target_pairs={{0,255},{1,240},{2,241},{3,242},{4,243},{5,244},{6,245},{7,246},{8... | collective-permute-start | bytes 36872 | tf_op jit(solution)/shard_map/ppermute | solution.py:39
  17.6 0.0 collective-permute-start.6
  17.6 5.4 %collective-permute-start.5 = (f32[24,128]{1,0:T(8,128)S(1)}, f32[24,128]{1,0:T(8,128)S(1)}, u32[]{:S(2)}, u32[]{:S(2)}) collective-permute-start(f32[24,128]{1,0:T(8,128)S(1)} %get-tuple-element.35), channel_id=1, source_target_pairs={{0,31},{1,16},{2,17},{3,18},{4,19},{5,20},{6,21},{7,22},{8,23},{9,... | collective-permute-start | bytes 36872 | tf_op jit(solution)/shard_map/ppermute | solution.py:39
  23.0 0.0 collective-permute-start.4
  23.0 3.6 %collective-permute-start.3 = (f32[24,128]{1,0:T(8,128)S(1)}, f32[24,128]{1,0:T(8,128)S(1)}, u32[]{:S(2)}, u32[]{:S(2)}) collective-permute-start(f32[24,128]{1,0:T(8,128)S(1)} %get-tuple-element.37), channel_id=1, source_target_pairs={{0,15},{1,0},{2,1},{3,2},{4,3},{5,4},{6,5},{7,6},{8,7},{9,8},{10,9... | collective-permute-start | bytes 36872 | tf_op jit(solution)/shard_map/ppermute | solution.py:33
  26.6 0.0 collective-permute-done.7.refs_7_
  26.6 4.2 %collective-permute-start.1 = (f32[24,128]{1,0:T(8,128)S(1)}, f32[24,128]{1,0:T(8,128)S(1)}, u32[]{:S(2)}, u32[]{:S(2)}) collective-permute-start(f32[24,128]{1,0:T(8,128)S(1)} %get-tuple-element.39), channel_id=1, source_target_pairs={{0,240},{16,0},{32,16},{48,32},{64,48},{80,64},{96,80},{112,96},{1... | collective-permute-start | bytes 36872 | tf_op jit(solution)/shard_map/ppermute | solution.py:31
  30.8 0.0 collective-permute-start
  30.8 0.7 collective-permute-done.4.refs_4_
  31.5 2.4 %collective-permute-done.2.refs_2_ = f32[24,128]{1,0:T(8,128)S(1)} collective-permute-done((f32[24,128]{1,0:T(8,128)S(1)}, f32[24,128]{1,0:T(8,128)S(1)}, u32[]{:S(2)}, u32[]{:S(2)}) %collective-permute-start.2) | collective-permute-done | bytes 12320 | tf_op jit(solution)/shard_map/ppermute | solution.py:33
  33.9 2.2 %collective-permute-done.refs_0_ = f32[24,128]{1,0:T(8,128)S(1)} collective-permute-done((f32[24,128]{1,0:T(8,128)S(1)}, f32[24,128]{1,0:T(8,128)S(1)}, u32[]{:S(2)}, u32[]{:S(2)}) %collective-permute-start) | collective-permute-done | bytes 12320 | tf_op jit(solution)/shard_map/ppermute | solution.py:31
  36.1 0.8 arrive.1
  37.0 4.5 %collective-permute-start.10 = (f32[6,144,128]{2,1,0:T(8,128)S(1)}, f32[6,144,128]{2,1,0:T(8,128)S(1)}, u32[]{:S(2)}, u32[]{:S(2)}) collective-permute-start(f32[6,144,128]{2,1,0:T(8,128)S(1)} %get-tuple-element.18.home.coords), channel_id=1, source_target_pairs={{0,255},{1,240},{2,241},{3,242},{4,243},{5,244},{6,245},{7,246},{8... | collective-permute-start | bytes 1327112 | tf_op jit(solution)/shard_map/ppermute | solution.py:39
  41.5 1.6 %collective-permute-start.9 = (f32[6,144,128]{2,1,0:T(8,128)S(1)}, f32[6,144,128]{2,1,0:T(8,128)S(1)}, u32[]{:S(2)}, u32[]{:S(2)}) collective-permute-start(f32[6,144,128]{2,1,0:T(8,128)S(1)} %get-tuple-element.18.home.coords), channel_id=1, source_target_pairs={{0,15},{1,0},{2,1},{3,2},{4,3},{5,4},{6,5},{7,6},{8,7},{9,8},{10,9... | collective-permute-start | bytes 1327112 | tf_op jit(solution)/shard_map/ppermute | solution.py:33
  43.0 0.0 collective-permute-start.8
  43.1 8.1 %collective-permute-done.10.corner = f32[6,144,128]{2,1,0:T(8,128)S(1)} collective-permute-done((f32[6,144,128]{2,1,0:T(8,128)S(1)}, f32[6,144,128]{2,1,0:T(8,128)S(1)}, u32[]{:S(2)}, u32[]{:S(2)}) %collective-permute-start.10) | collective-permute-done | bytes 442400 | tf_op jit(solution)/shard_map/ppermute | solution.py:39
  51.2 9.5 %collective-permute-done.9.north = f32[6,144,128]{2,1,0:T(8,128)S(1)} collective-permute-done((f32[6,144,128]{2,1,0:T(8,128)S(1)}, f32[6,144,128]{2,1,0:T(8,128)S(1)}, u32[]{:S(2)}, u32[]{:S(2)}) %collective-permute-start.9) | collective-permute-done | bytes 442400 | tf_op jit(solution)/shard_map/ppermute | solution.py:33
  60.7 49.4 %pair.1 = (f32[3,144,128]{2,1,0:T(8,128)S(1)}, f32[3,144,128]{2,1,0:T(8,128)S(1)}, f32[3,144,128]{2,1,0:T(8,128)S(1)}, f32[3,144,128]{2,1,0:T(8,128)S(1)}) custom-call(s32[4608]{0:T(1024)S(1)} %reshape.43.tiles, f32[6,144,128]{2,1,0:T(8,128)S(1)} %get-tuple-element.18.home.coords, f32[6,144,128]{2,1,0:T(8,128)S(1)} %collective-permute-done.8.east, ...), custom_call_target="tpu_custom_call" | custom-call | tf_op jit(solution)/shard_map/pair/pallas_call | solution.py:262
  110.1 1.0 collective-permute-start.11
  111.2 1.3 collective-permute-start.12
  112.4 6.3 %collective-permute-done.11.east = f32[3,144,128]{2,1,0:T(8,128)S(1)} collective-permute-done((f32[3,144,128]{2,1,0:T(8,128)S(1)}, f32[3,144,128]{2,1,0:T(8,128)S(1)}, u32[]{:S(2)}, u32[]{:S(2)}) %collective-permute-start.11) | collective-permute-done | bytes 221216 | tf_op jit(solution)/shard_map/ppermute | solution.py:31
  118.8 4.4 %collective-permute-done.12.north = f32[3,144,128]{2,1,0:T(8,128)S(1)} collective-permute-done((f32[3,144,128]{2,1,0:T(8,128)S(1)}, f32[3,144,128]{2,1,0:T(8,128)S(1)}, u32[]{:S(2)}, u32[]{:S(2)}) %collective-permute-start.12) | collective-permute-done | bytes 221216 | tf_op jit(solution)/shard_map/ppermute | solution.py:33
  123.2 7.1 %collective-permute-done.13.corner = f32[3,144,128]{2,1,0:T(8,128)S(1)} collective-permute-done((f32[3,144,128]{2,1,0:T(8,128)S(1)}, f32[3,144,128]{2,1,0:T(8,128)S(1)}, u32[]{:S(2)}, u32[]{:S(2)}) %collective-permute-start.13) | collective-permute-done | bytes 221216 | tf_op jit(solution)/shard_map/ppermute | solution.py:39
  130.3 0.9 update.1
  (20 shorter events, 0.1 us)
Async XLA Ops:
  0.6 0.7 copy-start.6
  1.3 0.9 copy-start
  2.2 0.9 copy-start.1
  3.1 0.8 copy-start.2
  4.0 0.8 copy-start.3
  4.8 0.8 copy-start.4
  5.7 0.8 copy-start.5
  9.3 17.3 %collective-permute-start.7 = (f32[24,128]{1,0:T(8,128)S(1)}, f32[24,128]{1,0:T(8,128)S(1)}, u32[]{:S(2)}, u32[]{:S(2)}) collective-permute-start(f32[24,128]{1,0:T(8,128)S(1)} %get-tuple-element.33), channel_id=1, source_target_pairs={{0,255},{1,240},{2,241},{3,242},{4,243},{5,244},{6,245},{7,246},{8... | collective-permute-start | bytes 36872 | tf_op jit(solution)/shard_map/ppermute | solution.py:39
  17.6 9.0 %collective-permute-start.6 = (f32[24,128]{1,0:T(8,128)S(1)}, f32[24,128]{1,0:T(8,128)S(1)}, u32[]{:S(2)}, u32[]{:S(2)}) collective-permute-start(f32[24,128]{1,0:T(8,128)S(1)} %get-tuple-element.34), channel_id=1, source_target_pairs={{0,241},{1,242},{2,243},{3,244},{4,245},{5,246},{6,247},{7,248},{8... | collective-permute-start | bytes 36872 | tf_op jit(solution)/shard_map/ppermute | solution.py:39
  17.6 13.2 %collective-permute-start.5 = (f32[24,128]{1,0:T(8,128)S(1)}, f32[24,128]{1,0:T(8,128)S(1)}, u32[]{:S(2)}, u32[]{:S(2)}) collective-permute-start(f32[24,128]{1,0:T(8,128)S(1)} %get-tuple-element.35), channel_id=1, source_target_pairs={{0,31},{1,16},{2,17},{3,18},{4,19},{5,20},{6,21},{7,22},{8,23},{9,... | collective-permute-start | bytes 36872 | tf_op jit(solution)/shard_map/ppermute | solution.py:39
  23.0 8.6 %collective-permute-start.4 = (f32[24,128]{1,0:T(8,128)S(1)}, f32[24,128]{1,0:T(8,128)S(1)}, u32[]{:S(2)}, u32[]{:S(2)}) collective-permute-start(f32[24,128]{1,0:T(8,128)S(1)} %get-tuple-element.36), channel_id=1, source_target_pairs={{0,17},{1,18},{2,19},{3,20},{4,21},{5,22},{6,23},{7,24},{8,25},{9,... | collective-permute-start | bytes 36872 | tf_op jit(solution)/shard_map/ppermute | solution.py:39
  23.0 8.6 %collective-permute-start.3 = (f32[24,128]{1,0:T(8,128)S(1)}, f32[24,128]{1,0:T(8,128)S(1)}, u32[]{:S(2)}, u32[]{:S(2)}) collective-permute-start(f32[24,128]{1,0:T(8,128)S(1)} %get-tuple-element.37), channel_id=1, source_target_pairs={{0,15},{1,0},{2,1},{3,2},{4,3},{5,4},{6,5},{7,6},{8,7},{9,8},{10,9... | collective-permute-start | bytes 36872 | tf_op jit(solution)/shard_map/ppermute | solution.py:33
  26.6 7.3 %collective-permute-start.2 = (f32[24,128]{1,0:T(8,128)S(1)}, f32[24,128]{1,0:T(8,128)S(1)}, u32[]{:S(2)}, u32[]{:S(2)}) collective-permute-start(f32[24,128]{1,0:T(8,128)S(1)} %get-tuple-element.38), channel_id=1, source_target_pairs={{0,1},{1,2},{2,3},{3,4},{4,5},{5,6},{6,7},{7,8},{8,9},{9,10},{10,1... | collective-permute-start | bytes 36872 | tf_op jit(solution)/shard_map/ppermute | solution.py:33
  26.6 7.3 %collective-permute-start.1 = (f32[24,128]{1,0:T(8,128)S(1)}, f32[24,128]{1,0:T(8,128)S(1)}, u32[]{:S(2)}, u32[]{:S(2)}) collective-permute-start(f32[24,128]{1,0:T(8,128)S(1)} %get-tuple-element.39), channel_id=1, source_target_pairs={{0,240},{16,0},{32,16},{48,32},{64,48},{80,64},{96,80},{112,96},{1... | collective-permute-start | bytes 36872 | tf_op jit(solution)/shard_map/ppermute | solution.py:31
  30.8 5.3 %collective-permute-start = (f32[24,128]{1,0:T(8,128)S(1)}, f32[24,128]{1,0:T(8,128)S(1)}, u32[]{:S(2)}, u32[]{:S(2)}) collective-permute-start(f32[24,128]{1,0:T(8,128)S(1)} %get-tuple-element.40), channel_id=1, source_target_pairs={{0,16},{16,32},{32,48},{48,64},{64,80},{80,96},{96,112},{112,128},... | collective-permute-start | bytes 36872 | tf_op jit(solution)/shard_map/ppermute | solution.py:31
  36.1 6.9 %copy-start.7 = (s32[1,1,2304,2]{2,3,1,0:T(2,128)S(1)}, s32[1,1,2304,2]{2,3,1,0:T(2,128)}, u32[]{:S(2)}) copy-start(s32[1,1,2304,2]{2,3,1,0:T(2,128)} %param.15) | copy-start | bytes 55300
  37.0 14.2 %collective-permute-start.10 = (f32[6,144,128]{2,1,0:T(8,128)S(1)}, f32[6,144,128]{2,1,0:T(8,128)S(1)}, u32[]{:S(2)}, u32[]{:S(2)}) collective-permute-start(f32[6,144,128]{2,1,0:T(8,128)S(1)} %get-tuple-element.18.home.coords), channel_id=1, source_target_pairs={{0,255},{1,240},{2,241},{3,242},{4,243},{5,244},{6,245},{7,246},{8... | collective-permute-start | bytes 1327112 | tf_op jit(solution)/shard_map/ppermute | solution.py:39
  41.5 19.2 %collective-permute-start.9 = (f32[6,144,128]{2,1,0:T(8,128)S(1)}, f32[6,144,128]{2,1,0:T(8,128)S(1)}, u32[]{:S(2)}, u32[]{:S(2)}) collective-permute-start(f32[6,144,128]{2,1,0:T(8,128)S(1)} %get-tuple-element.18.home.coords), channel_id=1, source_target_pairs={{0,15},{1,0},{2,1},{3,2},{4,3},{5,4},{6,5},{7,6},{8,7},{9,8},{10,9... | collective-permute-start | bytes 1327112 | tf_op jit(solution)/shard_map/ppermute | solution.py:33
  43.0 17.6 %collective-permute-start.8 = (f32[6,144,128]{2,1,0:T(8,128)S(1)}, f32[6,144,128]{2,1,0:T(8,128)S(1)}, u32[]{:S(2)}, u32[]{:S(2)}) collective-permute-start(f32[6,144,128]{2,1,0:T(8,128)S(1)} %get-tuple-element.18.home.coords), channel_id=1, source_target_pairs={{0,240},{16,0},{32,16},{48,32},{64,48},{80,64},{96,80},{112,96},{1... | collective-permute-start | bytes 1327112 | tf_op jit(solution)/shard_map/ppermute | solution.py:31
  110.1 8.6 %collective-permute-start.11 = (f32[3,144,128]{2,1,0:T(8,128)S(1)}, f32[3,144,128]{2,1,0:T(8,128)S(1)}, u32[]{:S(2)}, u32[]{:S(2)}) collective-permute-start(f32[3,144,128]{2,1,0:T(8,128)S(1)} %get-tuple-element.20), channel_id=1, source_target_pairs={{0,16},{16,32},{32,48},{48,64},{64,80},{80,96},{96,112},{112,128},... | collective-permute-start | bytes 663560 | tf_op jit(solution)/shard_map/ppermute | solution.py:31
  111.2 12.0 %collective-permute-start.12 = (f32[3,144,128]{2,1,0:T(8,128)S(1)}, f32[3,144,128]{2,1,0:T(8,128)S(1)}, u32[]{:S(2)}, u32[]{:S(2)}) collective-permute-start(f32[3,144,128]{2,1,0:T(8,128)S(1)} %get-tuple-element.21), channel_id=1, source_target_pairs={{0,1},{1,2},{2,3},{3,4},{4,5},{5,6},{6,7},{7,8},{8,9},{9,10},{10,1... | collective-permute-start | bytes 663560 | tf_op jit(solution)/shard_map/ppermute | solution.py:33
  112.4 17.9 %collective-permute-start.13 = (f32[3,144,128]{2,1,0:T(8,128)S(1)}, f32[3,144,128]{2,1,0:T(8,128)S(1)}, u32[]{:S(2)}, u32[]{:S(2)}) collective-permute-start(f32[3,144,128]{2,1,0:T(8,128)S(1)} %get-tuple-element.22), channel_id=1, source_target_pairs={{0,17},{1,18},{2,19},{3,20},{4,21},{5,22},{6,23},{7,24},{8,25},{9,... | collective-permute-start | bytes 663560 | tf_op jit(solution)/shard_map/ppermute | solution.py:39
where the time goes:
time: 132 us; the launch traced here: 131 us
  Pallas kernels  54 us (41%)
  waiting for transfers between devices  40.8 us (31%)
  starting transfers between devices  29.9 us (23%)
  local copies, waits for them, and re-layouts  5.91 us (4%)
    pallas_call x1, Pallas kernels, body(): pl.pallas_call(pair_kernel, out_shape=(planes(3),) * 4, in_specs=[SM] + [...  49.4 us
    ppermute x6, starting transfers between devices, passed_along(): return lax.ppermute(value, ('gx', 'gy'), pairs)  18.2 us
    ppermute x4, waiting for transfers between devices, passed_along(): lax.ppermute(value, 'gy', [(s, (s + step_y) % ny) for s in range(ny)])  16.3 us
    ppermute x6, waiting for transfers between devices, passed_along(): return lax.ppermute(value, ('gx', 'gy'), pairs)  15.9 us
    ppermute x4, waiting for transfers between devices, passed_along(): lax.ppermute(value, 'gx', [(s, (s + step_x) % nx) for s in range(nx)])  8.57 us
    ppermute x4, starting transfers between devices, passed_along(): lax.ppermute(value, 'gy', [(s, (s + step_y) % ny) for s in range(ny)])  6.42 us
    unnamed x16, local copies, waits for them, and re-layouts  5.86 us
    ppermute x4, starting transfers between devices, passed_along(): lax.ppermute(value, 'gx', [(s, (s + step_x) % nx) for s in range(nx)])  5.26 us
  transfers between devices with their start and end apart: 14, of which 8 were waited for; matrix products, arithmetic and copies ran while one was open for 0% of the time, Pallas kernels for 0%

commit v1 on v0

--- a/solution.py
+++ b/solution.py
@@ -39,7 +39,16 @@
     return lax.ppermute(value, ("gx", "gy"), pairs)
 
 
-def pack_kernel(move, pos, vel, chg, rep, dis, inv, stay, parcels, staying, tally):
+def pack_kernel(*refs):
+    sources, (stay, parcels, staying), scratch = refs[:7], refs[7:10], refs[10:]
+    move, pos, vel, chg, rep, dis, inv = scratch[:7]
+    tally, arrival = scratch[7:]
+    copies = [
+        pltpu.make_async_copy(source, held, arrival.at[k])
+        for k, (source, held) in enumerate(zip(sources, scratch))
+    ]
+    for copy in copies:
+        copy.start()
     zero = jnp.zeros((8, BLOCK), jnp.float32)
     for f in range(10):
         for u in range(CAPACITY // 8):
@@ -48,6 +57,8 @@
         for u in range(3):
             parcels[p, 8 * u : 8 * u + 8, :] = zero
         tally[p] = 0
+    for copy in copies:
+        copy.wait()
 
     def rows(k):
         at = pl.ds(k, 1)
@@ -101,9 +112,9 @@
         rest[k] = held[f, 0:CAPACITY, :]
 
 
-def update_kernel(home, east, north, corner, coords, rest, new_x, new_v, total):
+def update_kernel(home, east, north, coords, rest, new_x, new_v, total):
     for d in range(3):
-        force = home[d] + east[d] + north[d] + corner[d]
+        force = home[d] + east[d] + north[d]
         fresh = rest[d] + TSTEP * rest[3] * force
         total[d] = force
         new_v[d] = fresh
@@ -114,7 +125,7 @@
     return (b // 8) * 256 + (b % 8) * 16
 
 
-def pair_kernel(tiles, home, east, north, corner, fh, fe, fn, fc, zone, ac0, ac1, ac2, ibuf0, ibuf1, vbuf0, vbuf1, wbuf, *, T=2, mxu=True):
+def pair_kernel(tiles, home, east, north, corner, fh, fx, fn, zone, ac0, ac1, ac2, ibuf0, ibuf1, vbuf0, vbuf1, wbuf, *, T=2, mxu=True):
     acc=(ac0,ac1,ac2)
     sub = lax.broadcasted_iota(jnp.int32,(8,128),0)
     lane = lax.broadcasted_iota(jnp.int32,(8,128),1)
@@ -207,14 +218,14 @@
     lax.fori_loop(0,CAPACITY//2,two,0)
     settle(CAPACITY-1,vbuf1)
     for d in range(3):
-        for z,ref in enumerate((fh,fe,fn,fc)):
+        for z,(ref,o) in enumerate(((fh,0),(fx,0),(fn,0),(fx,3))):
             def red(k,_):
                 for u in range(3):
                     k8=pl.multiple_of(k*24+8*u,8)
                     r=[acc[d][pl.ds((z*CAPACITY+k8)*8+q,8,stride=8),:] for q in range(8)]
                     r=((r[0]+r[1])+(r[2]+r[3]))+((r[4]+r[5])+(r[6]+r[7]))
-                    if z==0: ref[d,pl.ds(k8,8),:]=ref[d,pl.ds(k8,8),:]-r
-                    else: ref[d,pl.ds(k8,8),:]=-r
+                    if z==0: ref[o+d,pl.ds(k8,8),:]=ref[o+d,pl.ds(k8,8),:]-r
+                    else: ref[o+d,pl.ds(k8,8),:]=-r
                 return 0
             lax.fori_loop(0,CAPACITY//24,red,0)
 
@@ -232,9 +243,12 @@
     stay, parcels, staying = pl.pallas_call(
         pack_kernel,
         out_shape=(planes(10), planes(9, 24), jax.ShapeDtypeStruct((1,), jnp.int32)),
-        in_specs=[SM] + [VM] * 6,
+        in_specs=[pl.BlockSpec(memory_space=pltpu.HBM)] * 7,
         out_specs=(VM, VM, SM),
-        scratch_shapes=[pltpu.SMEM((9,), jnp.int32)],
+        scratch_shapes=[pltpu.SMEM((NB,), jnp.int32)]
+        + [pltpu.VMEM((3, NB, BLOCK), jnp.float32)] * 2
+        + [pltpu.VMEM((NB, BLOCK), jnp.float32)] * 4
+        + [pltpu.SMEM((9,), jnp.int32), pltpu.SemaphoreType.DMA((7,))],
         compiler_params=PARAMS,
         name="pack",
     )(
@@ -258,27 +272,26 @@
     )(staying, stay, *arrived)
     east = passed_along(coords, -1, 0)
     north = passed_along(coords, 0, -1)
-    corner = passed_along(coords, -1, -1)
-    on_home, on_east, on_north, on_corner = pl.pallas_call(
+    corner = passed_along(north, -1, 0)
+    on_home, on_x, on_north = pl.pallas_call(
         pair_kernel,
-        out_shape=(planes(3),) * 4,
+        out_shape=(planes(3), planes(6), planes(3)),
         in_specs=[SM] + [VM] * 4,
-        out_specs=(VM,) * 4,
+        out_specs=(VM,) * 3,
         scratch_shapes=[pltpu.VMEM((6,4 * CAPACITY,128),jnp.float32)]+[pltpu.VMEM((4 * CAPACITY*8,128),jnp.float32)]*3+[pltpu.VMEM((6,16,8,128),jnp.float32)]*2+[pltpu.VMEM((3,2,16,8,128),jnp.float32)]*2+[pltpu.VMEM((17,8,128),jnp.float32)],
         compiler_params=PARAMS,
         name="pair",
     )(tiles.reshape(18, 128, 2).transpose(0, 2, 1).reshape(-1), coords, east, north, corner)
-    from_east = passed_along(on_east, 1, 0)
-    from_north = passed_along(on_north, 0, 1)
-    from_corner = passed_along(on_corner, 1, 1)
+    from_x = passed_along(on_x, 1, 0)
+    from_north = passed_along(on_north + from_x[3:6], 0, 1)
     out = pl.pallas_call(
         update_kernel,
         out_shape=(planes(3),) * 3,
-        in_specs=[VM] * 6,
+        in_specs=[VM] * 5,
         out_specs=(VM,) * 3,
         compiler_params=PARAMS,
         name="update",
-    )(on_home, from_east, from_north, from_corner, coords, rest)
+    )(on_home, from_x, from_north, coords, rest)
     return tuple(value.reshape(3, 1, 1, CAPACITY * BLOCK) for value in out)
 
 

time: 132 us -> 129 us (0.977)
  starting transfers between devices: 29.9 us -> 27.6 us
    ppermute x6 -> x4, waiting for transfers between devices: 15.9 us -> 0.71 us  [passed_along(): return lax.ppermute(value, ('gx', 'gy'), pairs)]
    ppermute x4 -> x5, waiting for transfers between devices: 8.57 us -> 18.1 us  [passed_along(): lax.ppermute(value, 'gx', [(s, (s + step_x) % nx) for s in range(nx)])]
    ppermute x4, waiting for transfers between devices: 16.3 us -> 21.4 us  [passed_along(): lax.ppermute(value, 'gy', [(s, (s + step_y) % ny) for s in range(ny)])]
    ppermute x6 -> x4, starting transfers between devices: 18.2 us -> 13.6 us  [passed_along(): return lax.ppermute(value, ('gx', 'gy'), pairs)]
    ppermute x4, starting transfers between devices: 6.42 us -> 9.63 us  [passed_along(): lax.ppermute(value, 'gy', [(s, (s + step_y) % ny) for s in range(ny)])]
    ppermute x4 -> x5, starting transfers between devices: 5.26 us -> 4.31 us  [passed_along(): lax.ppermute(value, 'gx', [(s, (s + step_x) % nx) for s in range(nx)])]
  transfers between devices with their start and end apart: 14 -> 13, of which waited for: 8 -> 7; matrix products, arithmetic and copies ran while one was open for 0% -> 0% of each run, Pallas kernels for 0% -> 0%
where the time goes in v1:
time: 129 us
  Pallas kernels  54.2 us (42%)
  waiting for transfers between devices  40.3 us (31%)
  starting transfers between devices  27.6 us (21%)
  local copies, waits for them, and re-layouts  5.91 us (5%)
    pallas_call x1, Pallas kernels, body(): pl.pallas_call(pair_kernel, out_shape=(planes(3), planes(6), planes(3)),...  49.4 us
    ppermute x4, waiting for transfers between devices, passed_along(): lax.ppermute(value, 'gy', [(s, (s + step_y) % ny) for s in range(ny)])  21.4 us
    ppermute x5, waiting for transfers between devices, passed_along(): lax.ppermute(value, 'gx', [(s, (s + step_x) % nx) for s in range(nx)])  18.1 us
    ppermute x4, starting transfers between devices, passed_along(): return lax.ppermute(value, ('gx', 'gy'), pairs)  13.6 us
    ppermute x4, starting transfers between devices, passed_along(): lax.ppermute(value, 'gy', [(s, (s + step_y) % ny) for s in range(ny)])  9.63 us
    unnamed x16, local copies, waits for them, and re-layouts  5.86 us
    ppermute x5, starting transfers between devices, passed_along(): lax.ppermute(value, 'gx', [(s, (s + step_x) % nx) for s in range(nx)])  4.31 us
    pallas_call x1, Pallas kernels, body(): pl.pallas_call(pack_kernel, out_shape=(planes(10), planes(9, 24), jax.Sha...  3.14 us
  transfers between devices with their start and end apart: 13, of which 7 were waited for; matrix products, arithmetic and copies ran while one was open for 0% of the time, Pallas kernels for 0%

profile of v1, /device:TPU:0, one launch (start us, length us, event | category | flops | bytes accessed | tf_op | source)
XLA Modules:
  0.0 128.8 jit_solution(4295548869647630596)
XLA Ops:
  0.6 0.6 copy-done.6
  1.3 0.9 copy-done
  2.2 0.9 copy-done.1
  3.1 0.8 copy-done.2
  4.0 0.8 copy-done.3
  4.8 0.8 copy-done.4
  5.7 0.8 copy-done.5
  6.5 3.1 %pack.1 = (f32[10,144,128]{2,1,0:T(8,128)S(1)}, f32[9,24,128]{2,1,0:T(8,128)S(1)}, s32[1]{0:T(128)}) custom-call(s32[128]{0:T(128)S(1)} %bitcast.37, f32[3,128,128]{2,1,0:T(8,128)S(1)} %bitcast.31, f32[3,128,128]{2,1,0:T(8,128)S(1)} %bitcast.32, f32[128,128]{1,0:T(8,128)S(1)} %bitcast.33, f32[128,128]{1,0:T(8,128)S(1)} %bitcast.34, f32[128,128]{1,0:T(8,128)S(1)} %bitcast.35, ...), custom_call_target="tpu_custom_call" | custom-call | tf_op jit(solution)/shard_map/pack/pallas_call | solution.py:243
  9.7 8.3 %collective-permute-start.7 = (f32[24,128]{1,0:T(8,128)S(1)}, f32[24,128]{1,0:T(8,128)S(1)}, u32[]{:S(2)}, u32[]{:S(2)}) collective-permute-start(f32[24,128]{1,0:T(8,128)S(1)} %get-tuple-element.31), channel_id=1, source_target_pairs={{0,255},{1,240},{2,241},{3,242},{4,243},{5,244},{6,245},{7,246},{8... | collective-permute-start | bytes 36872 | tf_op jit(solution)/shard_map/ppermute | solution.py:39
  18.0 0.0 collective-permute-start.6
  18.0 5.4 %collective-permute-start.5 = (f32[24,128]{1,0:T(8,128)S(1)}, f32[24,128]{1,0:T(8,128)S(1)}, u32[]{:S(2)}, u32[]{:S(2)}) collective-permute-start(f32[24,128]{1,0:T(8,128)S(1)} %get-tuple-element.33), channel_id=1, source_target_pairs={{0,31},{1,16},{2,17},{3,18},{4,19},{5,20},{6,21},{7,22},{8,23},{9,... | collective-permute-start | bytes 36872 | tf_op jit(solution)/shard_map/ppermute | solution.py:39
  23.3 0.0 collective-permute-start.4
  23.3 3.6 %collective-permute-start.3 = (f32[24,128]{1,0:T(8,128)S(1)}, f32[24,128]{1,0:T(8,128)S(1)}, u32[]{:S(2)}, u32[]{:S(2)}) collective-permute-start(f32[24,128]{1,0:T(8,128)S(1)} %get-tuple-element.35), channel_id=1, source_target_pairs={{0,15},{1,0},{2,1},{3,2},{4,3},{5,4},{6,5},{7,6},{8,7},{9,8},{10,9... | collective-permute-start | bytes 36872 | tf_op jit(solution)/shard_map/ppermute | solution.py:33
  26.9 0.0 collective-permute-done.7.refs_7_
  26.9 0.0 collective-permute-start.2
  26.9 0.0 collective-permute-done.6.refs_6_
  26.9 4.2 %collective-permute-start.1 = (f32[24,128]{1,0:T(8,128)S(1)}, f32[24,128]{1,0:T(8,128)S(1)}, u32[]{:S(2)}, u32[]{:S(2)}) collective-permute-start(f32[24,128]{1,0:T(8,128)S(1)} %get-tuple-element.37), channel_id=1, source_target_pairs={{0,240},{16,0},{32,16},{48,32},{64,48},{80,64},{96,80},{112,96},{1... | collective-permute-start | bytes 36872 | tf_op jit(solution)/shard_map/ppermute | solution.py:31
  31.2 0.0 collective-permute-done.5.refs_5_
  31.2 0.7 collective-permute-done.4.refs_4_
  31.9 2.4 %collective-permute-done.2.refs_2_ = f32[24,128]{1,0:T(8,128)S(1)} collective-permute-done((f32[24,128]{1,0:T(8,128)S(1)}, f32[24,128]{1,0:T(8,128)S(1)}, u32[]{:S(2)}, u32[]{:S(2)}) %collective-permute-start.2) | collective-permute-done | bytes 12320 | tf_op jit(solution)/shard_map/ppermute | solution.py:33
  34.2 2.3 %collective-permute-done.refs_0_ = f32[24,128]{1,0:T(8,128)S(1)} collective-permute-done((f32[24,128]{1,0:T(8,128)S(1)}, f32[24,128]{1,0:T(8,128)S(1)}, u32[]{:S(2)}, u32[]{:S(2)}) %collective-permute-start) | collective-permute-done | bytes 12320 | tf_op jit(solution)/shard_map/ppermute | solution.py:31
  36.5 0.8 arrive.1
  37.4 5.9 %collective-permute-start.9 = (f32[6,144,128]{2,1,0:T(8,128)S(1)}, f32[6,144,128]{2,1,0:T(8,128)S(1)}, u32[]{:S(2)}, u32[]{:S(2)}) collective-permute-start(f32[6,144,128]{2,1,0:T(8,128)S(1)} %get-tuple-element.17.home.coords), channel_id=1, source_target_pairs={{0,15},{1,0},{2,1},{3,2},{4,3},{5,4},{6,5},{7,6},{8,7},{9,8},{10,9... | collective-permute-start | bytes 1327112 | tf_op jit(solution)/shard_map/ppermute | solution.py:33
  43.3 8.3 %collective-permute-done.9.north = f32[6,144,128]{2,1,0:T(8,128)S(1)} collective-permute-done((f32[6,144,128]{2,1,0:T(8,128)S(1)}, f32[6,144,128]{2,1,0:T(8,128)S(1)}, u32[]{:S(2)}, u32[]{:S(2)}) %collective-permute-start.9) | collective-permute-done | bytes 442400 | tf_op jit(solution)/shard_map/ppermute | solution.py:33
  51.6 0.0 collective-permute-start.10
  51.7 5.7 %collective-permute-done.10.corner = f32[6,144,128]{2,1,0:T(8,128)S(1)} collective-permute-done((f32[6,144,128]{2,1,0:T(8,128)S(1)}, f32[6,144,128]{2,1,0:T(8,128)S(1)}, u32[]{:S(2)}, u32[]{:S(2)}) %collective-permute-start.10) | collective-permute-done | bytes 442400 | tf_op jit(solution)/shard_map/ppermute | solution.py:31
  57.4 49.4 %pair.1 = (f32[3,144,128]{2,1,0:T(8,128)S(1)}, f32[6,144,128]{2,1,0:T(8,128)S(1)}, f32[3,144,128]{2,1,0:T(8,128)S(1)}) custom-call(s32[4608]{0:T(1024)S(1)} %reshape.43.tiles, f32[6,144,128]{2,1,0:T(8,128)S(1)} %get-tuple-element.17.home.coords, f32[6,144,128]{2,1,0:T(8,128)S(1)} %collective-permute-done.8.east, ...), custom_call_target="tpu_custom_call" | custom-call | tf_op jit(solution)/shard_map/pair/pallas_call | solution.py:276
  106.8 0.1 collective-permute-start.11
  106.9 10.1 %collective-permute-done.11.east = f32[6,144,128]{2,1,0:T(8,128)S(1)} collective-permute-done((f32[6,144,128]{2,1,0:T(8,128)S(1)}, f32[6,144,128]{2,1,0:T(8,128)S(1)}, u32[]{:S(2)}, u32[]{:S(2)}) %collective-permute-start.11) | collective-permute-done | bytes 442400 | tf_op jit(solution)/shard_map/ppermute | solution.py:31
  117.0 0.1 collective-permute-start.12
  117.1 10.8 %collective-permute-done.12.north = f32[3,144,128]{2,1,0:T(8,128)S(1)} collective-permute-done((f32[3,144,128]{2,1,0:T(8,128)S(1)}, f32[3,144,128]{2,1,0:T(8,128)S(1)}, u32[]{:S(2)}, u32[]{:S(2)}) %collective-permute-start.12) | collective-permute-done | bytes 221216 | tf_op jit(solution)/shard_map/ppermute | solution.py:33
  127.9 0.9 update.1
  (19 shorter events, 0.1 us)
Async XLA Ops:
  0.6 0.7 copy-start.6
  1.3 0.9 copy-start
  2.2 0.9 copy-start.1
  3.1 0.8 copy-start.2
  4.0 0.8 copy-start.3
  4.8 0.8 copy-start.4
  5.7 0.8 copy-start.5
  9.7 17.3 %collective-permute-start.7 = (f32[24,128]{1,0:T(8,128)S(1)}, f32[24,128]{1,0:T(8,128)S(1)}, u32[]{:S(2)}, u32[]{:S(2)}) collective-permute-start(f32[24,128]{1,0:T(8,128)S(1)} %get-tuple-element.31), channel_id=1, source_target_pairs={{0,255},{1,240},{2,241},{3,242},{4,243},{5,244},{6,245},{7,246},{8... | collective-permute-start | bytes 36872 | tf_op jit(solution)/shard_map/ppermute | solution.py:39
  18.0 9.0 %collective-permute-start.6 = (f32[24,128]{1,0:T(8,128)S(1)}, f32[24,128]{1,0:T(8,128)S(1)}, u32[]{:S(2)}, u32[]{:S(2)}) collective-permute-start(f32[24,128]{1,0:T(8,128)S(1)} %get-tuple-element.32), channel_id=1, source_target_pairs={{0,241},{1,242},{2,243},{3,244},{4,245},{5,246},{6,247},{7,248},{8... | collective-permute-start | bytes 36872 | tf_op jit(solution)/shard_map/ppermute | solution.py:39
  18.0 13.2 %collective-permute-start.5 = (f32[24,128]{1,0:T(8,128)S(1)}, f32[24,128]{1,0:T(8,128)S(1)}, u32[]{:S(2)}, u32[]{:S(2)}) collective-permute-start(f32[24,128]{1,0:T(8,128)S(1)} %get-tuple-element.33), channel_id=1, source_target_pairs={{0,31},{1,16},{2,17},{3,18},{4,19},{5,20},{6,21},{7,22},{8,23},{9,... | collective-permute-start | bytes 36872 | tf_op jit(solution)/shard_map/ppermute | solution.py:39
  23.3 8.6 %collective-permute-start.4 = (f32[24,128]{1,0:T(8,128)S(1)}, f32[24,128]{1,0:T(8,128)S(1)}, u32[]{:S(2)}, u32[]{:S(2)}) collective-permute-start(f32[24,128]{1,0:T(8,128)S(1)} %get-tuple-element.34), channel_id=1, source_target_pairs={{0,17},{1,18},{2,19},{3,20},{4,21},{5,22},{6,23},{7,24},{8,25},{9,... | collective-permute-start | bytes 36872 | tf_op jit(solution)/shard_map/ppermute | solution.py:39
  23.3 8.6 %collective-permute-start.3 = (f32[24,128]{1,0:T(8,128)S(1)}, f32[24,128]{1,0:T(8,128)S(1)}, u32[]{:S(2)}, u32[]{:S(2)}) collective-permute-start(f32[24,128]{1,0:T(8,128)S(1)} %get-tuple-element.35), channel_id=1, source_target_pairs={{0,15},{1,0},{2,1},{3,2},{4,3},{5,4},{6,5},{7,6},{8,7},{9,8},{10,9... | collective-permute-start | bytes 36872 | tf_op jit(solution)/shard_map/ppermute | solution.py:33
  26.9 7.3 %collective-permute-start.2 = (f32[24,128]{1,0:T(8,128)S(1)}, f32[24,128]{1,0:T(8,128)S(1)}, u32[]{:S(2)}, u32[]{:S(2)}) collective-permute-start(f32[24,128]{1,0:T(8,128)S(1)} %get-tuple-element.36), channel_id=1, source_target_pairs={{0,1},{1,2},{2,3},{3,4},{4,5},{5,6},{6,7},{7,8},{8,9},{9,10},{10,1... | collective-permute-start | bytes 36872 | tf_op jit(solution)/shard_map/ppermute | solution.py:33
  26.9 7.3 %collective-permute-start.1 = (f32[24,128]{1,0:T(8,128)S(1)}, f32[24,128]{1,0:T(8,128)S(1)}, u32[]{:S(2)}, u32[]{:S(2)}) collective-permute-start(f32[24,128]{1,0:T(8,128)S(1)} %get-tuple-element.37), channel_id=1, source_target_pairs={{0,240},{16,0},{32,16},{48,32},{64,48},{80,64},{96,80},{112,96},{1... | collective-permute-start | bytes 36872 | tf_op jit(solution)/shard_map/ppermute | solution.py:31
  31.2 5.4 %collective-permute-start = (f32[24,128]{1,0:T(8,128)S(1)}, f32[24,128]{1,0:T(8,128)S(1)}, u32[]{:S(2)}, u32[]{:S(2)}) collective-permute-start(f32[24,128]{1,0:T(8,128)S(1)} %get-tuple-element.38), channel_id=1, source_target_pairs={{0,16},{16,32},{32,48},{48,64},{64,80},{80,96},{96,112},{112,128},... | collective-permute-start | bytes 36872 | tf_op jit(solution)/shard_map/ppermute | solution.py:31
  36.5 15.1 %copy-start.7 = (s32[1,1,2304,2]{2,3,1,0:T(2,128)S(1)}, s32[1,1,2304,2]{2,3,1,0:T(2,128)}, u32[]{:S(2)}) copy-start(s32[1,1,2304,2]{2,3,1,0:T(2,128)} %param.15) | copy-start | bytes 55300
  37.4 14.2 %collective-permute-start.9 = (f32[6,144,128]{2,1,0:T(8,128)S(1)}, f32[6,144,128]{2,1,0:T(8,128)S(1)}, u32[]{:S(2)}, u32[]{:S(2)}) collective-permute-start(f32[6,144,128]{2,1,0:T(8,128)S(1)} %get-tuple-element.17.home.coords), channel_id=1, source_target_pairs={{0,15},{1,0},{2,1},{3,2},{4,3},{5,4},{6,5},{7,6},{8,7},{9,8},{10,9... | collective-permute-start | bytes 1327112 | tf_op jit(solution)/shard_map/ppermute | solution.py:33
  43.3 8.4 %collective-permute-start.8 = (f32[6,144,128]{2,1,0:T(8,128)S(1)}, f32[6,144,128]{2,1,0:T(8,128)S(1)}, u32[]{:S(2)}, u32[]{:S(2)}) collective-permute-start(f32[6,144,128]{2,1,0:T(8,128)S(1)} %get-tuple-element.17.home.coords), channel_id=1, source_target_pairs={{0,240},{16,0},{32,16},{48,32},{64,48},{80,64},{96,80},{112,96},{1... | collective-permute-start | bytes 1327112 | tf_op jit(solution)/shard_map/ppermute | solution.py:31
  51.6 5.8 %collective-permute-start.10 = (f32[6,144,128]{2,1,0:T(8,128)S(1)}, f32[6,144,128]{2,1,0:T(8,128)S(1)}, u32[]{:S(2)}, u32[]{:S(2)}) collective-permute-start(f32[6,144,128]{2,1,0:T(8,128)S(1)} %collective-permute-done.9.north), channel_id=1, source_target_pairs={{0,240},{16,0},{32,16},{48,32},{64,48},{80,64},{96,80},{112,96},{1... | collective-permute-start | bytes 1327112 | tf_op jit(solution)/shard_map/ppermute | solution.py:31
  106.8 10.2 %collective-permute-start.11 = (f32[6,144,128]{2,1,0:T(8,128)S(1)}, f32[6,144,128]{2,1,0:T(8,128)S(1)}, u32[]{:S(2)}, u32[]{:S(2)}) collective-permute-start(f32[6,144,128]{2,1,0:T(8,128)S(1)} %get-tuple-element.19), channel_id=1, source_target_pairs={{0,16},{16,32},{32,48},{48,64},{64,80},{80,96},{96,112},{112,128},... | collective-permute-start | bytes 1327112 | tf_op jit(solution)/shard_map/ppermute | solution.py:31
  117.0 10.9 %collective-permute-start.12 = (f32[3,144,128]{2,1,0:T(8,128)S(1)}, f32[3,144,128]{2,1,0:T(8,128)S(1)}, u32[]{:S(2)}, u32[]{:S(2)}) collective-permute-start(f32[3,144,128]{2,1,0:T(8,128)S(1)} %slice_add_fusion), channel_id=1, source_target_pairs={{0,1},{1,2},{2,3},{3,4},{4,5},{5,6},{6,7},{7,8},{8,9},{9,10},{10,1... | collective-permute-start | bytes 663560 | tf_op jit(solution)/shard_map/ppermute | solution.py:33

commit v2 on v1

--- a/solution.py
+++ b/solution.py
@@ -39,61 +39,99 @@
     return lax.ppermute(value, ("gx", "gy"), pairs)
 
 
-def pack_kernel(*refs):
-    sources, (stay, parcels, staying), scratch = refs[:7], refs[7:10], refs[10:]
-    move, pos, vel, chg, rep, dis, inv = scratch[:7]
-    tally, arrival = scratch[7:]
+PLACE = (8, 0, 3, 6, 7, 1, 2, 4, 5)
+
+
+def fetch(sources, scratch, arrival):
     copies = [
         pltpu.make_async_copy(source, held, arrival.at[k])
         for k, (source, held) in enumerate(zip(sources, scratch))
     ]
     for copy in copies:
         copy.start()
+    return copies
+
+
+def block_rows(scratch, k):
+    pos, vel, chg, rep, dis, inv = scratch[1:7]
+    at = pl.ds(k, 1)
+    return [pos[d, at, :] for d in range(3)] + [vel[d, at, :] for d in range(3)] + [
+        ref[at, :] for ref in (chg, rep, dis, inv)
+    ]
+
+
+def pack_kernel(*refs):
+    sources, parcels, scratch, tally, arrival = refs[:7], refs[7], refs[8:15], refs[15], refs[16]
+    move = scratch[0]
+    copies = fetch(sources, scratch, arrival)
+    zero = jnp.zeros((8, BLOCK), jnp.float32)
+    for p in range(8):
+        for u in range(3):
+            parcels[p, 8 * u : 8 * u + 8, :] = zero
+    for code in range(9):
+        tally[code] = 0
+    for copy in copies:
+        copy.wait()
+
+    def one(k, carry):
+        code = move[k]
+
+        @pl.when(code != 0)
+        def _():
+            seen = tally[code]
+            tally[code] = seen + 1
+            to = tally[9 + code]
+            slot = jnp.minimum(seen, 1) * 10
+            for f, value in enumerate(block_rows(scratch, k)):
+                parcels[to, pl.ds(slot + f, 1), :] = value
+
+        return carry
+
+    for code in range(1, 9):
+        tally[9 + code] = PLACE[code]
+    lax.fori_loop(0, NB, one, 0, unroll=4)
+    for code in range(1, 9):
+        step_x, step_y = OFFSETS[code]
+        to = PLACE[code]
+        for n in range(2):
+            if step_x != 0:
+                parcels[to, 10 * n : 10 * n + 1, :] = parcels[to, 10 * n : 10 * n + 1, :] - step_x * CELL
+            if step_y != 0:
+                parcels[to, 10 * n + 1 : 10 * n + 2, :] = parcels[to, 10 * n + 1 : 10 * n + 2, :] - step_y * CELL
+        parcels[to, 20:21, :] = jnp.broadcast_to(tally[code], (1, BLOCK)).astype(jnp.float32)
+
+
+def stay_kernel(*refs):
+    sources, (stay, staying), scratch, arrival = refs[:7], refs[7:9], refs[9:16], refs[16]
+    move = scratch[0]
+    copies = fetch(sources, scratch, arrival)
     zero = jnp.zeros((8, BLOCK), jnp.float32)
     for f in range(10):
         for u in range(CAPACITY // 8):
             stay[f, 8 * u : 8 * u + 8, :] = zero
-    for p in range(9):
-        for u in range(3):
-            parcels[p, 8 * u : 8 * u + 8, :] = zero
-        tally[p] = 0
     for copy in copies:
         copy.wait()
 
-    def rows(k):
-        at = pl.ds(k, 1)
-        return [pos[d, at, :] for d in range(3)] + [vel[d, at, :] for d in range(3)] + [
-            ref[at, :] for ref in (chg, rep, dis, inv)
-        ]
-
     def one(k, kept):
-        code = move[k]
-        values = rows(k)
-        for f in range(10):
-            stay[f, pl.ds(kept, 1), :] = values[f]
-        seen = tally[code]
-        tally[code] = seen + 1
-        slot = jnp.where(code == 0, 0, jnp.minimum(seen, 1)) * 10
-        for f in range(10):
-            parcels[code, pl.ds(slot + f, 1), :] = values[f]
-        return kept + jnp.where(code == 0, 1, 0)
+        for f, value in enumerate(block_rows(scratch, k)):
+            stay[f, pl.ds(kept, 1), :] = value
+        return kept + jnp.where(move[k] == 0, 1, 0)
 
     kept = lax.fori_loop(0, NB, one, 0)
     for f in range(10):
         stay[f, pl.ds(kept, 1), :] = zero[0:1]
     staying[0] = kept
-    for code in range(1, 9):
-        step_x, step_y = OFFSETS[code]
-        for n in range(2):
-            if step_x != 0:
-                parcels[code, 10 * n : 10 * n + 1, :] = parcels[code, 10 * n : 10 * n + 1, :] - step_x * CELL
-            if step_y != 0:
-                parcels[code, 10 * n + 1 : 10 * n + 2, :] = parcels[code, 10 * n + 1 : 10 * n + 2, :] - step_y * CELL
-        parcels[code, 20:21, :] = jnp.broadcast_to(tally[code], (1, BLOCK)).astype(jnp.float32)
+
+
+def turn_kernel(parcels, left, right, up, down):
+    up[0], down[0] = parcels[6], parcels[7]
+    up[1], down[1] = left[1], left[2]
+    up[2], down[2] = right[1], right[2]
 
 
 def arrive_kernel(staying, stay, *refs):
-    parcels, coords, rest, held = refs[:8], refs[8], refs[9], refs[10]
+    left, right, up, down, coords, rest, held = refs
+    parcels = [left.at[0], right.at[0], up.at[0], down.at[0], up.at[1], down.at[1], up.at[2], down.at[2]]
     for f in range(10):
         held[f, 0:CAPACITY, :] = stay[f]
     counts = jnp.concatenate([p[20:21, :] for p in parcels], axis=0).astype(jnp.int32)
@@ -232,7 +270,9 @@
 
 VM = pl.BlockSpec(memory_space=pltpu.VMEM)
 SM = pl.BlockSpec(memory_space=pltpu.SMEM)
+HBM = pl.BlockSpec(memory_space=pltpu.HBM)
 PARAMS = pltpu.CompilerParams(vmem_limit_bytes=48 * 1024 * 1024)
+WIDE = pltpu.CompilerParams(vmem_limit_bytes=56 * 1024 * 1024)
 
 
 def planes(count, rows=CAPACITY):
@@ -240,18 +280,7 @@
 
 
 def body(positions, velocities, charges, repel_root, disperse_root, inverse_mass, move, tiles):
-    stay, parcels, staying = pl.pallas_call(
-        pack_kernel,
-        out_shape=(planes(10), planes(9, 24), jax.ShapeDtypeStruct((1,), jnp.int32)),
-        in_specs=[pl.BlockSpec(memory_space=pltpu.HBM)] * 7,
-        out_specs=(VM, VM, SM),
-        scratch_shapes=[pltpu.SMEM((NB,), jnp.int32)]
-        + [pltpu.VMEM((3, NB, BLOCK), jnp.float32)] * 2
-        + [pltpu.VMEM((NB, BLOCK), jnp.float32)] * 4
-        + [pltpu.SMEM((9,), jnp.int32), pltpu.SemaphoreType.DMA((7,))],
-        compiler_params=PARAMS,
-        name="pack",
-    )(
+    inputs = (
         move.reshape(NB),
         positions.reshape(3, NB, BLOCK),
         velocities.reshape(3, NB, BLOCK),
@@ -260,16 +289,51 @@
         disperse_root.reshape(NB, BLOCK),
         inverse_mass.reshape(NB, BLOCK),
     )
-    arrived = [passed_along(parcels[code], *OFFSETS[code]) for code in range(1, 9)]
+    held = (
+        [pltpu.SMEM((NB,), jnp.int32)]
+        + [pltpu.VMEM((3, NB, BLOCK), jnp.float32)] * 2
+        + [pltpu.VMEM((NB, BLOCK), jnp.float32)] * 4
+    )
+    parcels = pl.pallas_call(
+        pack_kernel,
+        out_shape=planes(8, 24),
+        in_specs=[HBM] * 7,
+        out_specs=VM,
+        scratch_shapes=held + [pltpu.SMEM((18,), jnp.int32), pltpu.SemaphoreType.DMA((7,))],
+        compiler_params=WIDE,
+        name="pack",
+    )(*inputs)
+    left = passed_along(parcels[0:3], 1, 0)
+    right = passed_along(parcels[3:6], -1, 0)
+    stay, staying = pl.pallas_call(
+        stay_kernel,
+        out_shape=(planes(10), jax.ShapeDtypeStruct((1,), jnp.int32)),
+        in_specs=[HBM] * 7,
+        out_specs=(VM, SM),
+        scratch_shapes=held + [pltpu.SemaphoreType.DMA((7,))],
+        compiler_params=WIDE,
+        cost_estimate=pl.CostEstimate(flops=0, bytes_accessed=6_000_000, transcendentals=0),
+        name="stay",
+    )(*inputs)
+    up, down = pl.pallas_call(
+        turn_kernel,
+        out_shape=(planes(3, 24),) * 2,
+        in_specs=[VM] * 3,
+        out_specs=(VM,) * 2,
+        compiler_params=PARAMS,
+        name="turn",
+    )(parcels, left, right)
+    up = passed_along(up, 0, 1)
+    down = passed_along(down, 0, -1)
     coords, rest = pl.pallas_call(
         arrive_kernel,
         out_shape=(planes(6), planes(4)),
-        in_specs=[SM] + [VM] * 9,
+        in_specs=[SM] + [VM] * 5,
         out_specs=(VM, VM),
         scratch_shapes=[pltpu.VMEM((10, CAPACITY + 8, BLOCK), jnp.float32)],
         compiler_params=PARAMS,
         name="arrive",
-    )(staying, stay, *arrived)
+    )(staying, stay, left, right, up, down)
     east = passed_along(coords, -1, 0)
     north = passed_along(coords, 0, -1)
     corner = passed_along(north, -1, 0)

time: 129 us -> 116 us (0.90)
  the two profiles are of different devices: /device:TPU:0 before, /device:TPU:96 now
where the time goes in v2:
time: 116 us; the launch traced here: 115 us
  Pallas kernels  57.3 us (49%)
  waiting for transfers between devices  38 us (33%)
  starting transfers between devices  16.7 us (14%)
  local copies, waits for them, and re-layouts  2.01 us (2%)
    pallas_call x1, Pallas kernels, body(): pl.pallas_call(pair_kernel, out_shape=(planes(3), planes(6), planes(3)),...  49.3 us
    ppermute x5, waiting for transfers between devices, passed_along(): lax.ppermute(value, 'gx', [(s, (s + step_x) % nx) for s in range(nx)])  21.2 us
    ppermute x4, waiting for transfers between devices, passed_along(): lax.ppermute(value, 'gy', [(s, (s + step_y) % ny) for s in range(ny)])  16.7 us
    ppermute x4, starting transfers between devices, passed_along(): lax.ppermute(value, 'gy', [(s, (s + step_y) % ny) for s in range(ny)])  13.6 us
    pallas_call x1, Pallas kernels, body(): pl.pallas_call(pack_kernel, out_shape=planes(8, 24), in_specs=[HBM] * 7,...  3.2 us
    ppermute x5, starting transfers between devices, passed_along(): lax.ppermute(value, 'gx', [(s, (s + step_x) % nx) for s in range(nx)])  3.17 us
    pallas_call x1, Pallas kernels, body(): pl.pallas_call(stay_kernel, out_shape=(planes(10), jax.ShapeDtypeStruct((...  3.08 us
  transfers between devices with their start and end apart: 9, of which 7 were waited for; matrix products, arithmetic and copies ran while one was open for 0% of the time, Pallas kernels for 3%

profile of v2, /device:TPU:96, one launch (start us, length us, event | category | flops | bytes accessed | tf_op | source)
XLA Modules:
  0.0 114.8 jit_solution(852530850425241583)
XLA Ops:
  0.6 3.2 %pack.1.parcels = f32[8,24,128]{2,1,0:T(8,128)} custom-call(s32[128]{0:T(128)} %bitcast.28, f32[3,128,128]{2,1,0:T(8,128)} %bitcast.15, f32[3,128,128]{2,1,0:T(8,128)} %bitcast.17, f32[128,128]{1,0:T(8,128)} %bitcast.19, f32[128,128]{1,0:T(8,128)} %bitcast.21, f32[128,128]{1,0:T(8,128)} %bitcast.23, f32[128,128]{1,0:T(8,128)} %bitcast.25), custom_call_target="tpu_custom_call" | custom-call | tf_op jit(solution)/shard_map/pack/pallas_call | solution.py:297
  3.8 0.0 copy-start
  3.9 0.8 fusion
  4.7 3.1 %collective-permute-start.1 = (f32[3,24,128]{2,1,0:T(8,128)S(1)}, f32[3,24,128]{2,1,0:T(8,128)S(1)}, u32[]{:S(2)}, u32[]{:S(2)}) collective-permute-start(f32[3,24,128]{2,1,0:T(8,128)S(1)} %get-tuple-element.33), channel_id=1, source_target_pairs={{0,240},{16,0},{32,16},{48,32},{64,48},{80,64},{96,80},{112,96},{1... | collective-permute-start | bytes 110600 | tf_op jit(solution)/shard_map/ppermute | solution.py:31
  7.8 0.0 collective-permute-start
  7.8 1.6 %collective-permute-done.1.right.refs_1_ = f32[3,24,128]{2,1,0:T(8,128)S(1)} collective-permute-done((f32[3,24,128]{2,1,0:T(8,128)S(1)}, f32[3,24,128]{2,1,0:T(8,128)S(1)}, u32[]{:S(2)}, u32[]{:S(2)}) %collective-permute-start.1) | collective-permute-done | bytes 36896 | tf_op jit(solution)/shard_map/ppermute | solution.py:31
  9.4 3.9 %collective-permute-done.left.refs_0_ = f32[3,24,128]{2,1,0:T(8,128)S(1)} collective-permute-done((f32[3,24,128]{2,1,0:T(8,128)S(1)}, f32[3,24,128]{2,1,0:T(8,128)S(1)}, u32[]{:S(2)}, u32[]{:S(2)}) %collective-permute-start) | collective-permute-done | bytes 36896 | tf_op jit(solution)/shard_map/ppermute | solution.py:31
  13.3 0.0 copy-done
  13.3 3.2 %collective-permute-start.2 = (f32[3,24,128]{2,1,0:T(8,128)S(1)}, f32[3,24,128]{2,1,0:T(8,128)S(1)}, u32[]{:S(2)}, u32[]{:S(2)}) collective-permute-start(f32[3,24,128]{2,1,0:T(8,128)S(1)} %get-tuple-element.17), channel_id=1, source_target_pairs={{0,1},{1,2},{2,3},{3,4},{4,5},{5,6},{6,7},{7,8},{8,9},{9,10},{10,1... | collective-permute-start | bytes 110600 | tf_op jit(solution)/shard_map/ppermute | solution.py:33
  16.5 1.3 %collective-permute-start.3 = (f32[3,24,128]{2,1,0:T(8,128)S(1)}, f32[3,24,128]{2,1,0:T(8,128)S(1)}, u32[]{:S(2)}, u32[]{:S(2)}) collective-permute-start(f32[3,24,128]{2,1,0:T(8,128)S(1)} %get-tuple-element.18), channel_id=1, source_target_pairs={{0,15},{1,0},{2,1},{3,2},{4,3},{5,4},{6,5},{7,6},{8,7},{9,8},{10,9... | collective-permute-start | bytes 110600 | tf_op jit(solution)/shard_map/ppermute | solution.py:33
  17.8 3.1 %stay.1 = (f32[10,144,128]{2,1,0:T(8,128)}, s32[1]{0:T(128)}) custom-call(s32[128]{0:T(128)} %bitcast.29, f32[3,128,128]{2,1,0:T(8,128)} %bitcast.16, f32[3,128,128]{2,1,0:T(8,128)} %bitcast.18, f32[128,128]{1,0:T(8,128)} %bitcast.20, f32[128,128]{1,0:T(8,128)} %bitcast.22, f32[128,128]{1,0:T(8,128)} %bitcast.24, f32[128,128]{1,0:T(8,128)} %bitcast.26), custom_call_target="tpu_custom_call" | custom-call | bytes 6000000 | tf_op jit(solution)/shard_map/stay/pallas_call | solution.py:308
  20.9 0.0 collective-permute-done.2.refs_2_
  20.9 1.1 collective-permute-done.3.refs_3_
  22.0 0.0 copy-start.1
  22.0 1.1 copy-done.1
  23.1 0.0 copy-start.2
  23.1 0.8 arrive.1
  24.0 2.2 %collective-permute-start.5 = (f32[6,144,128]{2,1,0:T(8,128)S(1)}, f32[6,144,128]{2,1,0:T(8,128)S(1)}, u32[]{:S(2)}, u32[]{:S(2)}) collective-permute-start(f32[6,144,128]{2,1,0:T(8,128)S(1)} %get-tuple-element.19.home.coords), channel_id=1, source_target_pairs={{0,15},{1,0},{2,1},{3,2},{4,3},{5,4},{6,5},{7,6},{8,7},{9,8},{10,9... | collective-permute-start | bytes 1327112 | tf_op jit(solution)/shard_map/ppermute | solution.py:33
  26.2 0.0 collective-permute-start.4
  26.2 12.2 %collective-permute-done.5.north = f32[6,144,128]{2,1,0:T(8,128)S(1)} collective-permute-done((f32[6,144,128]{2,1,0:T(8,128)S(1)}, f32[6,144,128]{2,1,0:T(8,128)S(1)}, u32[]{:S(2)}, u32[]{:S(2)}) %collective-permute-start.5) | collective-permute-done | bytes 442400 | tf_op jit(solution)/shard_map/ppermute | solution.py:33
  38.4 0.0 collective-permute-start.6
  38.4 0.0 copy-done.2
  38.5 0.0 collective-permute-done.4.east
  38.5 5.7 %collective-permute-done.6.corner = f32[6,144,128]{2,1,0:T(8,128)S(1)} collective-permute-done((f32[6,144,128]{2,1,0:T(8,128)S(1)}, f32[6,144,128]{2,1,0:T(8,128)S(1)}, u32[]{:S(2)}, u32[]{:S(2)}) %collective-permute-start.6) | collective-permute-done | bytes 442400 | tf_op jit(solution)/shard_map/ppermute | solution.py:31
  44.2 49.3 %pair.1 = (f32[3,144,128]{2,1,0:T(8,128)S(1)}, f32[6,144,128]{2,1,0:T(8,128)S(1)}, f32[3,144,128]{2,1,0:T(8,128)S(1)}) custom-call(s32[4608]{0:T(1024)S(1)} %reshape.43.tiles, f32[6,144,128]{2,1,0:T(8,128)S(1)} %get-tuple-element.19.home.coords, f32[6,144,128]{2,1,0:T(8,128)S(1)} %collective-permute-done.4.east, ...), custom_call_target="tpu_custom_call" | custom-call | tf_op jit(solution)/shard_map/pair/pallas_call | solution.py:340
  93.5 0.1 collective-permute-start.7
  93.6 10.0 %collective-permute-done.7.east = f32[6,144,128]{2,1,0:T(8,128)S(1)} collective-permute-done((f32[6,144,128]{2,1,0:T(8,128)S(1)}, f32[6,144,128]{2,1,0:T(8,128)S(1)}, u32[]{:S(2)}, u32[]{:S(2)}) %collective-permute-start.7) | collective-permute-done | bytes 442400 | tf_op jit(solution)/shard_map/ppermute | solution.py:31
  103.6 6.8 %collective-permute-start.8 = (f32[3,144,128]{2,1,0:T(8,128)S(1)}, f32[3,144,128]{2,1,0:T(8,128)S(1)}, u32[]{:S(2)}, u32[]{:S(2)}) collective-permute-start(f32[3,144,128]{2,1,0:T(8,128)S(1)} %slice_add_fusion), channel_id=1, source_target_pairs={{0,1},{1,2},{2,3},{3,4},{4,5},{5,6},{6,7},{7,8},{8,9},{9,10},{10,1... | collective-permute-start | bytes 663560 | tf_op jit(solution)/shard_map/ppermute | solution.py:33
  110.5 3.5 %collective-permute-done.8.north = f32[3,144,128]{2,1,0:T(8,128)S(1)} collective-permute-done((f32[3,144,128]{2,1,0:T(8,128)S(1)}, f32[3,144,128]{2,1,0:T(8,128)S(1)}, u32[]{:S(2)}, u32[]{:S(2)}) %collective-permute-start.8) | collective-permute-done | bytes 221216 | tf_op jit(solution)/shard_map/ppermute | solution.py:33
  113.9 0.9 update.1
  (5 shorter events, 0.1 us)
Async XLA Ops:
  3.8 9.4 %copy-start = (f32[8,24,128]{2,1,0:T(8,128)S(1)}, f32[8,24,128]{2,1,0:T(8,128)}, u32[]{:S(2)}) copy-start(f32[8,24,128]{2,1,0:T(8,128)} %pack.1.parcels) | copy-start | bytes 294916
  4.7 4.7 %collective-permute-start.1 = (f32[3,24,128]{2,1,0:T(8,128)S(1)}, f32[3,24,128]{2,1,0:T(8,128)S(1)}, u32[]{:S(2)}, u32[]{:S(2)}) collective-permute-start(f32[3,24,128]{2,1,0:T(8,128)S(1)} %get-tuple-element.33), channel_id=1, source_target_pairs={{0,240},{16,0},{32,16},{48,32},{64,48},{80,64},{96,80},{112,96},{1... | collective-permute-start | bytes 110600 | tf_op jit(solution)/shard_map/ppermute | solution.py:31
  7.8 5.5 %collective-permute-start = (f32[3,24,128]{2,1,0:T(8,128)S(1)}, f32[3,24,128]{2,1,0:T(8,128)S(1)}, u32[]{:S(2)}, u32[]{:S(2)}) collective-permute-start(f32[3,24,128]{2,1,0:T(8,128)S(1)} %get-tuple-element.34), channel_id=1, source_target_pairs={{0,16},{16,32},{32,48},{48,64},{64,80},{80,96},{96,112},{112,128},... | collective-permute-start | bytes 110600 | tf_op jit(solution)/shard_map/ppermute | solution.py:31
  13.3 7.6 %collective-permute-start.2 = (f32[3,24,128]{2,1,0:T(8,128)S(1)}, f32[3,24,128]{2,1,0:T(8,128)S(1)}, u32[]{:S(2)}, u32[]{:S(2)}) collective-permute-start(f32[3,24,128]{2,1,0:T(8,128)S(1)} %get-tuple-element.17), channel_id=1, source_target_pairs={{0,1},{1,2},{2,3},{3,4},{4,5},{5,6},{6,7},{7,8},{8,9},{9,10},{10,1... | collective-permute-start | bytes 110600 | tf_op jit(solution)/shard_map/ppermute | solution.py:33
  16.5 5.5 %collective-permute-start.3 = (f32[3,24,128]{2,1,0:T(8,128)S(1)}, f32[3,24,128]{2,1,0:T(8,128)S(1)}, u32[]{:S(2)}, u32[]{:S(2)}) collective-permute-start(f32[3,24,128]{2,1,0:T(8,128)S(1)} %get-tuple-element.18), channel_id=1, source_target_pairs={{0,15},{1,0},{2,1},{3,2},{4,3},{5,4},{6,5},{7,6},{8,7},{9,8},{10,9... | collective-permute-start | bytes 110600 | tf_op jit(solution)/shard_map/ppermute | solution.py:33
  22.0 1.1 copy-start.1
  23.1 15.3 %copy-start.2 = (s32[1,1,2304,2]{2,3,1,0:T(2,128)S(1)}, s32[1,1,2304,2]{2,3,1,0:T(2,128)}, u32[]{:S(2)}) copy-start(s32[1,1,2304,2]{2,3,1,0:T(2,128)} %param.15) | copy-start | bytes 55300
  24.0 14.4 %collective-permute-start.5 = (f32[6,144,128]{2,1,0:T(8,128)S(1)}, f32[6,144,128]{2,1,0:T(8,128)S(1)}, u32[]{:S(2)}, u32[]{:S(2)}) collective-permute-start(f32[6,144,128]{2,1,0:T(8,128)S(1)} %get-tuple-element.19.home.coords), channel_id=1, source_target_pairs={{0,15},{1,0},{2,1},{3,2},{4,3},{5,4},{6,5},{7,6},{8,7},{9,8},{10,9... | collective-permute-start | bytes 1327112 | tf_op jit(solution)/shard_map/ppermute | solution.py:33
  26.2 12.3 %collective-permute-start.4 = (f32[6,144,128]{2,1,0:T(8,128)S(1)}, f32[6,144,128]{2,1,0:T(8,128)S(1)}, u32[]{:S(2)}, u32[]{:S(2)}) collective-permute-start(f32[6,144,128]{2,1,0:T(8,128)S(1)} %get-tuple-element.19.home.coords), channel_id=1, source_target_pairs={{0,240},{16,0},{32,16},{48,32},{64,48},{80,64},{96,80},{112,96},{1... | collective-permute-start | bytes 1327112 | tf_op jit(solution)/shard_map/ppermute | solution.py:31
  38.4 5.8 %collective-permute-start.6 = (f32[6,144,128]{2,1,0:T(8,128)S(1)}, f32[6,144,128]{2,1,0:T(8,128)S(1)}, u32[]{:S(2)}, u32[]{:S(2)}) collective-permute-start(f32[6,144,128]{2,1,0:T(8,128)S(1)} %collective-permute-done.5.north), channel_id=1, source_target_pairs={{0,240},{16,0},{32,16},{48,32},{64,48},{80,64},{96,80},{112,96},{1... | collective-permute-start | bytes 1327112 | tf_op jit(solution)/shard_map/ppermute | solution.py:31
  93.5 10.1 %collective-permute-start.7 = (f32[6,144,128]{2,1,0:T(8,128)S(1)}, f32[6,144,128]{2,1,0:T(8,128)S(1)}, u32[]{:S(2)}, u32[]{:S(2)}) collective-permute-start(f32[6,144,128]{2,1,0:T(8,128)S(1)} %get-tuple-element.21), channel_id=1, source_target_pairs={{0,16},{16,32},{32,48},{48,64},{64,80},{80,96},{96,112},{112,128},... | collective-permute-start | bytes 1327112 | tf_op jit(solution)/shard_map/ppermute | solution.py:31
  103.6 10.3 %collective-permute-start.8 = (f32[3,144,128]{2,1,0:T(8,128)S(1)}, f32[3,144,128]{2,1,0:T(8,128)S(1)}, u32[]{:S(2)}, u32[]{:S(2)}) collective-permute-start(f32[3,144,128]{2,1,0:T(8,128)S(1)} %slice_add_fusion), channel_id=1, source_target_pairs={{0,1},{1,2},{2,3},{3,4},{4,5},{5,6},{6,7},{7,8},{8,9},{9,10},{10,1... | collective-permute-start | bytes 663560 | tf_op jit(solution)/shard_map/ppermute | solution.py:33

commit v3 on v2

--- a/solution.py
+++ b/solution.py
@@ -13,16 +13,8 @@
 CELL = 2.0
 TSTEP = 0.05
 OFFSETS = ((0, 0), (1, 0), (-1, 0), (0, 1), (0, -1), (1, 1), (1, -1), (-1, 1), (-1, -1))
-RECIP_GAP = (
-    0.004694723058491945,
-    5.942236423492432,
-    -13.92039680480957,
-    18.602458953857422,
-    -16.470346450805664,
-    9.659473419189453,
-    -3.41253399848938,
-    0.5484030246734619,
-)
+LOG2E = 1.4426950408889634
+HALFC = 1.1283791670955126
 
 
 def passed_along(value, step_x, step_y):
@@ -61,7 +53,8 @@
 
 
 def pack_kernel(*refs):
-    sources, parcels, scratch, tally, arrival = refs[:7], refs[7], refs[8:15], refs[15], refs[16]
+    sources, outs, scratch, tally, arrival = refs[:7], refs[7:10], refs[10:17], refs[17], refs[18]
+    parcels = refs[19]
     move = scratch[0]
     copies = fetch(sources, scratch, arrival)
     zero = jnp.zeros((8, BLOCK), jnp.float32)
@@ -99,6 +92,9 @@
             if step_y != 0:
                 parcels[to, 10 * n + 1 : 10 * n + 2, :] = parcels[to, 10 * n + 1 : 10 * n + 2, :] - step_y * CELL
         parcels[to, 20:21, :] = jnp.broadcast_to(tally[code], (1, BLOCK)).astype(jnp.float32)
+    for ref, first in zip(outs, (0, 3, 6)):
+        for p in range(ref.shape[0]):
+            ref[p] = parcels[first + p]
 
 
 def stay_kernel(*refs):
@@ -123,8 +119,8 @@
     staying[0] = kept
 
 
-def turn_kernel(parcels, left, right, up, down):
-    up[0], down[0] = parcels[6], parcels[7]
+def turn_kernel(staying, own, left, right, up, down):
+    up[0], down[0] = own[0], own[1]
     up[1], down[1] = left[1], left[2]
     up[2], down[2] = right[1], right[2]
 
@@ -163,19 +159,20 @@
     return (b // 8) * 256 + (b % 8) * 16
 
 
-def pair_kernel(tiles, home, east, north, corner, fh, fx, fn, zone, ac0, ac1, ac2, ibuf0, ibuf1, vbuf0, vbuf1, wbuf, *, T=2, mxu=True):
+def pair_kernel(tiles, home, east, north, corner, fh, fe, fn, fc, zone, ac0, ac1, ac2, ibuf0, ibuf1, vbuf0, vbuf1, wbuf, *, T=2, mxu=True):
     acc=(ac0,ac1,ac2)
     sub = lax.broadcasted_iota(jnp.int32,(8,128),0)
     lane = lax.broadcasted_iota(jnp.int32,(8,128),1)
     rel = lane//4 - sub//4
     for c in range(16):
-        wbuf[c]=jnp.where(rel==2*c,0.0,1.0)
-    wbuf[16]=jnp.ones((8,128),jnp.float32)
+        wbuf[c]=jnp.where(rel==2*c,0.0,4.0)
+    wbuf[16]=jnp.full((8,128),4.0,jnp.float32)
     for z,(ref,sx,sy) in enumerate(((home,0.,0.),(east,2.,0.),(north,0.,2.),(corner,2.,2.))):
         for f in range(6):
             v = ref[f]
             if f==0 and sx: v=v+sx
             if f==1 and sy: v=v+sy
+            if f<3: v=v*2.0
             zone[f, pl.ds(z*CAPACITY,CAPACITY), :] = v
     zero = jnp.zeros((8,128),jnp.float32)
     def clear(k,_):
@@ -187,7 +184,7 @@
 
     def row(f,j):
         return jnp.broadcast_to(zone[f, pl.ds(j,1), :],(8,128))
-    SC=jnp.where(sub==4,12.0,jnp.where(sub==5,6.0,1.0)).astype(jnp.float32)
+    SC=jnp.where(sub==4,6144.0,jnp.where(sub==5,48.0,jnp.where(sub==3,0.25,2.0))).astype(jnp.float32)
     kk=lax.broadcasted_iota(jnp.int32,(24,768),0); nn=lax.broadcasted_iota(jnp.int32,(24,768),1)
     pick=jnp.where(kk%8==nn//128,1.0,0.0).astype(jnp.bfloat16)
 
@@ -227,14 +224,13 @@
                 dx=xi-row(0,j); dy=yi-row(1,j); dz=zi-row(2,j)
                 r2=dx*dx+dy*dy+dz*dz
                 w=jnp.maximum(wbuf[jnp.where(j==b,c,16)]-r2,0.0)
-                s=jnp.clip(r2,0.25,1.0)
+                s=jnp.clip(r2,1.0,4.0)
                 rs=lax.rsqrt(s)
                 inv=rs*rs
                 cube=inv*inv*inv
-                h=RECIP_GAP[-1]
-                for n in range(len(RECIP_GAP)-2,-1,-1):
-                    h=h*s+RECIP_GAP[n]
-                g=(qi*row(3,j))*(rs-h)+cube*((ai*row(4,j))*cube-bi*row(5,j))
+                ew=jnp.exp2(s*-LOG2E)
+                kc=(1.0-lax.erf(s*rs))*rs+ew*HALFC
+                g=(qi*row(3,j))*kc+cube*((ai*row(4,j))*cube-bi*row(5,j))
                 g=g*(inv*(w*w))
                 vbuf[0,t,c]=g*dx
                 vbuf[1,t,c]=g*dy
@@ -244,29 +240,28 @@
     for d in range(3):
         for t in range(T):
             for c in range(16): vbuf1[d,t,c]=zero
-    def two(k,_):
-        b=2*k
-        settle(jnp.maximum(b-1,0),vbuf1)
-        spread(b+1,ibuf1)
-        block(b,ibuf0,vbuf0)
-        settle(b,vbuf0)
-        spread(jnp.minimum(b+2,CAPACITY-1),ibuf0)
-        block(b+1,ibuf1,vbuf1)
+    ib=(ibuf0,ibuf0); vb=(vbuf0,vbuf1)
+    def some(k,_):
+        b=4*k
+        for n in range(4):
+            settle(jnp.maximum(b+n-1,0),vb[(n+1)%2])
+            pass
+            block(b+n,ib[n%2],vb[n%2])
+            spread(jnp.minimum(b+n+1,CAPACITY-1),ib[(n+1)%2])
         return 0
-    lax.fori_loop(0,CAPACITY//2,two,0)
-    settle(CAPACITY-1,vbuf1)
+    lax.fori_loop(0,CAPACITY//4,some,0)
+    settle(CAPACITY-1,vb[1])
     for d in range(3):
-        for z,(ref,o) in enumerate(((fh,0),(fx,0),(fn,0),(fx,3))):
+        for z,ref in enumerate((fh,fe,fn,fc)):
             def red(k,_):
                 for u in range(3):
                     k8=pl.multiple_of(k*24+8*u,8)
                     r=[acc[d][pl.ds((z*CAPACITY+k8)*8+q,8,stride=8),:] for q in range(8)]
                     r=((r[0]+r[1])+(r[2]+r[3]))+((r[4]+r[5])+(r[6]+r[7]))
-                    if z==0: ref[o+d,pl.ds(k8,8),:]=ref[o+d,pl.ds(k8,8),:]-r
-                    else: ref[o+d,pl.ds(k8,8),:]=-r
+                    if z==0: ref[d,pl.ds(k8,8),:]=ref[d,pl.ds(k8,8),:]-r
+                    else: ref[d,pl.ds(k8,8),:]=-r
                 return 0
             lax.fori_loop(0,CAPACITY//24,red,0)
-
 
 VM = pl.BlockSpec(memory_space=pltpu.VMEM)
 SM = pl.BlockSpec(memory_space=pltpu.SMEM)
@@ -294,17 +289,18 @@
         + [pltpu.VMEM((3, NB, BLOCK), jnp.float32)] * 2
         + [pltpu.VMEM((NB, BLOCK), jnp.float32)] * 4
     )
-    parcels = pl.pallas_call(
+    going_up_x, going_down_x, own = pl.pallas_call(
         pack_kernel,
-        out_shape=planes(8, 24),
+        out_shape=(planes(3, 24), planes(3, 24), planes(2, 24)),
         in_specs=[HBM] * 7,
-        out_specs=VM,
-        scratch_shapes=held + [pltpu.SMEM((18,), jnp.int32), pltpu.SemaphoreType.DMA((7,))],
+        out_specs=(VM,) * 3,
+        scratch_shapes=held
+        + [pltpu.SMEM((18,), jnp.int32), pltpu.SemaphoreType.DMA((7,)), pltpu.VMEM((8, 24, BLOCK), jnp.float32)],
         compiler_params=WIDE,
         name="pack",
     )(*inputs)
-    left = passed_along(parcels[0:3], 1, 0)
-    right = passed_along(parcels[3:6], -1, 0)
+    left = passed_along(going_up_x, 1, 0)
+    right = passed_along(going_down_x, -1, 0)
     stay, staying = pl.pallas_call(
         stay_kernel,
         out_shape=(planes(10), jax.ShapeDtypeStruct((1,), jnp.int32)),
@@ -318,11 +314,11 @@
     up, down = pl.pallas_call(
         turn_kernel,
         out_shape=(planes(3, 24),) * 2,
-        in_specs=[VM] * 3,
+        in_specs=[SM] + [VM] * 3,
         out_specs=(VM,) * 2,
         compiler_params=PARAMS,
         name="turn",
-    )(parcels, left, right)
+    )(staying, own, left, right)
     up = passed_along(up, 0, 1)
     down = passed_along(down, 0, -1)
     coords, rest = pl.pallas_call(
@@ -337,17 +333,18 @@
     east = passed_along(coords, -1, 0)
     north = passed_along(coords, 0, -1)
     corner = passed_along(north, -1, 0)
-    on_home, on_x, on_north = pl.pallas_call(
+    on_home, on_east, on_north, on_corner = pl.pallas_call(
         pair_kernel,
-        out_shape=(planes(3), planes(6), planes(3)),
+        out_shape=(planes(3),) * 4,
         in_specs=[SM] + [VM] * 4,
-        out_specs=(VM,) * 3,
+        out_specs=(VM,) * 4,
         scratch_shapes=[pltpu.VMEM((6,4 * CAPACITY,128),jnp.float32)]+[pltpu.VMEM((4 * CAPACITY*8,128),jnp.float32)]*3+[pltpu.VMEM((6,16,8,128),jnp.float32)]*2+[pltpu.VMEM((3,2,16,8,128),jnp.float32)]*2+[pltpu.VMEM((17,8,128),jnp.float32)],
         compiler_params=PARAMS,
         name="pair",
     )(tiles.reshape(18, 128, 2).transpose(0, 2, 1).reshape(-1), coords, east, north, corner)
-    from_x = passed_along(on_x, 1, 0)
-    from_north = passed_along(on_north + from_x[3:6], 0, 1)
+    from_corner = passed_along(on_corner, 1, 0)
+    from_east = passed_along(on_east, 1, 0)
+    from_north = passed_along(on_north + from_corner, 0, 1)
     out = pl.pallas_call(
         update_kernel,
         out_shape=(planes(3),) * 3,
@@ -355,7 +352,7 @@
         out_specs=(VM,) * 3,
         compiler_params=PARAMS,
         name="update",
-    )(on_home, from_x, from_north, coords, rest)
+    )(on_home, from_east, from_north, coords, rest)
     return tuple(value.reshape(3, 1, 1, CAPACITY * BLOCK) for value in out)
 
 

time: 116 us -> 111 us (0.957)
  waiting for transfers between devices: 38 us -> 34.3 us
  Pallas kernels: 57.3 us -> 54.5 us
  starting transfers between devices: 16.7 us -> 19 us
    ppermute x5 -> x6, waiting for transfers between devices: 21.2 us -> 13.5 us  [passed_along(): lax.ppermute(value, 'gx', [(s, (s + step_x) % nx) for s in range(nx)])]
    ppermute x4, waiting for transfers between devices: 16.7 us -> 20.8 us  [passed_along(): lax.ppermute(value, 'gy', [(s, (s + step_y) % ny) for s in range(ny)])]
    pallas_call x3, Pallas kernels: 52.5 us -> 49.7 us  [the longest x1 45.9 us: body(): pl.pallas_call(pair_kernel, out_shape=(planes(3),) * 4, in_specs=[SM] + [...]
    ppermute x5 -> x6, starting transfers between devices: 3.17 us -> 5.58 us  [passed_along(): lax.ppermute(value, 'gx', [(s, (s + step_x) % nx) for s in range(nx)])]
  transfers between devices with their start and end apart: 9 -> 10, of which waited for: 7 -> 6; matrix products, arithmetic and copies ran while one was open for 0% -> 0% of each run, Pallas kernels for 3% -> 3%
where the time goes in v3:
time: 111 us; the launch traced here: 110 us
  Pallas kernels  54.5 us (49%)
  waiting for transfers between devices  34.3 us (31%)
  starting transfers between devices  19 us (17%)
  local copies, waits for them, and re-layouts  1.17 us (1%)
    pallas_call x1, Pallas kernels, body(): pl.pallas_call(pair_kernel, out_shape=(planes(3),) * 4, in_specs=[SM] + [...  45.9 us
    ppermute x4, waiting for transfers between devices, passed_along(): lax.ppermute(value, 'gy', [(s, (s + step_y) % ny) for s in range(ny)])  20.8 us
    ppermute x6, waiting for transfers between devices, passed_along(): lax.ppermute(value, 'gx', [(s, (s + step_x) % nx) for s in range(nx)])  13.5 us
    ppermute x4, starting transfers between devices, passed_along(): lax.ppermute(value, 'gy', [(s, (s + step_y) % ny) for s in range(ny)])  13.4 us
    ppermute x6, starting transfers between devices, passed_along(): lax.ppermute(value, 'gx', [(s, (s + step_x) % nx) for s in range(nx)])  5.58 us
    pallas_call x1, Pallas kernels, body(): pl.pallas_call(pack_kernel, out_shape=(planes(3, 24), planes(3, 24), plan...  3.09 us
    pallas_call x1, Pallas kernels, body(): pl.pallas_call(stay_kernel, out_shape=(planes(10), jax.ShapeDtypeStruct((...  3.08 us
  transfers between devices with their start and end apart: 10, of which 6 were waited for; matrix products, arithmetic and copies ran while one was open for 0% of the time, Pallas kernels for 3%

profile of v3, /device:TPU:96, one launch (start us, length us, event | category | flops | bytes accessed | tf_op | source)
XLA Modules:
  0.0 109.8 jit_solution(11397503747411332855)
XLA Ops:
  0.6 3.1 %pack.1 = (f32[3,24,128]{2,1,0:T(8,128)}, f32[3,24,128]{2,1,0:T(8,128)}, f32[2,24,128]{2,1,0:T(8,128)}) custom-call(s32[128]{0:T(128)} %bitcast.28, f32[3,128,128]{2,1,0:T(8,128)} %bitcast.15, f32[3,128,128]{2,1,0:T(8,128)} %bitcast.17, f32[128,128]{1,0:T(8,128)} %bitcast.19, f32[128,128]{1,0:T(8,128)} %bitcast.21, f32[128,128]{1,0:T(8,128)} %bitcast.23, ...), custom_call_target="tpu_custom_call" | custom-call | tf_op jit(solution)/shard_map/pack/pallas_call | solution.py:292
  3.7 0.1 collective-permute-start
  3.8 0.0 copy-start.1
  3.8 3.8 %collective-permute-start.1 = (f32[3,24,128]{2,1,0:T(8,128)}, f32[3,24,128]{2,1,0:T(8,128)S(1)}, u32[]{:S(2)}, u32[]{:S(2)}) collective-permute-start(f32[3,24,128]{2,1,0:T(8,128)} %get-tuple-element.22), channel_id=1, source_target_pairs={{0,240},{16,0},{32,16},{48,32},{64,48},{80,64},{96,80},{112,96},{1... | collective-permute-start | bytes 110600 | tf_op jit(solution)/shard_map/ppermute | solution.py:23
  7.7 3.1 %stay.1 = (f32[10,144,128]{2,1,0:T(8,128)}, s32[1]{0:T(128)}) custom-call(s32[128]{0:T(128)} %bitcast.29, f32[3,128,128]{2,1,0:T(8,128)} %bitcast.16, f32[3,128,128]{2,1,0:T(8,128)} %bitcast.18, f32[128,128]{1,0:T(8,128)} %bitcast.20, f32[128,128]{1,0:T(8,128)} %bitcast.22, f32[128,128]{1,0:T(8,128)} %bitcast.24, f32[128,128]{1,0:T(8,128)} %bitcast.26), custom_call_target="tpu_custom_call" | custom-call | bytes 6000000 | tf_op jit(solution)/shard_map/stay/pallas_call | solution.py:304
  10.7 0.0 collective-permute-done.left.refs_0_
  10.8 0.0 collective-permute-done.1.right.refs_1_
  10.8 0.0 copy-done.1
  10.8 0.7 turn.1
  11.5 2.9 %collective-permute-start.2 = (f32[3,24,128]{2,1,0:T(8,128)S(1)}, f32[3,24,128]{2,1,0:T(8,128)S(1)}, u32[]{:S(2)}, u32[]{:S(2)}) collective-permute-start(f32[3,24,128]{2,1,0:T(8,128)S(1)} %get-tuple-element.24), channel_id=1, source_target_pairs={{0,1},{1,2},{2,3},{3,4},{4,5},{5,6},{6,7},{7,8},{8,9},{9,10},{10,1... | collective-permute-start | bytes 110600 | tf_op jit(solution)/shard_map/ppermute | solution.py:25
  14.4 1.6 %collective-permute-start.3 = (f32[3,24,128]{2,1,0:T(8,128)S(1)}, f32[3,24,128]{2,1,0:T(8,128)S(1)}, u32[]{:S(2)}, u32[]{:S(2)}) collective-permute-start(f32[3,24,128]{2,1,0:T(8,128)S(1)} %get-tuple-element.25), channel_id=1, source_target_pairs={{0,15},{1,0},{2,1},{3,2},{4,3},{5,4},{6,5},{7,6},{8,7},{9,8},{10,9... | collective-permute-start | bytes 110600 | tf_op jit(solution)/shard_map/ppermute | solution.py:25
  16.0 1.9 %collective-permute-done.2.refs_2_ = f32[3,24,128]{2,1,0:T(8,128)S(1)} collective-permute-done((f32[3,24,128]{2,1,0:T(8,128)S(1)}, f32[3,24,128]{2,1,0:T(8,128)S(1)}, u32[]{:S(2)}, u32[]{:S(2)}) %collective-permute-start.2) | collective-permute-done | bytes 36896 | tf_op jit(solution)/shard_map/ppermute | solution.py:25
  17.9 2.0 %collective-permute-done.3.refs_3_ = f32[3,24,128]{2,1,0:T(8,128)S(1)} collective-permute-done((f32[3,24,128]{2,1,0:T(8,128)S(1)}, f32[3,24,128]{2,1,0:T(8,128)S(1)}, u32[]{:S(2)}, u32[]{:S(2)}) %collective-permute-start.3) | collective-permute-done | bytes 36896 | tf_op jit(solution)/shard_map/ppermute | solution.py:25
  19.9 0.0 copy-start
  19.9 1.1 %copy-done = f32[10,144,128]{2,1,0:T(8,128)S(1)} copy-done((f32[10,144,128]{2,1,0:T(8,128)S(1)}, f32[10,144,128]{2,1,0:T(8,128)}, u32[]{:S(2)}) %copy-start) | copy-done | bytes 737304
  21.0 0.0 copy-start.2
  21.0 0.9 arrive.1
  21.9 2.5 %collective-permute-start.5 = (f32[6,144,128]{2,1,0:T(8,128)S(1)}, f32[6,144,128]{2,1,0:T(8,128)S(1)}, u32[]{:S(2)}, u32[]{:S(2)}) collective-permute-start(f32[6,144,128]{2,1,0:T(8,128)S(1)} %get-tuple-element.26.home.coords), channel_id=1, source_target_pairs={{0,15},{1,0},{2,1},{3,2},{4,3},{5,4},{6,5},{7,6},{8,7},{9,8},{10,9... | collective-permute-start | bytes 1327112 | tf_op jit(solution)/shard_map/ppermute | solution.py:25
  24.4 1.5 %collective-permute-start.4 = (f32[6,144,128]{2,1,0:T(8,128)S(1)}, f32[6,144,128]{2,1,0:T(8,128)S(1)}, u32[]{:S(2)}, u32[]{:S(2)}) collective-permute-start(f32[6,144,128]{2,1,0:T(8,128)S(1)} %get-tuple-element.26.home.coords), channel_id=1, source_target_pairs={{0,240},{16,0},{32,16},{48,32},{64,48},{80,64},{96,80},{112,96},{1... | collective-permute-start | bytes 1327112 | tf_op jit(solution)/shard_map/ppermute | solution.py:23
  25.9 13.4 %collective-permute-done.5.north = f32[6,144,128]{2,1,0:T(8,128)S(1)} collective-permute-done((f32[6,144,128]{2,1,0:T(8,128)S(1)}, f32[6,144,128]{2,1,0:T(8,128)S(1)}, u32[]{:S(2)}, u32[]{:S(2)}) %collective-permute-start.5) | collective-permute-done | bytes 442400 | tf_op jit(solution)/shard_map/ppermute | solution.py:25
  39.4 0.0 collective-permute-start.6
  39.4 0.0 copy-done.2
  39.4 0.0 collective-permute-done.4.east
  39.4 6.0 %collective-permute-done.6.corner = f32[6,144,128]{2,1,0:T(8,128)S(1)} collective-permute-done((f32[6,144,128]{2,1,0:T(8,128)S(1)}, f32[6,144,128]{2,1,0:T(8,128)S(1)}, u32[]{:S(2)}, u32[]{:S(2)}) %collective-permute-start.6) | collective-permute-done | bytes 442400 | tf_op jit(solution)/shard_map/ppermute | solution.py:23
  45.4 45.9 %pair.1 = (f32[3,144,128]{2,1,0:T(8,128)S(1)}, f32[3,144,128]{2,1,0:T(8,128)S(1)}, f32[3,144,128]{2,1,0:T(8,128)S(1)}, f32[3,144,128]{2,1,0:T(8,128)S(1)}) custom-call(s32[4608]{0:T(1024)S(1)} %reshape.43.tiles, f32[6,144,128]{2,1,0:T(8,128)S(1)} %get-tuple-element.26.home.coords, f32[6,144,128]{2,1,0:T(8,128)S(1)} %collective-permute-done.4.east, ...), custom_call_target="tpu_custom_call" | custom-call | tf_op jit(solution)/shard_map/pair/pallas_call | solution.py:336
  91.3 0.1 collective-permute-start.8
  91.4 0.1 collective-permute-start.7
  91.5 7.6 %collective-permute-done.8 = f32[3,144,128]{2,1,0:T(8,128)S(1)} collective-permute-done((f32[3,144,128]{2,1,0:T(8,128)S(1)}, f32[3,144,128]{2,1,0:T(8,128)S(1)}, u32[]{:S(2)}, u32[]{:S(2)}) %collective-permute-start.8) | collective-permute-done | bytes 221216 | tf_op jit(solution)/shard_map/ppermute | solution.py:23
  99.0 6.3 %collective-permute-start.9 = (f32[3,144,128]{2,1,0:T(8,128)S(1)}, f32[3,144,128]{2,1,0:T(8,128)S(1)}, u32[]{:S(2)}, u32[]{:S(2)}) collective-permute-start(f32[3,144,128]{2,1,0:T(8,128)S(1)} %add.3), channel_id=1, source_target_pairs={{0,1},{1,2},{2,3},{3,4},{4,5},{5,6},{6,7},{7,8},{8,9},{9,10},{10,1... | collective-permute-start | bytes 663560 | tf_op jit(solution)/shard_map/ppermute | solution.py:25
  105.4 0.0 collective-permute-done.7.east
  105.4 3.4 %collective-permute-done.9.north = f32[3,144,128]{2,1,0:T(8,128)S(1)} collective-permute-done((f32[3,144,128]{2,1,0:T(8,128)S(1)}, f32[3,144,128]{2,1,0:T(8,128)S(1)}, u32[]{:S(2)}, u32[]{:S(2)}) %collective-permute-start.9) | collective-permute-done | bytes 221216 | tf_op jit(solution)/shard_map/ppermute | solution.py:25
  108.8 0.9 update.1
  (4 shorter events, 0.1 us)
Async XLA Ops:
  3.7 7.0 %collective-permute-start = (f32[3,24,128]{2,1,0:T(8,128)}, f32[3,24,128]{2,1,0:T(8,128)S(1)}, u32[]{:S(2)}, u32[]{:S(2)}) collective-permute-start(f32[3,24,128]{2,1,0:T(8,128)} %get-tuple-element.21), channel_id=1, source_target_pairs={{0,16},{16,32},{32,48},{48,64},{64,80},{80,96},{96,112},{112,128},... | collective-permute-start | bytes 110600 | tf_op jit(solution)/shard_map/ppermute | solution.py:23
  3.8 7.0 %copy-start.1 = (f32[2,24,128]{2,1,0:T(8,128)S(1)}, f32[2,24,128]{2,1,0:T(8,128)}, u32[]{:S(2)}) copy-start(f32[2,24,128]{2,1,0:T(8,128)} %get-tuple-element.23.own) | copy-start | bytes 73732
  3.8 6.9 %collective-permute-start.1 = (f32[3,24,128]{2,1,0:T(8,128)}, f32[3,24,128]{2,1,0:T(8,128)S(1)}, u32[]{:S(2)}, u32[]{:S(2)}) collective-permute-start(f32[3,24,128]{2,1,0:T(8,128)} %get-tuple-element.22), channel_id=1, source_target_pairs={{0,240},{16,0},{32,16},{48,32},{64,48},{80,64},{96,80},{112,96},{1... | collective-permute-start | bytes 110600 | tf_op jit(solution)/shard_map/ppermute | solution.py:23
  11.5 6.4 %collective-permute-start.2 = (f32[3,24,128]{2,1,0:T(8,128)S(1)}, f32[3,24,128]{2,1,0:T(8,128)S(1)}, u32[]{:S(2)}, u32[]{:S(2)}) collective-permute-start(f32[3,24,128]{2,1,0:T(8,128)S(1)} %get-tuple-element.24), channel_id=1, source_target_pairs={{0,1},{1,2},{2,3},{3,4},{4,5},{5,6},{6,7},{7,8},{8,9},{9,10},{10,1... | collective-permute-start | bytes 110600 | tf_op jit(solution)/shard_map/ppermute | solution.py:25
  14.4 5.5 %collective-permute-start.3 = (f32[3,24,128]{2,1,0:T(8,128)S(1)}, f32[3,24,128]{2,1,0:T(8,128)S(1)}, u32[]{:S(2)}, u32[]{:S(2)}) collective-permute-start(f32[3,24,128]{2,1,0:T(8,128)S(1)} %get-tuple-element.25), channel_id=1, source_target_pairs={{0,15},{1,0},{2,1},{3,2},{4,3},{5,4},{6,5},{7,6},{8,7},{9,8},{10,9... | collective-permute-start | bytes 110600 | tf_op jit(solution)/shard_map/ppermute | solution.py:25
  19.9 1.1 %copy-start = (f32[10,144,128]{2,1,0:T(8,128)S(1)}, f32[10,144,128]{2,1,0:T(8,128)}, u32[]{:S(2)}) copy-start(f32[10,144,128]{2,1,0:T(8,128)} %get-tuple-element.20.stay) | copy-start | bytes 2211844
  21.0 18.4 %copy-start.2 = (s32[1,1,2304,2]{2,3,1,0:T(2,128)S(1)}, s32[1,1,2304,2]{2,3,1,0:T(2,128)}, u32[]{:S(2)}) copy-start(s32[1,1,2304,2]{2,3,1,0:T(2,128)} %param.15) | copy-start | bytes 55300
  21.9 17.5 %collective-permute-start.5 = (f32[6,144,128]{2,1,0:T(8,128)S(1)}, f32[6,144,128]{2,1,0:T(8,128)S(1)}, u32[]{:S(2)}, u32[]{:S(2)}) collective-permute-start(f32[6,144,128]{2,1,0:T(8,128)S(1)} %get-tuple-element.26.home.coords), channel_id=1, source_target_pairs={{0,15},{1,0},{2,1},{3,2},{4,3},{5,4},{6,5},{7,6},{8,7},{9,8},{10,9... | collective-permute-start | bytes 1327112 | tf_op jit(solution)/shard_map/ppermute | solution.py:25
  24.4 15.0 %collective-permute-start.4 = (f32[6,144,128]{2,1,0:T(8,128)S(1)}, f32[6,144,128]{2,1,0:T(8,128)S(1)}, u32[]{:S(2)}, u32[]{:S(2)}) collective-permute-start(f32[6,144,128]{2,1,0:T(8,128)S(1)} %get-tuple-element.26.home.coords), channel_id=1, source_target_pairs={{0,240},{16,0},{32,16},{48,32},{64,48},{80,64},{96,80},{112,96},{1... | collective-permute-start | bytes 1327112 | tf_op jit(solution)/shard_map/ppermute | solution.py:23
  39.4 6.0 %collective-permute-start.6 = (f32[6,144,128]{2,1,0:T(8,128)S(1)}, f32[6,144,128]{2,1,0:T(8,128)S(1)}, u32[]{:S(2)}, u32[]{:S(2)}) collective-permute-start(f32[6,144,128]{2,1,0:T(8,128)S(1)} %collective-permute-done.5.north), channel_id=1, source_target_pairs={{0,240},{16,0},{32,16},{48,32},{64,48},{80,64},{96,80},{112,96},{1... | collective-permute-start | bytes 1327112 | tf_op jit(solution)/shard_map/ppermute | solution.py:23
  91.3 7.7 %collective-permute-start.8 = (f32[3,144,128]{2,1,0:T(8,128)S(1)}, f32[3,144,128]{2,1,0:T(8,128)S(1)}, u32[]{:S(2)}, u32[]{:S(2)}) collective-permute-start(f32[3,144,128]{2,1,0:T(8,128)S(1)} %get-tuple-element.30), channel_id=1, source_target_pairs={{0,16},{16,32},{32,48},{48,64},{64,80},{80,96},{96,112},{112,128},... | collective-permute-start | bytes 663560 | tf_op jit(solution)/shard_map/ppermute | solution.py:23
  91.4 14.0 %collective-permute-start.7 = (f32[3,144,128]{2,1,0:T(8,128)S(1)}, f32[3,144,128]{2,1,0:T(8,128)S(1)}, u32[]{:S(2)}, u32[]{:S(2)}) collective-permute-start(f32[3,144,128]{2,1,0:T(8,128)S(1)} %get-tuple-element.28), channel_id=1, source_target_pairs={{0,16},{16,32},{32,48},{48,64},{64,80},{80,96},{96,112},{112,128},... | collective-permute-start | bytes 663560 | tf_op jit(solution)/shard_map/ppermute | solution.py:23
  99.0 9.8 %collective-permute-start.9 = (f32[3,144,128]{2,1,0:T(8,128)S(1)}, f32[3,144,128]{2,1,0:T(8,128)S(1)}, u32[]{:S(2)}, u32[]{:S(2)}) collective-permute-start(f32[3,144,128]{2,1,0:T(8,128)S(1)} %add.3), channel_id=1, source_target_pairs={{0,1},{1,2},{2,3},{3,4},{4,5},{5,6},{6,7},{7,8},{8,9},{9,10},{10,1... | collective-permute-start | bytes 663560 | tf_op jit(solution)/shard_map/ppermute | solution.py:25

commit v4 on v3

--- a/solution.py
+++ b/solution.py
@@ -32,6 +32,19 @@
 
 
 PLACE = (8, 0, 3, 6, 7, 1, 2, 4, 5)
+
+
+def sent(value, step_x, step_y, parity):
+    nx, ny = lax.axis_size("gx"), lax.axis_size("gy")
+    if step_y == 0:
+        return lax.ppermute(value, "gx", [(s, (s + step_x) % nx) for s in range(nx) if s % 2 == parity])
+    pairs = [
+        (i * ny + j, ((i + step_x) % nx) * ny + (j + step_y) % ny)
+        for i in range(nx)
+        for j in range(ny)
+        if i % 2 == parity
+    ]
+    return lax.ppermute(value, ("gx", "gy"), pairs)
 
 
 def fetch(sources, scratch, arrival):
@@ -146,9 +159,9 @@
         rest[k] = held[f, 0:CAPACITY, :]
 
 
-def update_kernel(home, east, north, coords, rest, new_x, new_v, total):
+def update_kernel(home, east, north, far, coords, rest, new_x, new_v, total):
     for d in range(3):
-        force = home[d] + east[d] + north[d]
+        force = home[d] + east[d] + north[d] + far[d]
         fresh = rest[d] + TSTEP * rest[3] * force
         total[d] = force
         new_v[d] = fresh
@@ -159,7 +172,7 @@
     return (b // 8) * 256 + (b % 8) * 16
 
 
-def pair_kernel(tiles, home, east, north, corner, fh, fe, fn, fc, zone, ac0, ac1, ac2, ibuf0, ibuf1, vbuf0, vbuf1, wbuf, *, T=2, mxu=True):
+def pair_kernel(tiles, home, east, north, near, far, fh, fe, fn, fc, zone, ac0, ac1, ac2, ibuf0, ibuf1, vbuf0, vbuf1, wbuf, *, T=2, mxu=True):
     acc=(ac0,ac1,ac2)
     sub = lax.broadcasted_iota(jnp.int32,(8,128),0)
     lane = lax.broadcasted_iota(jnp.int32,(8,128),1)
@@ -167,9 +180,9 @@
     for c in range(16):
         wbuf[c]=jnp.where(rel==2*c,0.0,4.0)
     wbuf[16]=jnp.full((8,128),4.0,jnp.float32)
-    for z,(ref,sx,sy) in enumerate(((home,0.,0.),(east,2.,0.),(north,0.,2.),(corner,2.,2.))):
+    for z,(ref,sx,sy) in enumerate(((home,0.,0.),(east,2.,0.),(north,0.,2.),(near,2.,2.))):
         for f in range(6):
-            v = ref[f]
+            v = ref[f]+far[f] if z==3 else ref[f]
             if f==0 and sx: v=v+sx
             if f==1 and sy: v=v+sy
             if f<3: v=v*2.0
@@ -332,27 +345,29 @@
     )(staying, stay, left, right, up, down)
     east = passed_along(coords, -1, 0)
     north = passed_along(coords, 0, -1)
-    corner = passed_along(north, -1, 0)
+    far = sent(coords, -1, -1, 0)
+    near = sent(north, -1, 0, 1)
     on_home, on_east, on_north, on_corner = pl.pallas_call(
         pair_kernel,
         out_shape=(planes(3),) * 4,
-        in_specs=[SM] + [VM] * 4,
+        in_specs=[SM] + [VM] * 5,
         out_specs=(VM,) * 4,
         scratch_shapes=[pltpu.VMEM((6,4 * CAPACITY,128),jnp.float32)]+[pltpu.VMEM((4 * CAPACITY*8,128),jnp.float32)]*3+[pltpu.VMEM((6,16,8,128),jnp.float32)]*2+[pltpu.VMEM((3,2,16,8,128),jnp.float32)]*2+[pltpu.VMEM((17,8,128),jnp.float32)],
         compiler_params=PARAMS,
         name="pair",
-    )(tiles.reshape(18, 128, 2).transpose(0, 2, 1).reshape(-1), coords, east, north, corner)
-    from_corner = passed_along(on_corner, 1, 0)
+    )(tiles.reshape(18, 128, 2).transpose(0, 2, 1).reshape(-1), coords, east, north, near, far)
+    from_near = sent(on_corner, 1, 0, 0)
+    from_far = sent(on_corner, 1, 1, 1)
     from_east = passed_along(on_east, 1, 0)
-    from_north = passed_along(on_north + from_corner, 0, 1)
+    from_north = passed_along(on_north + from_near, 0, 1)
     out = pl.pallas_call(
         update_kernel,
         out_shape=(planes(3),) * 3,
-        in_specs=[VM] * 5,
+        in_specs=[VM] * 6,
         out_specs=(VM,) * 3,
         compiler_params=PARAMS,
         name="update",
-    )(on_home, from_east, from_north, coords, rest)
+    )(on_home, from_east, from_north, from_far, coords, rest)
     return tuple(value.reshape(3, 1, 1, CAPACITY * BLOCK) for value in out)
 
 

time: 111 us -> 112 us (level)
  starting transfers between devices: 19 us -> 29 us
  waiting for transfers between devices: 34.3 us -> 24.9 us
    ppermute x6 -> x4, starting transfers between devices: 5.58 us -> 13.2 us  [passed_along(): lax.ppermute(value, 'gx', [(s, (s + step_x) % nx) for s in range(nx)])]
    ppermute x4, waiting for transfers between devices: 20.8 us -> 13.2 us  [passed_along(): lax.ppermute(value, 'gy', [(s, (s + step_y) % ny) for s in range(ny)])]
    ppermute x0 -> x4, starting transfers between devices: none -> 7.55 us  [the longest x2 4.07 us: sent(): return lax.ppermute(value, ('gx', 'gy'), pairs)]
    ppermute x6 -> x4, waiting for transfers between devices: 13.5 us -> 8.31 us  [passed_along(): lax.ppermute(value, 'gx', [(s, (s + step_x) % nx) for s in range(nx)])]
    ppermute x4, starting transfers between devices: 13.4 us -> 8.23 us  [passed_along(): lax.ppermute(value, 'gy', [(s, (s + step_y) % ny) for s in range(ny)])]
    ppermute x0 -> x4, waiting for transfers between devices: none -> 3.38 us  [the longest x2 3.38 us: sent(): return lax.ppermute(value, ('gx', 'gy'), pairs)]
  transfers between devices with their start and end apart: 10 -> 12, of which waited for: 6 -> 6; matrix products, arithmetic and copies ran while one was open for 0% -> 0% of each run, Pallas kernels for 3% -> 3%
where the time goes in v4:
time: 112 us; the launch traced here: 110 us
  Pallas kernels  54.4 us (49%)
  starting transfers between devices  29 us (26%)
  waiting for transfers between devices  24.9 us (22%)
  local copies, waits for them, and re-layouts  1.17 us (1%)
    pallas_call x1, Pallas kernels, body(): pl.pallas_call(pair_kernel, out_shape=(planes(3),) * 4, in_specs=[SM] + [...  45.9 us
    ppermute x4, starting transfers between devices, passed_along(): lax.ppermute(value, 'gx', [(s, (s + step_x) % nx) for s in range(nx)])  13.2 us
    ppermute x4, waiting for transfers between devices, passed_along(): lax.ppermute(value, 'gy', [(s, (s + step_y) % ny) for s in range(ny)])  13.2 us
    ppermute x4, waiting for transfers between devices, passed_along(): lax.ppermute(value, 'gx', [(s, (s + step_x) % nx) for s in range(nx)])  8.31 us
    ppermute x4, starting transfers between devices, passed_along(): lax.ppermute(value, 'gy', [(s, (s + step_y) % ny) for s in range(ny)])  8.23 us
    ppermute x2, starting transfers between devices, sent(): return lax.ppermute(value, ('gx', 'gy'), pairs)  4.07 us
    ppermute x2, starting transfers between devices, sent(): lax.ppermute(value, 'gx', [(s, (s + step_x) % nx) for s in range(nx) if s...  3.48 us
    ppermute x2, waiting for transfers between devices, sent(): return lax.ppermute(value, ('gx', 'gy'), pairs)  3.38 us
  transfers between devices with their start and end apart: 12, of which 6 were waited for; matrix products, arithmetic and copies ran while one was open for 0% of the time, Pallas kernels for 3%

profile of v4, /device:TPU:96, one launch (start us, length us, event | category | flops | bytes accessed | tf_op | source)
XLA Modules:
  0.0 110.2 jit_solution(8235502409150875548)
XLA Ops:
  0.6 3.1 %pack.1 = (f32[3,24,128]{2,1,0:T(8,128)}, f32[3,24,128]{2,1,0:T(8,128)}, f32[2,24,128]{2,1,0:T(8,128)}) custom-call(s32[128]{0:T(128)} %bitcast.28, f32[3,128,128]{2,1,0:T(8,128)} %bitcast.15, f32[3,128,128]{2,1,0:T(8,128)} %bitcast.17, f32[128,128]{1,0:T(8,128)} %bitcast.19, f32[128,128]{1,0:T(8,128)} %bitcast.21, f32[128,128]{1,0:T(8,128)} %bitcast.23, ...), custom_call_target="tpu_custom_call" | custom-call | tf_op jit(solution)/shard_map/pack/pallas_call | solution.py:305
  3.7 0.1 collective-permute-start
  3.8 0.0 copy-start.1
  3.8 3.8 %collective-permute-start.1 = (f32[3,24,128]{2,1,0:T(8,128)}, f32[3,24,128]{2,1,0:T(8,128)S(1)}, u32[]{:S(2)}, u32[]{:S(2)}) collective-permute-start(f32[3,24,128]{2,1,0:T(8,128)} %get-tuple-element.22), channel_id=1, source_target_pairs={{0,240},{16,0},{32,16},{48,32},{64,48},{80,64},{96,80},{112,96},{1... | collective-permute-start | bytes 110600 | tf_op jit(solution)/shard_map/ppermute | solution.py:23
  7.6 3.1 %stay.1 = (f32[10,144,128]{2,1,0:T(8,128)}, s32[1]{0:T(128)}) custom-call(s32[128]{0:T(128)} %bitcast.29, f32[3,128,128]{2,1,0:T(8,128)} %bitcast.16, f32[3,128,128]{2,1,0:T(8,128)} %bitcast.18, f32[128,128]{1,0:T(8,128)} %bitcast.20, f32[128,128]{1,0:T(8,128)} %bitcast.22, f32[128,128]{1,0:T(8,128)} %bitcast.24, f32[128,128]{1,0:T(8,128)} %bitcast.26), custom_call_target="tpu_custom_call" | custom-call | bytes 6000000 | tf_op jit(solution)/shard_map/stay/pallas_call | solution.py:317
  10.7 0.0 collective-permute-done.left.refs_0_
  10.7 0.0 collective-permute-done.1.right.refs_1_
  10.7 0.6 turn.1
  11.4 3.0 %collective-permute-start.2 = (f32[3,24,128]{2,1,0:T(8,128)S(1)}, f32[3,24,128]{2,1,0:T(8,128)S(1)}, u32[]{:S(2)}, u32[]{:S(2)}) collective-permute-start(f32[3,24,128]{2,1,0:T(8,128)S(1)} %get-tuple-element.24), channel_id=1, source_target_pairs={{0,1},{1,2},{2,3},{3,4},{4,5},{5,6},{6,7},{7,8},{8,9},{9,10},{10,1... | collective-permute-start | bytes 110600 | tf_op jit(solution)/shard_map/ppermute | solution.py:25
  14.4 1.5 %collective-permute-start.3 = (f32[3,24,128]{2,1,0:T(8,128)S(1)}, f32[3,24,128]{2,1,0:T(8,128)S(1)}, u32[]{:S(2)}, u32[]{:S(2)}) collective-permute-start(f32[3,24,128]{2,1,0:T(8,128)S(1)} %get-tuple-element.25), channel_id=1, source_target_pairs={{0,15},{1,0},{2,1},{3,2},{4,3},{5,4},{6,5},{7,6},{8,7},{9,8},{10,9... | collective-permute-start | bytes 110600 | tf_op jit(solution)/shard_map/ppermute | solution.py:25
  15.9 1.9 %collective-permute-done.2.refs_2_ = f32[3,24,128]{2,1,0:T(8,128)S(1)} collective-permute-done((f32[3,24,128]{2,1,0:T(8,128)S(1)}, f32[3,24,128]{2,1,0:T(8,128)S(1)}, u32[]{:S(2)}, u32[]{:S(2)}) %collective-permute-start.2) | collective-permute-done | bytes 36896 | tf_op jit(solution)/shard_map/ppermute | solution.py:25
  17.8 2.0 %collective-permute-done.3.refs_3_ = f32[3,24,128]{2,1,0:T(8,128)S(1)} collective-permute-done((f32[3,24,128]{2,1,0:T(8,128)S(1)}, f32[3,24,128]{2,1,0:T(8,128)S(1)}, u32[]{:S(2)}, u32[]{:S(2)}) %collective-permute-start.3) | collective-permute-done | bytes 36896 | tf_op jit(solution)/shard_map/ppermute | solution.py:25
  19.8 1.1 %copy-done = f32[10,144,128]{2,1,0:T(8,128)S(1)} copy-done((f32[10,144,128]{2,1,0:T(8,128)S(1)}, f32[10,144,128]{2,1,0:T(8,128)}, u32[]{:S(2)}) %copy-start) | copy-done | bytes 737304
  20.9 0.8 arrive.1
  21.8 2.5 %collective-permute-start.5 = (f32[6,144,128]{2,1,0:T(8,128)S(1)}, f32[6,144,128]{2,1,0:T(8,128)S(1)}, u32[]{:S(2)}, u32[]{:S(2)}) collective-permute-start(f32[6,144,128]{2,1,0:T(8,128)S(1)} %get-tuple-element.26.home.coords), channel_id=1, source_target_pairs={{0,15},{1,0},{2,1},{3,2},{4,3},{5,4},{6,5},{7,6},{8,7},{9,8},{10,9... | collective-permute-start | bytes 1327112 | tf_op jit(solution)/shard_map/ppermute | solution.py:25
  24.3 2.8 %collective-permute-start.7 = (f32[6,144,128]{2,1,0:T(8,128)S(1)}, f32[6,144,128]{2,1,0:T(8,128)S(1)}, u32[]{:S(2)}, u32[]{:S(2)}) collective-permute-start(f32[6,144,128]{2,1,0:T(8,128)S(1)} %get-tuple-element.26.home.coords), channel_id=1, source_target_pairs={{0,255},{1,240},{2,241},{3,242},{4,243},{5,244},{6,245},{7,246},{8... | collective-permute-start | bytes 1327112 | tf_op jit(solution)/shard_map/ppermute | solution.py:47
  27.1 0.1 collective-permute-start.4
  27.2 8.9 %collective-permute-done.5.north = f32[6,144,128]{2,1,0:T(8,128)S(1)} collective-permute-done((f32[6,144,128]{2,1,0:T(8,128)S(1)}, f32[6,144,128]{2,1,0:T(8,128)S(1)}, u32[]{:S(2)}, u32[]{:S(2)}) %collective-permute-start.5) | collective-permute-done | bytes 442400 | tf_op jit(solution)/shard_map/ppermute | solution.py:25
  36.1 1.3 %collective-permute-start.6 = (f32[6,144,128]{2,1,0:T(8,128)S(1)}, f32[6,144,128]{2,1,0:T(8,128)S(1)}, u32[]{:S(2)}, u32[]{:S(2)}) collective-permute-start(f32[6,144,128]{2,1,0:T(8,128)S(1)} %collective-permute-done.5.north), channel_id=1, source_target_pairs={{16,0},{48,32},{80,64},{112,96},{144,128},{176,160},{208,192},{240... | collective-permute-start | bytes 1327112 | tf_op jit(solution)/shard_map/ppermute | solution.py:40
  37.5 3.4 %collective-permute-done.7.far = f32[6,144,128]{2,1,0:T(8,128)S(1)} collective-permute-done((f32[6,144,128]{2,1,0:T(8,128)S(1)}, f32[6,144,128]{2,1,0:T(8,128)S(1)}, u32[]{:S(2)}, u32[]{:S(2)}) %collective-permute-start.7) | collective-permute-done | bytes 442400 | tf_op jit(solution)/shard_map/ppermute | solution.py:47
  40.8 0.0 collective-permute-done.4.east
  40.8 0.0 collective-permute-done.6.near
  40.8 45.9 %pair.1 = (f32[3,144,128]{2,1,0:T(8,128)S(1)}, f32[3,144,128]{2,1,0:T(8,128)S(1)}, f32[3,144,128]{2,1,0:T(8,128)S(1)}, f32[3,144,128]{2,1,0:T(8,128)S(1)}) custom-call(s32[4608]{0:T(1024)S(1)} %reshape.43.tiles, f32[6,144,128]{2,1,0:T(8,128)S(1)} %get-tuple-element.26.home.coords, f32[6,144,128]{2,1,0:T(8,128)S(1)} %collective-permute-done.4.east, ...), custom_call_target="tpu_custom_call" | custom-call | tf_op jit(solution)/shard_map/pair/pallas_call | solution.py:350
  86.7 2.2 %collective-permute-start.9 = (f32[3,144,128]{2,1,0:T(8,128)S(1)}, f32[3,144,128]{2,1,0:T(8,128)S(1)}, u32[]{:S(2)}, u32[]{:S(2)}) collective-permute-start(f32[3,144,128]{2,1,0:T(8,128)S(1)} %get-tuple-element.30), channel_id=1, source_target_pairs={{0,16},{32,48},{64,80},{96,112},{128,144},{160,176},{192,208},{224... | collective-permute-start | bytes 663560 | tf_op jit(solution)/shard_map/ppermute | solution.py:40
  88.9 1.3 %collective-permute-start.11 = (f32[3,144,128]{2,1,0:T(8,128)S(1)}, f32[3,144,128]{2,1,0:T(8,128)S(1)}, u32[]{:S(2)}, u32[]{:S(2)}) collective-permute-start(f32[3,144,128]{2,1,0:T(8,128)S(1)} %get-tuple-element.30), channel_id=1, source_target_pairs={{16,33},{17,34},{18,35},{19,36},{20,37},{21,38},{22,39},{23,40},{2... | collective-permute-start | bytes 663560 | tf_op jit(solution)/shard_map/ppermute | solution.py:47
  90.2 9.2 %collective-permute-start.8 = (f32[3,144,128]{2,1,0:T(8,128)S(1)}, f32[3,144,128]{2,1,0:T(8,128)S(1)}, u32[]{:S(2)}, u32[]{:S(2)}) collective-permute-start(f32[3,144,128]{2,1,0:T(8,128)S(1)} %get-tuple-element.28), channel_id=1, source_target_pairs={{0,16},{16,32},{32,48},{48,64},{64,80},{80,96},{96,112},{112,128},... | collective-permute-start | bytes 663560 | tf_op jit(solution)/shard_map/ppermute | solution.py:23
  99.4 0.0 collective-permute-done.9
  99.4 1.2 %collective-permute-start.10 = (f32[3,144,128]{2,1,0:T(8,128)S(1)}, f32[3,144,128]{2,1,0:T(8,128)S(1)}, u32[]{:S(2)}, u32[]{:S(2)}) collective-permute-start(f32[3,144,128]{2,1,0:T(8,128)S(1)} %add.3), channel_id=1, source_target_pairs={{0,1},{1,2},{2,3},{3,4},{4,5},{5,6},{6,7},{7,8},{8,9},{9,10},{10,1... | collective-permute-start | bytes 663560 | tf_op jit(solution)/shard_map/ppermute | solution.py:25
  100.6 8.3 %collective-permute-done.8.east = f32[3,144,128]{2,1,0:T(8,128)S(1)} collective-permute-done((f32[3,144,128]{2,1,0:T(8,128)S(1)}, f32[3,144,128]{2,1,0:T(8,128)S(1)}, u32[]{:S(2)}, u32[]{:S(2)}) %collective-permute-start.8) | collective-permute-done | bytes 221216 | tf_op jit(solution)/shard_map/ppermute | solution.py:23
  108.9 0.0 collective-permute-done.11.far
  108.9 0.3 collective-permute-done.10.north
  109.3 0.9 update.1
  (8 shorter events, 0.1 us)
Async XLA Ops:
  3.7 7.0 %collective-permute-start = (f32[3,24,128]{2,1,0:T(8,128)}, f32[3,24,128]{2,1,0:T(8,128)S(1)}, u32[]{:S(2)}, u32[]{:S(2)}) collective-permute-start(f32[3,24,128]{2,1,0:T(8,128)} %get-tuple-element.21), channel_id=1, source_target_pairs={{0,16},{16,32},{32,48},{48,64},{64,80},{80,96},{96,112},{112,128},... | collective-permute-start | bytes 110600 | tf_op jit(solution)/shard_map/ppermute | solution.py:23
  3.8 6.9 %copy-start.1 = (f32[2,24,128]{2,1,0:T(8,128)S(1)}, f32[2,24,128]{2,1,0:T(8,128)}, u32[]{:S(2)}) copy-start(f32[2,24,128]{2,1,0:T(8,128)} %get-tuple-element.23.own) | copy-start | bytes 73732
  3.8 6.9 %collective-permute-start.1 = (f32[3,24,128]{2,1,0:T(8,128)}, f32[3,24,128]{2,1,0:T(8,128)S(1)}, u32[]{:S(2)}, u32[]{:S(2)}) collective-permute-start(f32[3,24,128]{2,1,0:T(8,128)} %get-tuple-element.22), channel_id=1, source_target_pairs={{0,240},{16,0},{32,16},{48,32},{64,48},{80,64},{96,80},{112,96},{1... | collective-permute-start | bytes 110600 | tf_op jit(solution)/shard_map/ppermute | solution.py:23
  11.4 6.4 %collective-permute-start.2 = (f32[3,24,128]{2,1,0:T(8,128)S(1)}, f32[3,24,128]{2,1,0:T(8,128)S(1)}, u32[]{:S(2)}, u32[]{:S(2)}) collective-permute-start(f32[3,24,128]{2,1,0:T(8,128)S(1)} %get-tuple-element.24), channel_id=1, source_target_pairs={{0,1},{1,2},{2,3},{3,4},{4,5},{5,6},{6,7},{7,8},{8,9},{9,10},{10,1... | collective-permute-start | bytes 110600 | tf_op jit(solution)/shard_map/ppermute | solution.py:25
  14.4 5.5 %collective-permute-start.3 = (f32[3,24,128]{2,1,0:T(8,128)S(1)}, f32[3,24,128]{2,1,0:T(8,128)S(1)}, u32[]{:S(2)}, u32[]{:S(2)}) collective-permute-start(f32[3,24,128]{2,1,0:T(8,128)S(1)} %get-tuple-element.25), channel_id=1, source_target_pairs={{0,15},{1,0},{2,1},{3,2},{4,3},{5,4},{6,5},{7,6},{8,7},{9,8},{10,9... | collective-permute-start | bytes 110600 | tf_op jit(solution)/shard_map/ppermute | solution.py:25
  19.8 1.1 %copy-start = (f32[10,144,128]{2,1,0:T(8,128)S(1)}, f32[10,144,128]{2,1,0:T(8,128)}, u32[]{:S(2)}) copy-start(f32[10,144,128]{2,1,0:T(8,128)} %get-tuple-element.20.stay) | copy-start | bytes 2211844
  20.9 16.4 %copy-start.2 = (s32[1,1,2304,2]{2,3,1,0:T(2,128)S(1)}, s32[1,1,2304,2]{2,3,1,0:T(2,128)}, u32[]{:S(2)}) copy-start(s32[1,1,2304,2]{2,3,1,0:T(2,128)} %param.15) | copy-start | bytes 55300
  21.8 14.3 %collective-permute-start.5 = (f32[6,144,128]{2,1,0:T(8,128)S(1)}, f32[6,144,128]{2,1,0:T(8,128)S(1)}, u32[]{:S(2)}, u32[]{:S(2)}) collective-permute-start(f32[6,144,128]{2,1,0:T(8,128)S(1)} %get-tuple-element.26.home.coords), channel_id=1, source_target_pairs={{0,15},{1,0},{2,1},{3,2},{4,3},{5,4},{6,5},{7,6},{8,7},{9,8},{10,9... | collective-permute-start | bytes 1327112 | tf_op jit(solution)/shard_map/ppermute | solution.py:25
  24.3 16.5 %collective-permute-start.7 = (f32[6,144,128]{2,1,0:T(8,128)S(1)}, f32[6,144,128]{2,1,0:T(8,128)S(1)}, u32[]{:S(2)}, u32[]{:S(2)}) collective-permute-start(f32[6,144,128]{2,1,0:T(8,128)S(1)} %get-tuple-element.26.home.coords), channel_id=1, source_target_pairs={{0,255},{1,240},{2,241},{3,242},{4,243},{5,244},{6,245},{7,246},{8... | collective-permute-start | bytes 1327112 | tf_op jit(solution)/shard_map/ppermute | solution.py:47
  27.1 13.8 %collective-permute-start.4 = (f32[6,144,128]{2,1,0:T(8,128)S(1)}, f32[6,144,128]{2,1,0:T(8,128)S(1)}, u32[]{:S(2)}, u32[]{:S(2)}) collective-permute-start(f32[6,144,128]{2,1,0:T(8,128)S(1)} %get-tuple-element.26.home.coords), channel_id=1, source_target_pairs={{0,240},{16,0},{32,16},{48,32},{64,48},{80,64},{96,80},{112,96},{1... | collective-permute-start | bytes 1327112 | tf_op jit(solution)/shard_map/ppermute | solution.py:23
  36.1 4.7 %collective-permute-start.6 = (f32[6,144,128]{2,1,0:T(8,128)S(1)}, f32[6,144,128]{2,1,0:T(8,128)S(1)}, u32[]{:S(2)}, u32[]{:S(2)}) collective-permute-start(f32[6,144,128]{2,1,0:T(8,128)S(1)} %collective-permute-done.5.north), channel_id=1, source_target_pairs={{16,0},{48,32},{80,64},{112,96},{144,128},{176,160},{208,192},{240... | collective-permute-start | bytes 1327112 | tf_op jit(solution)/shard_map/ppermute | solution.py:40
  86.7 12.7 %collective-permute-start.9 = (f32[3,144,128]{2,1,0:T(8,128)S(1)}, f32[3,144,128]{2,1,0:T(8,128)S(1)}, u32[]{:S(2)}, u32[]{:S(2)}) collective-permute-start(f32[3,144,128]{2,1,0:T(8,128)S(1)} %get-tuple-element.30), channel_id=1, source_target_pairs={{0,16},{32,48},{64,80},{96,112},{128,144},{160,176},{192,208},{224... | collective-permute-start | bytes 663560 | tf_op jit(solution)/shard_map/ppermute | solution.py:40
  88.9 20.0 %collective-permute-start.11 = (f32[3,144,128]{2,1,0:T(8,128)S(1)}, f32[3,144,128]{2,1,0:T(8,128)S(1)}, u32[]{:S(2)}, u32[]{:S(2)}) collective-permute-start(f32[3,144,128]{2,1,0:T(8,128)S(1)} %get-tuple-element.30), channel_id=1, source_target_pairs={{16,33},{17,34},{18,35},{19,36},{20,37},{21,38},{22,39},{23,40},{2... | collective-permute-start | bytes 663560 | tf_op jit(solution)/shard_map/ppermute | solution.py:47
  90.2 18.7 %collective-permute-start.8 = (f32[3,144,128]{2,1,0:T(8,128)S(1)}, f32[3,144,128]{2,1,0:T(8,128)S(1)}, u32[]{:S(2)}, u32[]{:S(2)}) collective-permute-start(f32[3,144,128]{2,1,0:T(8,128)S(1)} %get-tuple-element.28), channel_id=1, source_target_pairs={{0,16},{16,32},{32,48},{48,64},{64,80},{80,96},{96,112},{112,128},... | collective-permute-start | bytes 663560 | tf_op jit(solution)/shard_map/ppermute | solution.py:23
  99.4 9.8 %collective-permute-start.10 = (f32[3,144,128]{2,1,0:T(8,128)S(1)}, f32[3,144,128]{2,1,0:T(8,128)S(1)}, u32[]{:S(2)}, u32[]{:S(2)}) collective-permute-start(f32[3,144,128]{2,1,0:T(8,128)S(1)} %add.3), channel_id=1, source_target_pairs={{0,1},{1,2},{2,3},{3,4},{4,5},{5,6},{6,7},{7,8},{8,9},{9,10},{10,1... | collective-permute-start | bytes 663560 | tf_op jit(solution)/shard_map/ppermute | solution.py:25

commit v5 on v4

--- a/solution.py
+++ b/solution.py
@@ -159,9 +159,9 @@
         rest[k] = held[f, 0:CAPACITY, :]
 
 
-def update_kernel(home, east, north, far, coords, rest, new_x, new_v, total):
+def update_kernel(home, on_i, east, north, coords, rest, new_x, new_v, total):
     for d in range(3):
-        force = home[d] + east[d] + north[d] + far[d]
+        force = home[d] + on_i[d] + east[d] + north[d]
         fresh = rest[d] + TSTEP * rest[3] * force
         total[d] = force
         new_v[d] = fresh
@@ -172,7 +172,7 @@
     return (b // 8) * 256 + (b % 8) * 16
 
 
-def pair_kernel(tiles, home, east, north, near, far, fh, fe, fn, fc, zone, ac0, ac1, ac2, ibuf0, ibuf1, vbuf0, vbuf1, wbuf, *, T=2, mxu=True):
+def pair_kernel(tiles, home, east, north, near, far, fh, fe, fn, fc, ti, zone, ac0, ac1, ac2, ibuf0, ibuf1, ring, gone, wbuf, *, T=2, mxu=True):
     acc=(ac0,ac1,ac2)
     sub = lax.broadcasted_iota(jnp.int32,(8,128),0)
     lane = lax.broadcasted_iota(jnp.int32,(8,128),1)
@@ -210,28 +210,10 @@
         for f in range(6):
             for c in range(16): ibuf[f,c]=out[8*c:8*c+8,128*f:128*f+128]
 
-    def settle(b,vbuf):
-        tots=[]
-        for c in range(16):
-            tot=None
-            for t in range(T):
-                j8=pl.multiple_of(tiles[listed(b) + (128 * t + c)]*8,8)
-                v=[vbuf[d,t,c] for d in range(3)]
-                for d in range(3):
-                    acc[d][pl.ds(j8,8),:]=acc[d][pl.ds(j8,8),:]+v[d]
-                tot=v if tot is None else [p+q for p,q in zip(tot,v)]
-            tots.append(tot)
-        cc=[]
-        for c in range(16):
-            r=[jnp.sum(tots[c][d],axis=1,keepdims=True) for d in range(3)]
-            cc.append(jnp.where(lane==0,r[0],jnp.where(lane==1,r[1],r[2])))
-        m=jnp.concatenate(cc,axis=0)[:, :8].T
-        for d in range(3):
-            fh[d,pl.ds(b,1),:]=m[d:d+1]
-
-    def block(b,ibuf,vbuf):
+    def block(b,ibuf,slot,n):
         for c in range(16):
             xi,yi,zi,qi,ai,bi=[ibuf[f,c] for f in range(6)]
+            tot=None
             for t in range(T):
                 j=tiles[listed(b) + (128 * t + c)]
                 dx=xi-row(0,j); dy=yi-row(1,j); dz=zi-row(2,j)
@@ -245,36 +227,53 @@
                 kc=(1.0-lax.erf(s*rs))*rs+ew*HALFC
                 g=(qi*row(3,j))*kc+cube*((ai*row(4,j))*cube-bi*row(5,j))
                 g=g*(inv*(w*w))
-                vbuf[0,t,c]=g*dx
-                vbuf[1,t,c]=g*dy
-                vbuf[2,t,c]=g*dz
-
-    spread(0,ibuf0)
-    for d in range(3):
-        for t in range(T):
-            for c in range(16): vbuf1[d,t,c]=zero
-    ib=(ibuf0,ibuf0); vb=(vbuf0,vbuf1)
-    def some(k,_):
-        b=4*k
-        for n in range(4):
-            settle(jnp.maximum(b+n-1,0),vb[(n+1)%2])
-            pass
-            block(b+n,ib[n%2],vb[n%2])
-            spread(jnp.minimum(b+n+1,CAPACITY-1),ib[(n+1)%2])
+                v=(g*dx,g*dy,g*dz)
+                j8=pl.ds(pl.multiple_of(j*8,8),8)
+                old=[acc[d][j8,:] for d in range(3)]
+                for d in range(3):
+                    acc[d][j8,:]=old[d]+v[d]
+                tot=v if tot is None else tuple(p+q for p,q in zip(tot,v))
+            for d in range(3): ring[slot,3*n+d,c]=tot[d]
+
+    RING=3
+    spread(0,ibuf0); spread(1,ibuf1)
+    def out_copy(k):
+        slot=lax.rem(k,RING)
+        return pltpu.make_async_copy(ring.at[slot],ti.at[pl.ds(6*k,6)],gone.at[slot])
+    def two(k,_):
+        b=2*k
+        slot=lax.rem(k,RING)
+        @pl.when(k>=RING)
+        def _(): out_copy(k-RING).wait()
+        block(b,ibuf0,slot,0)
+        block(b+1,ibuf1,slot,1)
+        spread(jnp.minimum(b+2,CAPACITY-1),ibuf0)
+        spread(jnp.minimum(b+3,CAPACITY-1),ibuf1)
+        out_copy(k).start()
         return 0
-    lax.fori_loop(0,CAPACITY//4,some,0)
-    settle(CAPACITY-1,vb[1])
-    for d in range(3):
-        for z,ref in enumerate((fh,fe,fn,fc)):
-            def red(k,_):
-                for u in range(3):
-                    k8=pl.multiple_of(k*24+8*u,8)
-                    r=[acc[d][pl.ds((z*CAPACITY+k8)*8+q,8,stride=8),:] for q in range(8)]
-                    r=((r[0]+r[1])+(r[2]+r[3]))+((r[4]+r[5])+(r[6]+r[7]))
-                    if z==0: ref[d,pl.ds(k8,8),:]=ref[d,pl.ds(k8,8),:]-r
-                    else: ref[d,pl.ds(k8,8),:]=-r
-                return 0
-            lax.fori_loop(0,CAPACITY//24,red,0)
+    lax.fori_loop(0,CAPACITY//2,two,0)
+    def fold(k,_):
+        for d in range(3):
+            for z,ref in enumerate((fh,fe,fn,fc)):
+                k8=pl.multiple_of(k*8,8)
+                r=[acc[d][pl.ds((z*CAPACITY+k8)*8+q,8,stride=8),:] for q in range(8)]
+                r=((r[0]+r[1])+(r[2]+r[3]))+((r[4]+r[5])+(r[6]+r[7]))
+                ref[d,pl.ds(k8,8),:]=-r
+        return 0
+    lax.fori_loop(0,CAPACITY//8,fold,0)
+    for k in range(CAPACITY//2-RING,CAPACITY//2):
+        out_copy(k).wait()
+
+def ireduce_kernel(ti,fi):
+    lane = lax.broadcasted_iota(jnp.int32,(8,128),1)
+    for b in range(8):
+        cc=[]
+        for c in range(16):
+            r=[jnp.sum(ti[3*b+d,c],axis=1,keepdims=True) for d in range(3)]
+            cc.append(jnp.where(lane==0,r[0],jnp.where(lane==1,r[1],r[2])))
+        m=jnp.concatenate(cc,axis=0)[:, :8].T
+        for d in range(3): fi[d,b:b+1,:]=m[d:d+1]
+
 
 VM = pl.BlockSpec(memory_space=pltpu.VMEM)
 SM = pl.BlockSpec(memory_space=pltpu.SMEM)
@@ -347,19 +346,28 @@
     north = passed_along(coords, 0, -1)
     far = sent(coords, -1, -1, 0)
     near = sent(north, -1, 0, 1)
-    on_home, on_east, on_north, on_corner = pl.pallas_call(
+    on_home, on_east, on_north, on_corner, sums = pl.pallas_call(
         pair_kernel,
-        out_shape=(planes(3),) * 4,
+        out_shape=(planes(3),) * 4 + (jax.ShapeDtypeStruct((3 * CAPACITY, 16, 8, BLOCK), jnp.float32),),
         in_specs=[SM] + [VM] * 5,
-        out_specs=(VM,) * 4,
-        scratch_shapes=[pltpu.VMEM((6,4 * CAPACITY,128),jnp.float32)]+[pltpu.VMEM((4 * CAPACITY*8,128),jnp.float32)]*3+[pltpu.VMEM((6,16,8,128),jnp.float32)]*2+[pltpu.VMEM((3,2,16,8,128),jnp.float32)]*2+[pltpu.VMEM((17,8,128),jnp.float32)],
+        out_specs=(VM,) * 4 + (HBM,),
+        scratch_shapes=[pltpu.VMEM((6,4 * CAPACITY,128),jnp.float32)]+[pltpu.VMEM((4 * CAPACITY*8,128),jnp.float32)]*3+[pltpu.VMEM((6,16,8,128),jnp.float32)]*2+[pltpu.VMEM((3,6,16,8,128),jnp.float32),pltpu.SemaphoreType.DMA((3,))]+[pltpu.VMEM((17,8,128),jnp.float32)],
         compiler_params=PARAMS,
         name="pair",
     )(tiles.reshape(18, 128, 2).transpose(0, 2, 1).reshape(-1), coords, east, north, near, far)
-    from_near = sent(on_corner, 1, 0, 0)
-    from_far = sent(on_corner, 1, 1, 1)
+    from_corner = passed_along(on_corner, 1, 0)
     from_east = passed_along(on_east, 1, 0)
-    from_north = passed_along(on_north + from_near, 0, 1)
+    from_north = passed_along(on_north + from_corner, 0, 1)
+    on_i = pl.pallas_call(
+        ireduce_kernel,
+        grid=(CAPACITY // 8,),
+        out_shape=planes(3),
+        in_specs=[pl.BlockSpec((24, 16, 8, BLOCK), lambda i: (i, 0, 0, 0))],
+        out_specs=pl.BlockSpec((3, 8, BLOCK), lambda i: (0, i, 0)),
+        compiler_params=PARAMS,
+        cost_estimate=pl.CostEstimate(flops=20_000_000, bytes_accessed=28_000_000, transcendentals=0),
+        name="ireduce",
+    )(sums)
     out = pl.pallas_call(
         update_kernel,
         out_shape=(planes(3),) * 3,
@@ -367,7 +375,7 @@
         out_specs=(VM,) * 3,
         compiler_params=PARAMS,
         name="update",
-    )(on_home, from_east, from_north, from_far, coords, rest)
+    )(on_home, on_i, from_east, from_north, coords, rest)
     return tuple(value.reshape(3, 1, 1, CAPACITY * BLOCK) for value in out)
 
 

time: 112 us -> 124 us (1.11)
  Pallas kernels: 54.4 us -> 69.8 us
  waiting for transfers between devices: 24.9 us -> 21.5 us
  local copies, waits for them, and re-layouts: 1.17 us -> 2.62 us
    pallas_call x1 -> x2, Pallas kernels: 45.9 us -> 61.2 us  [the longest x1 41 us: body(): pl.pallas_call(pair_kernel, out_shape=(planes(3),) * 4 + (jax.ShapeDtypeS...]
    ppermute x4, starting transfers between devices: 8.23 us -> 15.5 us  [passed_along(): lax.ppermute(value, 'gy', [(s, (s + step_y) % ny) for s in range(ny)])]
    ppermute x4 -> x5, starting transfers between devices: 13.2 us -> 9.28 us  [passed_along(): lax.ppermute(value, 'gx', [(s, (s + step_x) % nx) for s in range(nx)])]
    ppermute x4 -> x5, waiting for transfers between devices: 8.31 us -> 5.4 us  [passed_along(): lax.ppermute(value, 'gx', [(s, (s + step_x) % nx) for s in range(nx)])]
    ppermute x2 -> x1, starting transfers between devices: 3.48 us -> 1.28 us  [sent(): lax.ppermute(value, 'gx', [(s, (s + step_x) % nx) for s in range(nx) if s...]
    ppermute x2 -> x1, starting transfers between devices: 4.07 us -> 2.5 us  [sent(): return lax.ppermute(value, ('gx', 'gy'), pairs)]
    ppermute x2 -> x1, waiting for transfers between devices: 3.38 us -> 2.67 us  [sent(): return lax.ppermute(value, ('gx', 'gy'), pairs)]
  transfers between devices with their start and end apart: 12 -> 11, of which waited for: 6 -> 5; matrix products, arithmetic and copies ran while one was open for 0% -> 1% of each run, Pallas kernels for 3% -> 19%
where the time goes in v5:
time: 124 us; the launch traced here: 123 us
  Pallas kernels  69.8 us (56%)
  starting transfers between devices  28.5 us (23%)
  waiting for transfers between devices  21.5 us (17%)
  local copies, waits for them, and re-layouts  2.62 us (2%)
    pallas_call x1, Pallas kernels, body(): pl.pallas_call(pair_kernel, out_shape=(planes(3),) * 4 + (jax.ShapeDtypeS...  41 us
    pallas_call x1, Pallas kernels, body(): pl.pallas_call(ireduce_kernel, grid=(CAPACITY // 8,), out_shape=planes(3)...  20.2 us
    ppermute x4, starting transfers between devices, passed_along(): lax.ppermute(value, 'gy', [(s, (s + step_y) % ny) for s in range(ny)])  15.5 us
    ppermute x4, waiting for transfers between devices, passed_along(): lax.ppermute(value, 'gy', [(s, (s + step_y) % ny) for s in range(ny)])  13.4 us
    ppermute x5, starting transfers between devices, passed_along(): lax.ppermute(value, 'gx', [(s, (s + step_x) % nx) for s in range(nx)])  9.28 us
    ppermute x5, waiting for transfers between devices, passed_along(): lax.ppermute(value, 'gx', [(s, (s + step_x) % nx) for s in range(nx)])  5.4 us
    pallas_call x1, Pallas kernels, body(): pl.pallas_call(stay_kernel, out_shape=(planes(10), jax.ShapeDtypeStruct((...  3.08 us
    pallas_call x1, Pallas kernels, body(): pl.pallas_call(pack_kernel, out_shape=(planes(3, 24), planes(3, 24), plan...  2.96 us
  transfers between devices with their start and end apart: 11, of which 5 were waited for; matrix products, arithmetic and copies ran while one was open for 1% of the time, Pallas kernels for 19%

profile of v5, /device:TPU:96, one launch (start us, length us, event | category | flops | bytes accessed | tf_op | source)
XLA Modules:
  0.0 123.2 jit_solution(4645671329730851667)
XLA Ops:
  0.6 3.0 %pack.1 = (f32[3,24,128]{2,1,0:T(8,128)}, f32[3,24,128]{2,1,0:T(8,128)}, f32[2,24,128]{2,1,0:T(8,128)}) custom-call(s32[128]{0:T(128)} %bitcast.28, f32[3,128,128]{2,1,0:T(8,128)} %bitcast.15, f32[3,128,128]{2,1,0:T(8,128)} %bitcast.17, f32[128,128]{1,0:T(8,128)} %bitcast.19, f32[128,128]{1,0:T(8,128)} %bitcast.21, f32[128,128]{1,0:T(8,128)} %bitcast.23, ...), custom_call_target="tpu_custom_call" | custom-call | tf_op jit(solution)/shard_map/pack/pallas_call | solution.py:304
  3.6 0.1 collective-permute-start
  3.7 3.8 %collective-permute-start.1 = (f32[3,24,128]{2,1,0:T(8,128)}, f32[3,24,128]{2,1,0:T(8,128)S(1)}, u32[]{:S(2)}, u32[]{:S(2)}) collective-permute-start(f32[3,24,128]{2,1,0:T(8,128)} %get-tuple-element.23), channel_id=1, source_target_pairs={{0,240},{16,0},{32,16},{48,32},{64,48},{80,64},{96,80},{112,96},{1... | collective-permute-start | bytes 110600 | tf_op jit(solution)/shard_map/ppermute | solution.py:23
  7.5 3.1 %stay.1 = (f32[10,144,128]{2,1,0:T(8,128)}, s32[1]{0:T(128)}) custom-call(s32[128]{0:T(128)} %bitcast.29, f32[3,128,128]{2,1,0:T(8,128)} %bitcast.16, f32[3,128,128]{2,1,0:T(8,128)} %bitcast.18, f32[128,128]{1,0:T(8,128)} %bitcast.20, f32[128,128]{1,0:T(8,128)} %bitcast.22, f32[128,128]{1,0:T(8,128)} %bitcast.24, f32[128,128]{1,0:T(8,128)} %bitcast.26), custom_call_target="tpu_custom_call" | custom-call | bytes 6000000 | tf_op jit(solution)/shard_map/stay/pallas_call | solution.py:316
  10.6 0.0 collective-permute-done.left.refs_0_
  10.6 0.0 copy-start.1
  10.7 0.7 copy-done.1
  11.4 0.7 turn.1
  12.1 3.3 %collective-permute-start.2 = (f32[3,24,128]{2,1,0:T(8,128)S(1)}, f32[3,24,128]{2,1,0:T(8,128)S(1)}, u32[]{:S(2)}, u32[]{:S(2)}) collective-permute-start(f32[3,24,128]{2,1,0:T(8,128)S(1)} %get-tuple-element.25), channel_id=1, source_target_pairs={{0,1},{1,2},{2,3},{3,4},{4,5},{5,6},{6,7},{7,8},{8,9},{9,10},{10,1... | collective-permute-start | bytes 110600 | tf_op jit(solution)/shard_map/ppermute | solution.py:25
  15.3 1.3 %collective-permute-start.3 = (f32[3,24,128]{2,1,0:T(8,128)S(1)}, f32[3,24,128]{2,1,0:T(8,128)S(1)}, u32[]{:S(2)}, u32[]{:S(2)}) collective-permute-start(f32[3,24,128]{2,1,0:T(8,128)S(1)} %get-tuple-element.26), channel_id=1, source_target_pairs={{0,15},{1,0},{2,1},{3,2},{4,3},{5,4},{6,5},{7,6},{8,7},{9,8},{10,9... | collective-permute-start | bytes 110600 | tf_op jit(solution)/shard_map/ppermute | solution.py:25
  16.6 1.9 %collective-permute-done.2.refs_2_ = f32[3,24,128]{2,1,0:T(8,128)S(1)} collective-permute-done((f32[3,24,128]{2,1,0:T(8,128)S(1)}, f32[3,24,128]{2,1,0:T(8,128)S(1)}, u32[]{:S(2)}, u32[]{:S(2)}) %collective-permute-start.2) | collective-permute-done | bytes 36896 | tf_op jit(solution)/shard_map/ppermute | solution.py:25
  18.5 2.3 %collective-permute-done.3.refs_3_ = f32[3,24,128]{2,1,0:T(8,128)S(1)} collective-permute-done((f32[3,24,128]{2,1,0:T(8,128)S(1)}, f32[3,24,128]{2,1,0:T(8,128)S(1)}, u32[]{:S(2)}, u32[]{:S(2)}) %collective-permute-start.3) | collective-permute-done | bytes 36896 | tf_op jit(solution)/shard_map/ppermute | solution.py:25
  20.8 1.1 copy-done
  21.9 0.9 arrive.1
  22.8 2.2 %collective-permute-start.5 = (f32[6,144,128]{2,1,0:T(8,128)S(1)}, f32[6,144,128]{2,1,0:T(8,128)S(1)}, u32[]{:S(2)}, u32[]{:S(2)}) collective-permute-start(f32[6,144,128]{2,1,0:T(8,128)S(1)} %get-tuple-element.27.home.coords), channel_id=1, source_target_pairs={{0,15},{1,0},{2,1},{3,2},{4,3},{5,4},{6,5},{7,6},{8,7},{9,8},{10,9... | collective-permute-start | bytes 1327112 | tf_op jit(solution)/shard_map/ppermute | solution.py:25
  25.0 2.5 %collective-permute-start.7 = (f32[6,144,128]{2,1,0:T(8,128)S(1)}, f32[6,144,128]{2,1,0:T(8,128)S(1)}, u32[]{:S(2)}, u32[]{:S(2)}) collective-permute-start(f32[6,144,128]{2,1,0:T(8,128)S(1)} %get-tuple-element.27.home.coords), channel_id=1, source_target_pairs={{0,255},{1,240},{2,241},{3,242},{4,243},{5,244},{6,245},{7,246},{8... | collective-permute-start | bytes 1327112 | tf_op jit(solution)/shard_map/ppermute | solution.py:47
  27.5 0.1 collective-permute-start.4
  27.6 9.2 %collective-permute-done.5.north = f32[6,144,128]{2,1,0:T(8,128)S(1)} collective-permute-done((f32[6,144,128]{2,1,0:T(8,128)S(1)}, f32[6,144,128]{2,1,0:T(8,128)S(1)}, u32[]{:S(2)}, u32[]{:S(2)}) %collective-permute-start.5) | collective-permute-done | bytes 442400 | tf_op jit(solution)/shard_map/ppermute | solution.py:25
  36.8 1.3 %collective-permute-start.6 = (f32[6,144,128]{2,1,0:T(8,128)S(1)}, f32[6,144,128]{2,1,0:T(8,128)S(1)}, u32[]{:S(2)}, u32[]{:S(2)}) collective-permute-start(f32[6,144,128]{2,1,0:T(8,128)S(1)} %collective-permute-done.5.north), channel_id=1, source_target_pairs={{16,0},{48,32},{80,64},{112,96},{144,128},{176,160},{208,192},{240... | collective-permute-start | bytes 1327112 | tf_op jit(solution)/shard_map/ppermute | solution.py:40
  38.1 0.7 reshape.42
  38.9 2.7 %collective-permute-done.7.far = f32[6,144,128]{2,1,0:T(8,128)S(1)} collective-permute-done((f32[6,144,128]{2,1,0:T(8,128)S(1)}, f32[6,144,128]{2,1,0:T(8,128)S(1)}, u32[]{:S(2)}, u32[]{:S(2)}) %collective-permute-start.7) | collective-permute-done | bytes 442400 | tf_op jit(solution)/shard_map/ppermute | solution.py:47
  41.6 0.0 collective-permute-done.4.east
  41.6 0.0 collective-permute-done.6.near
  41.6 41.0 %pair.1 = (f32[3,144,128]{2,1,0:T(8,128)S(1)}, f32[3,144,128]{2,1,0:T(8,128)S(1)}, f32[3,144,128]{2,1,0:T(8,128)S(1)}, f32[3,144,128]{2,1,0:T(8,128)S(1)}, f32[432,16,8,128]{3,2,1,0:T(8,128)}) custom-call(s32[4608]{0:T(1024)S(1)} %reshape.43.tiles, f32[6,144,128]{2,1,0:T(8,128)S(1)} %get-tuple-element.27.home.coords, ...), custom_call_target="tpu_custom_call" | custom-call | tf_op jit(solution)/shard_map/pair/pallas_call | solution.py:349
  82.6 0.3 collective-permute-start.9
  82.9 4.9 %collective-permute-start.8 = (f32[3,144,128]{2,1,0:T(8,128)S(1)}, f32[3,144,128]{2,1,0:T(8,128)S(1)}, u32[]{:S(2)}, u32[]{:S(2)}) collective-permute-start(f32[3,144,128]{2,1,0:T(8,128)S(1)} %get-tuple-element.30), channel_id=1, source_target_pairs={{0,16},{16,32},{32,48},{48,64},{64,80},{80,96},{96,112},{112,128},... | collective-permute-start | bytes 663560 | tf_op jit(solution)/shard_map/ppermute | solution.py:23
  87.9 5.4 %collective-permute-done.9 = f32[3,144,128]{2,1,0:T(8,128)S(1)} collective-permute-done((f32[3,144,128]{2,1,0:T(8,128)S(1)}, f32[3,144,128]{2,1,0:T(8,128)S(1)}, u32[]{:S(2)}, u32[]{:S(2)}) %collective-permute-start.9) | collective-permute-done | bytes 221216 | tf_op jit(solution)/shard_map/ppermute | solution.py:23
  93.3 8.7 %collective-permute-start.10 = (f32[3,144,128]{2,1,0:T(8,128)S(1)}, f32[3,144,128]{2,1,0:T(8,128)S(1)}, u32[]{:S(2)}, u32[]{:S(2)}) collective-permute-start(f32[3,144,128]{2,1,0:T(8,128)S(1)} %add.3), channel_id=1, source_target_pairs={{0,1},{1,2},{2,3},{3,4},{4,5},{5,6},{6,7},{7,8},{8,9},{9,10},{10,1... | collective-permute-start | bytes 663560 | tf_op jit(solution)/shard_map/ppermute | solution.py:25
  102.0 20.2 %ireduce.1.on_i = f32[3,144,128]{2,1,0:T(8,128)S(1)} custom-call(f32[432,16,8,128]{3,2,1,0:T(8,128)} %get-tuple-element.29.ti), custom_call_target="tpu_custom_call" | custom-call | flops 20000000 | bytes 28000000 | tf_op jit(solution)/shard_map/ireduce/pallas_call | solution.py:361
  122.2 0.0 collective-permute-done.8.east
  122.2 0.0 collective-permute-done.10.north
  122.3 0.9 update.1
  (5 shorter events, 0.1 us)
Async XLA Ops:
  3.6 7.0 %collective-permute-start = (f32[3,24,128]{2,1,0:T(8,128)}, f32[3,24,128]{2,1,0:T(8,128)S(1)}, u32[]{:S(2)}, u32[]{:S(2)}) collective-permute-start(f32[3,24,128]{2,1,0:T(8,128)} %get-tuple-element.22), channel_id=1, source_target_pairs={{0,16},{16,32},{32,48},{48,64},{64,80},{80,96},{96,112},{112,128},... | collective-permute-start | bytes 110600 | tf_op jit(solution)/shard_map/ppermute | solution.py:23
  3.7 6.9 %collective-permute-start.1 = (f32[3,24,128]{2,1,0:T(8,128)}, f32[3,24,128]{2,1,0:T(8,128)S(1)}, u32[]{:S(2)}, u32[]{:S(2)}) collective-permute-start(f32[3,24,128]{2,1,0:T(8,128)} %get-tuple-element.23), channel_id=1, source_target_pairs={{0,240},{16,0},{32,16},{48,32},{64,48},{80,64},{96,80},{112,96},{1... | collective-permute-start | bytes 110600 | tf_op jit(solution)/shard_map/ppermute | solution.py:23
  10.6 0.7 copy-start.1
  12.1 6.4 %collective-permute-start.2 = (f32[3,24,128]{2,1,0:T(8,128)S(1)}, f32[3,24,128]{2,1,0:T(8,128)S(1)}, u32[]{:S(2)}, u32[]{:S(2)}) collective-permute-start(f32[3,24,128]{2,1,0:T(8,128)S(1)} %get-tuple-element.25), channel_id=1, source_target_pairs={{0,1},{1,2},{2,3},{3,4},{4,5},{5,6},{6,7},{7,8},{8,9},{9,10},{10,1... | collective-permute-start | bytes 110600 | tf_op jit(solution)/shard_map/ppermute | solution.py:25
  15.3 5.5 %collective-permute-start.3 = (f32[3,24,128]{2,1,0:T(8,128)S(1)}, f32[3,24,128]{2,1,0:T(8,128)S(1)}, u32[]{:S(2)}, u32[]{:S(2)}) collective-permute-start(f32[3,24,128]{2,1,0:T(8,128)S(1)} %get-tuple-element.26), channel_id=1, source_target_pairs={{0,15},{1,0},{2,1},{3,2},{4,3},{5,4},{6,5},{7,6},{8,7},{9,8},{10,9... | collective-permute-start | bytes 110600 | tf_op jit(solution)/shard_map/ppermute | solution.py:25
  20.8 1.1 copy-start
  22.8 14.0 %collective-permute-start.5 = (f32[6,144,128]{2,1,0:T(8,128)S(1)}, f32[6,144,128]{2,1,0:T(8,128)S(1)}, u32[]{:S(2)}, u32[]{:S(2)}) collective-permute-start(f32[6,144,128]{2,1,0:T(8,128)S(1)} %get-tuple-element.27.home.coords), channel_id=1, source_target_pairs={{0,15},{1,0},{2,1},{3,2},{4,3},{5,4},{6,5},{7,6},{8,7},{9,8},{10,9... | collective-permute-start | bytes 1327112 | tf_op jit(solution)/shard_map/ppermute | solution.py:25
  25.0 16.5 %collective-permute-start.7 = (f32[6,144,128]{2,1,0:T(8,128)S(1)}, f32[6,144,128]{2,1,0:T(8,128)S(1)}, u32[]{:S(2)}, u32[]{:S(2)}) collective-permute-start(f32[6,144,128]{2,1,0:T(8,128)S(1)} %get-tuple-element.27.home.coords), channel_id=1, source_target_pairs={{0,255},{1,240},{2,241},{3,242},{4,243},{5,244},{6,245},{7,246},{8... | collective-permute-start | bytes 1327112 | tf_op jit(solution)/shard_map/ppermute | solution.py:47
  27.5 14.0 %collective-permute-start.4 = (f32[6,144,128]{2,1,0:T(8,128)S(1)}, f32[6,144,128]{2,1,0:T(8,128)S(1)}, u32[]{:S(2)}, u32[]{:S(2)}) collective-permute-start(f32[6,144,128]{2,1,0:T(8,128)S(1)} %get-tuple-element.27.home.coords), channel_id=1, source_target_pairs={{0,240},{16,0},{32,16},{48,32},{64,48},{80,64},{96,80},{112,96},{1... | collective-permute-start | bytes 1327112 | tf_op jit(solution)/shard_map/ppermute | solution.py:23
  36.8 4.7 %collective-permute-start.6 = (f32[6,144,128]{2,1,0:T(8,128)S(1)}, f32[6,144,128]{2,1,0:T(8,128)S(1)}, u32[]{:S(2)}, u32[]{:S(2)}) collective-permute-start(f32[6,144,128]{2,1,0:T(8,128)S(1)} %collective-permute-done.5.north), channel_id=1, source_target_pairs={{16,0},{48,32},{80,64},{112,96},{144,128},{176,160},{208,192},{240... | collective-permute-start | bytes 1327112 | tf_op jit(solution)/shard_map/ppermute | solution.py:40
  82.6 10.7 %collective-permute-start.9 = (f32[3,144,128]{2,1,0:T(8,128)S(1)}, f32[3,144,128]{2,1,0:T(8,128)S(1)}, u32[]{:S(2)}, u32[]{:S(2)}) collective-permute-start(f32[3,144,128]{2,1,0:T(8,128)S(1)} %get-tuple-element.32), channel_id=1, source_target_pairs={{0,16},{16,32},{32,48},{48,64},{64,80},{80,96},{96,112},{112,128},... | collective-permute-start | bytes 663560 | tf_op jit(solution)/shard_map/ppermute | solution.py:23
  82.9 39.3 %collective-permute-start.8 = (f32[3,144,128]{2,1,0:T(8,128)S(1)}, f32[3,144,128]{2,1,0:T(8,128)S(1)}, u32[]{:S(2)}, u32[]{:S(2)}) collective-permute-start(f32[3,144,128]{2,1,0:T(8,128)S(1)} %get-tuple-element.30), channel_id=1, source_target_pairs={{0,16},{16,32},{32,48},{48,64},{64,80},{80,96},{96,112},{112,128},... | collective-permute-start | bytes 663560 | tf_op jit(solution)/shard_map/ppermute | solution.py:23
  93.3 29.0 %collective-permute-start.10 = (f32[3,144,128]{2,1,0:T(8,128)S(1)}, f32[3,144,128]{2,1,0:T(8,128)S(1)}, u32[]{:S(2)}, u32[]{:S(2)}) collective-permute-start(f32[3,144,128]{2,1,0:T(8,128)S(1)} %add.3), channel_id=1, source_target_pairs={{0,1},{1,2},{2,3},{3,4},{4,5},{5,6},{6,7},{7,8},{8,9},{9,10},{10,1... | collective-permute-start | bytes 663560 | tf_op jit(solution)/shard_map/ppermute | solution.py:25

commit v6 on v5

--- a/solution.py
+++ b/solution.py
@@ -159,9 +159,10 @@
         rest[k] = held[f, 0:CAPACITY, :]
 
 
-def update_kernel(home, on_i, east, north, coords, rest, new_x, new_v, total):
+def update_kernel(home, first, second, east, north, coords, rest, new_x, new_v, total):
     for d in range(3):
-        force = home[d] + on_i[d] + east[d] + north[d]
+        on_i = jnp.concatenate([first[d], second[d]], axis=0)
+        force = home[d] + on_i + east[d] + north[d]
         fresh = rest[d] + TSTEP * rest[3] * force
         total[d] = force
         new_v[d] = fresh
@@ -264,15 +265,23 @@
     for k in range(CAPACITY//2-RING,CAPACITY//2):
         out_copy(k).wait()
 
-def ireduce_kernel(ti,fi):
-    lane = lax.broadcasted_iota(jnp.int32,(8,128),1)
+def ireduce_kernel(*refs):
+    fi = refs[8]
+    lane = lax.broadcasted_iota(jnp.int32, (8, BLOCK), 1)
     for b in range(8):
-        cc=[]
+        ti = refs[b]
+        cc = []
         for c in range(16):
-            r=[jnp.sum(ti[3*b+d,c],axis=1,keepdims=True) for d in range(3)]
-            cc.append(jnp.where(lane==0,r[0],jnp.where(lane==1,r[1],r[2])))
-        m=jnp.concatenate(cc,axis=0)[:, :8].T
-        for d in range(3): fi[d,b:b+1,:]=m[d:d+1]
+            r = [jnp.sum(ti[d, c], axis=1, keepdims=True) for d in range(3)]
+            cc.append(jnp.where(lane == 0, r[0], jnp.where(lane == 1, r[1], r[2])))
+        m = jnp.concatenate(cc, axis=0)[:, :8].T
+        for d in range(3):
+            fi[d, b : b + 1, :] = m[d : d + 1]
+
+
+def onward_kernel(first, on_north, from_corner, out):
+    for d in range(3):
+        out[d] = on_north[d] + from_corner[d]
 
 
 VM = pl.BlockSpec(memory_space=pltpu.VMEM)
@@ -284,6 +293,22 @@
 
 def planes(count, rows=CAPACITY):
     return jax.ShapeDtypeStruct((count, rows, BLOCK), jnp.float32)
+
+
+def lane_sums(sums, step):
+    def stream(n):
+        return pl.BlockSpec((3, 16, 8, BLOCK), lambda i: (8 * (i + step) + n, 0, 0, 0))
+
+    return pl.pallas_call(
+        ireduce_kernel,
+        grid=(CAPACITY // 16,),
+        out_shape=planes(3, CAPACITY // 2),
+        in_specs=[stream(n) for n in range(8)],
+        out_specs=pl.BlockSpec((3, 8, BLOCK), lambda i: (0, i, 0)),
+        compiler_params=PARAMS,
+        cost_estimate=pl.CostEstimate(flops=10_000_000, bytes_accessed=14_000_000, transcendentals=0),
+        name="lane_sums",
+    )(*[sums] * 8)
 
 
 def body(positions, velocities, charges, repel_root, disperse_root, inverse_mass, move, tiles):
@@ -357,25 +382,25 @@
     )(tiles.reshape(18, 128, 2).transpose(0, 2, 1).reshape(-1), coords, east, north, near, far)
     from_corner = passed_along(on_corner, 1, 0)
     from_east = passed_along(on_east, 1, 0)
-    from_north = passed_along(on_north + from_corner, 0, 1)
-    on_i = pl.pallas_call(
-        ireduce_kernel,
-        grid=(CAPACITY // 8,),
+    first = lane_sums(sums, 0)
+    onward = pl.pallas_call(
+        onward_kernel,
         out_shape=planes(3),
-        in_specs=[pl.BlockSpec((24, 16, 8, BLOCK), lambda i: (i, 0, 0, 0))],
-        out_specs=pl.BlockSpec((3, 8, BLOCK), lambda i: (0, i, 0)),
-        compiler_params=PARAMS,
-        cost_estimate=pl.CostEstimate(flops=20_000_000, bytes_accessed=28_000_000, transcendentals=0),
-        name="ireduce",
-    )(sums)
+        in_specs=[pl.BlockSpec(memory_space=pl.ANY)] + [VM] * 2,
+        out_specs=VM,
+        compiler_params=PARAMS,
+        name="onward",
+    )(first, on_north, from_corner)
+    from_north = passed_along(onward, 0, 1)
+    second = lane_sums(sums, CAPACITY // 16)
     out = pl.pallas_call(
         update_kernel,
         out_shape=(planes(3),) * 3,
-        in_specs=[VM] * 6,
+        in_specs=[VM] * 7,
         out_specs=(VM,) * 3,
         compiler_params=PARAMS,
         name="update",
-    )(on_home, on_i, from_east, from_north, coords, rest)
+    )(on_home, first, second, from_east, from_north, coords, rest)
     return tuple(value.reshape(3, 1, 1, CAPACITY * BLOCK) for value in out)
 
 

time: 124 us -> 117 us (0.944)
  waiting for transfers between devices: 21.5 us -> 16.2 us
  starting transfers between devices: 28.5 us -> 25.6 us
    ppermute x5, waiting for transfers between devices: 5.4 us -> 0.01 us  [passed_along(): lax.ppermute(value, 'gx', [(s, (s + step_x) % nx) for s in range(nx)])]
    ppermute x4, starting transfers between devices: 15.5 us -> 12.1 us  [passed_along(): lax.ppermute(value, 'gy', [(s, (s + step_y) % ny) for s in range(ny)])]
    pallas_call x1 -> x3, Pallas kernels: 20.2 us -> 20.9 us  [the longest x2 20.9 us: lane_sums(): pl.pallas_call(ireduce_kernel, grid=(CAPACITY // 16,), out_shape=planes(3...]
  transfers between devices with their start and end apart: 11 -> 11, of which waited for: 5 -> 4; matrix products, arithmetic and copies ran while one was open for 1% -> 1% of each run, Pallas kernels for 19% -> 21%
where the time goes in v6:
time: 117 us; the launch traced here: 115 us
  Pallas kernels  70.2 us (60%)
  starting transfers between devices  25.6 us (22%)
  waiting for transfers between devices  16.2 us (14%)
  local copies, waits for them, and re-layouts  2.62 us (2%)
    pallas_call x1, Pallas kernels, body(): pl.pallas_call(pair_kernel, out_shape=(planes(3),) * 4 + (jax.ShapeDtypeS...  40.9 us
    pallas_call x2, Pallas kernels, lane_sums(): pl.pallas_call(ireduce_kernel, grid=(CAPACITY // 16,), out_shape=planes(3...  20.9 us
    ppermute x4, waiting for transfers between devices, passed_along(): lax.ppermute(value, 'gy', [(s, (s + step_y) % ny) for s in range(ny)])  13.5 us
    ppermute x4, starting transfers between devices, passed_along(): lax.ppermute(value, 'gy', [(s, (s + step_y) % ny) for s in range(ny)])  12.1 us
    ppermute x5, starting transfers between devices, passed_along(): lax.ppermute(value, 'gx', [(s, (s + step_x) % nx) for s in range(nx)])  9.41 us
    pallas_call x1, Pallas kernels, body(): pl.pallas_call(stay_kernel, out_shape=(planes(10), jax.ShapeDtypeStruct((...  3.08 us
    ppermute x1, starting transfers between devices, sent(): return lax.ppermute(value, ('gx', 'gy'), pairs)  2.75 us
    pallas_call x1, Pallas kernels, body(): pl.pallas_call(pack_kernel, out_shape=(planes(3, 24), planes(3, 24), plan...  2.75 us
  transfers between devices with their start and end apart: 11, of which 4 were waited for; matrix products, arithmetic and copies ran while one was open for 1% of the time, Pallas kernels for 21%

profile of v6, /device:TPU:96, one launch (start us, length us, event | category | flops | bytes accessed | tf_op | source)
XLA Modules:
  0.0 115.3 jit_solution(9370113885893882528)
XLA Ops:
  0.6 2.8 %pack.1 = (f32[3,24,128]{2,1,0:T(8,128)}, f32[3,24,128]{2,1,0:T(8,128)}, f32[2,24,128]{2,1,0:T(8,128)}) custom-call(s32[128]{0:T(128)} %bitcast.28, f32[3,128,128]{2,1,0:T(8,128)} %bitcast.15, f32[3,128,128]{2,1,0:T(8,128)} %bitcast.17, f32[128,128]{1,0:T(8,128)} %bitcast.19, f32[128,128]{1,0:T(8,128)} %bitcast.21, f32[128,128]{1,0:T(8,128)} %bitcast.23, ...), custom_call_target="tpu_custom_call" | custom-call | tf_op jit(solution)/shard_map/pack/pallas_call | solution.py:329
  3.4 0.1 collective-permute-start
  3.5 3.8 %collective-permute-start.1 = (f32[3,24,128]{2,1,0:T(8,128)}, f32[3,24,128]{2,1,0:T(8,128)S(1)}, u32[]{:S(2)}, u32[]{:S(2)}) collective-permute-start(f32[3,24,128]{2,1,0:T(8,128)} %get-tuple-element.23), channel_id=1, source_target_pairs={{0,240},{16,0},{32,16},{48,32},{64,48},{80,64},{96,80},{112,96},{1... | collective-permute-start | bytes 110600 | tf_op jit(solution)/shard_map/ppermute | solution.py:23
  7.3 3.1 %stay.1 = (f32[10,144,128]{2,1,0:T(8,128)}, s32[1]{0:T(128)}) custom-call(s32[128]{0:T(128)} %bitcast.29, f32[3,128,128]{2,1,0:T(8,128)} %bitcast.16, f32[3,128,128]{2,1,0:T(8,128)} %bitcast.18, f32[128,128]{1,0:T(8,128)} %bitcast.20, f32[128,128]{1,0:T(8,128)} %bitcast.22, f32[128,128]{1,0:T(8,128)} %bitcast.24, f32[128,128]{1,0:T(8,128)} %bitcast.26), custom_call_target="tpu_custom_call" | custom-call | bytes 6000000 | tf_op jit(solution)/shard_map/stay/pallas_call | solution.py:341
  10.4 0.0 collective-permute-done.left.refs_0_
  10.4 0.0 collective-permute-done.1.right.refs_1_
  10.4 0.0 copy-start.1
  10.4 0.7 copy-done.1
  11.2 0.7 turn.1
  11.9 3.5 %collective-permute-start.2 = (f32[3,24,128]{2,1,0:T(8,128)S(1)}, f32[3,24,128]{2,1,0:T(8,128)S(1)}, u32[]{:S(2)}, u32[]{:S(2)}) collective-permute-start(f32[3,24,128]{2,1,0:T(8,128)S(1)} %get-tuple-element.25), channel_id=1, source_target_pairs={{0,1},{1,2},{2,3},{3,4},{4,5},{5,6},{6,7},{7,8},{8,9},{9,10},{10,1... | collective-permute-start | bytes 110600 | tf_op jit(solution)/shard_map/ppermute | solution.py:25
  15.4 1.0 collective-permute-start.3
  16.4 2.0 %collective-permute-done.2.refs_2_ = f32[3,24,128]{2,1,0:T(8,128)S(1)} collective-permute-done((f32[3,24,128]{2,1,0:T(8,128)S(1)}, f32[3,24,128]{2,1,0:T(8,128)S(1)}, u32[]{:S(2)}, u32[]{:S(2)}) %collective-permute-start.2) | collective-permute-done | bytes 36896 | tf_op jit(solution)/shard_map/ppermute | solution.py:25
  18.4 2.4 %collective-permute-done.3.refs_3_ = f32[3,24,128]{2,1,0:T(8,128)S(1)} collective-permute-done((f32[3,24,128]{2,1,0:T(8,128)S(1)}, f32[3,24,128]{2,1,0:T(8,128)S(1)}, u32[]{:S(2)}, u32[]{:S(2)}) %collective-permute-start.3) | collective-permute-done | bytes 36896 | tf_op jit(solution)/shard_map/ppermute | solution.py:25
  20.8 1.1 copy-done
  21.9 0.9 arrive.1
  22.8 2.0 %collective-permute-start.5 = (f32[6,144,128]{2,1,0:T(8,128)S(1)}, f32[6,144,128]{2,1,0:T(8,128)S(1)}, u32[]{:S(2)}, u32[]{:S(2)}) collective-permute-start(f32[6,144,128]{2,1,0:T(8,128)S(1)} %get-tuple-element.27.home.coords), channel_id=1, source_target_pairs={{0,15},{1,0},{2,1},{3,2},{4,3},{5,4},{6,5},{7,6},{8,7},{9,8},{10,9... | collective-permute-start | bytes 1327112 | tf_op jit(solution)/shard_map/ppermute | solution.py:25
  24.8 2.8 %collective-permute-start.7 = (f32[6,144,128]{2,1,0:T(8,128)S(1)}, f32[6,144,128]{2,1,0:T(8,128)S(1)}, u32[]{:S(2)}, u32[]{:S(2)}) collective-permute-start(f32[6,144,128]{2,1,0:T(8,128)S(1)} %get-tuple-element.27.home.coords), channel_id=1, source_target_pairs={{0,255},{1,240},{2,241},{3,242},{4,243},{5,244},{6,245},{7,246},{8... | collective-permute-start | bytes 1327112 | tf_op jit(solution)/shard_map/ppermute | solution.py:47
  27.6 0.1 collective-permute-start.4
  27.7 9.1 %collective-permute-done.5.north = f32[6,144,128]{2,1,0:T(8,128)S(1)} collective-permute-done((f32[6,144,128]{2,1,0:T(8,128)S(1)}, f32[6,144,128]{2,1,0:T(8,128)S(1)}, u32[]{:S(2)}, u32[]{:S(2)}) %collective-permute-start.5) | collective-permute-done | bytes 442400 | tf_op jit(solution)/shard_map/ppermute | solution.py:25
  36.7 1.3 %collective-permute-start.6 = (f32[6,144,128]{2,1,0:T(8,128)S(1)}, f32[6,144,128]{2,1,0:T(8,128)S(1)}, u32[]{:S(2)}, u32[]{:S(2)}) collective-permute-start(f32[6,144,128]{2,1,0:T(8,128)S(1)} %collective-permute-done.5.north), channel_id=1, source_target_pairs={{16,0},{48,32},{80,64},{112,96},{144,128},{176,160},{208,192},{240... | collective-permute-start | bytes 1327112 | tf_op jit(solution)/shard_map/ppermute | solution.py:40
  38.0 0.7 reshape.42
  38.8 2.7 %collective-permute-done.7.far = f32[6,144,128]{2,1,0:T(8,128)S(1)} collective-permute-done((f32[6,144,128]{2,1,0:T(8,128)S(1)}, f32[6,144,128]{2,1,0:T(8,128)S(1)}, u32[]{:S(2)}, u32[]{:S(2)}) %collective-permute-start.7) | collective-permute-done | bytes 442400 | tf_op jit(solution)/shard_map/ppermute | solution.py:47
  41.5 40.9 %pair.1 = (f32[3,144,128]{2,1,0:T(8,128)S(1)}, f32[3,144,128]{2,1,0:T(8,128)S(1)}, f32[3,144,128]{2,1,0:T(8,128)S(1)}, f32[3,144,128]{2,1,0:T(8,128)S(1)}, f32[432,16,8,128]{3,2,1,0:T(8,128)}) custom-call(s32[4608]{0:T(1024)S(1)} %reshape.43.tiles, f32[6,144,128]{2,1,0:T(8,128)S(1)} %get-tuple-element.27.home.coords, ...), custom_call_target="tpu_custom_call" | custom-call | tf_op jit(solution)/shard_map/pair/pallas_call | solution.py:374
  82.4 0.4 collective-permute-start.9
  82.8 5.0 %collective-permute-start.8 = (f32[3,144,128]{2,1,0:T(8,128)S(1)}, f32[3,144,128]{2,1,0:T(8,128)S(1)}, u32[]{:S(2)}, u32[]{:S(2)}) collective-permute-start(f32[3,144,128]{2,1,0:T(8,128)S(1)} %get-tuple-element.30), channel_id=1, source_target_pairs={{0,16},{16,32},{32,48},{48,64},{64,80},{80,96},{96,112},{112,128},... | collective-permute-start | bytes 663560 | tf_op jit(solution)/shard_map/ppermute | solution.py:23
  87.8 10.4 %lane_sums.2.first = f32[3,72,128]{2,1,0:T(8,128)S(1)} custom-call(f32[432,16,8,128]{3,2,1,0:T(8,128)} %get-tuple-element.29.refs_0_.refs_1_.refs_2_.refs_3_.refs_4_.refs_5_.refs_6_.refs_7_, f32[432,16,8,128]{3,2,1,0:T(8,128)} %get-tuple-element.29.refs_0_.refs_1_.refs_2_.refs_3_.refs_4_.refs_5_.refs_6_.refs_7_, ...), custom_call_target="tpu_custom_call" | custom-call | flops 10000000 | bytes 14000000 | tf_op jit(solution)/shard_map/lane_sums/pallas_call | solution.py:302
  98.3 0.0 collective-permute-done.9.from_corner
  98.3 5.6 %collective-permute-start.10 = (f32[3,144,128]{2,1,0:T(8,128)S(1)}, f32[3,144,128]{2,1,0:T(8,128)S(1)}, u32[]{:S(2)}, u32[]{:S(2)}) collective-permute-start(f32[3,144,128]{2,1,0:T(8,128)S(1)} %onward.1), channel_id=1, source_target_pairs={{0,1},{1,2},{2,3},{3,4},{4,5},{5,6},{6,7},{7,8},{8,9},{9,10},{10,1... | collective-permute-start | bytes 663560 | tf_op jit(solution)/shard_map/ppermute | solution.py:25
  103.9 10.4 %lane_sums.3.second = f32[3,72,128]{2,1,0:T(8,128)S(1)} custom-call(f32[432,16,8,128]{3,2,1,0:T(8,128)} %get-tuple-element.29.refs_0_.refs_1_.refs_2_.refs_3_.refs_4_.refs_5_.refs_6_.refs_7_, f32[432,16,8,128]{3,2,1,0:T(8,128)} %get-tuple-element.29.refs_0_.refs_1_.refs_2_.refs_3_.refs_4_.refs_5_.refs_6_.refs_7_, ...), custom_call_target="tpu_custom_call" | custom-call | flops 10000000 | bytes 14000000 | tf_op jit(solution)/shard_map/lane_sums/pallas_call | solution.py:302
  114.4 0.0 collective-permute-done.8.east
  114.4 0.0 collective-permute-done.10.north
  114.4 0.9 update.1
  (6 shorter events, 0.1 us)
Async XLA Ops:
  3.4 7.0 %collective-permute-start = (f32[3,24,128]{2,1,0:T(8,128)}, f32[3,24,128]{2,1,0:T(8,128)S(1)}, u32[]{:S(2)}, u32[]{:S(2)}) collective-permute-start(f32[3,24,128]{2,1,0:T(8,128)} %get-tuple-element.22), channel_id=1, source_target_pairs={{0,16},{16,32},{32,48},{48,64},{64,80},{80,96},{96,112},{112,128},... | collective-permute-start | bytes 110600 | tf_op jit(solution)/shard_map/ppermute | solution.py:23
  3.5 6.9 %collective-permute-start.1 = (f32[3,24,128]{2,1,0:T(8,128)}, f32[3,24,128]{2,1,0:T(8,128)S(1)}, u32[]{:S(2)}, u32[]{:S(2)}) collective-permute-start(f32[3,24,128]{2,1,0:T(8,128)} %get-tuple-element.23), channel_id=1, source_target_pairs={{0,240},{16,0},{32,16},{48,32},{64,48},{80,64},{96,80},{112,96},{1... | collective-permute-start | bytes 110600 | tf_op jit(solution)/shard_map/ppermute | solution.py:23
  10.4 0.7 copy-start.1
  11.9 6.5 %collective-permute-start.2 = (f32[3,24,128]{2,1,0:T(8,128)S(1)}, f32[3,24,128]{2,1,0:T(8,128)S(1)}, u32[]{:S(2)}, u32[]{:S(2)}) collective-permute-start(f32[3,24,128]{2,1,0:T(8,128)S(1)} %get-tuple-element.25), channel_id=1, source_target_pairs={{0,1},{1,2},{2,3},{3,4},{4,5},{5,6},{6,7},{7,8},{8,9},{9,10},{10,1... | collective-permute-start | bytes 110600 | tf_op jit(solution)/shard_map/ppermute | solution.py:25
  15.4 5.5 %collective-permute-start.3 = (f32[3,24,128]{2,1,0:T(8,128)S(1)}, f32[3,24,128]{2,1,0:T(8,128)S(1)}, u32[]{:S(2)}, u32[]{:S(2)}) collective-permute-start(f32[3,24,128]{2,1,0:T(8,128)S(1)} %get-tuple-element.26), channel_id=1, source_target_pairs={{0,15},{1,0},{2,1},{3,2},{4,3},{5,4},{6,5},{7,6},{8,7},{9,8},{10,9... | collective-permute-start | bytes 110600 | tf_op jit(solution)/shard_map/ppermute | solution.py:25
  20.8 1.1 copy-start
  22.8 13.9 %collective-permute-start.5 = (f32[6,144,128]{2,1,0:T(8,128)S(1)}, f32[6,144,128]{2,1,0:T(8,128)S(1)}, u32[]{:S(2)}, u32[]{:S(2)}) collective-permute-start(f32[6,144,128]{2,1,0:T(8,128)S(1)} %get-tuple-element.27.home.coords), channel_id=1, source_target_pairs={{0,15},{1,0},{2,1},{3,2},{4,3},{5,4},{6,5},{7,6},{8,7},{9,8},{10,9... | collective-permute-start | bytes 1327112 | tf_op jit(solution)/shard_map/ppermute | solution.py:25
  24.8 16.6 %collective-permute-start.7 = (f32[6,144,128]{2,1,0:T(8,128)S(1)}, f32[6,144,128]{2,1,0:T(8,128)S(1)}, u32[]{:S(2)}, u32[]{:S(2)}) collective-permute-start(f32[6,144,128]{2,1,0:T(8,128)S(1)} %get-tuple-element.27.home.coords), channel_id=1, source_target_pairs={{0,255},{1,240},{2,241},{3,242},{4,243},{5,244},{6,245},{7,246},{8... | collective-permute-start | bytes 1327112 | tf_op jit(solution)/shard_map/ppermute | solution.py:47
  27.6 13.9 %collective-permute-start.4 = (f32[6,144,128]{2,1,0:T(8,128)S(1)}, f32[6,144,128]{2,1,0:T(8,128)S(1)}, u32[]{:S(2)}, u32[]{:S(2)}) collective-permute-start(f32[6,144,128]{2,1,0:T(8,128)S(1)} %get-tuple-element.27.home.coords), channel_id=1, source_target_pairs={{0,240},{16,0},{32,16},{48,32},{64,48},{80,64},{96,80},{112,96},{1... | collective-permute-start | bytes 1327112 | tf_op jit(solution)/shard_map/ppermute | solution.py:23
  36.7 4.7 %collective-permute-start.6 = (f32[6,144,128]{2,1,0:T(8,128)S(1)}, f32[6,144,128]{2,1,0:T(8,128)S(1)}, u32[]{:S(2)}, u32[]{:S(2)}) collective-permute-start(f32[6,144,128]{2,1,0:T(8,128)S(1)} %collective-permute-done.5.north), channel_id=1, source_target_pairs={{16,0},{48,32},{80,64},{112,96},{144,128},{176,160},{208,192},{240... | collective-permute-start | bytes 1327112 | tf_op jit(solution)/shard_map/ppermute | solution.py:40
  82.4 15.9 %collective-permute-start.9 = (f32[3,144,128]{2,1,0:T(8,128)S(1)}, f32[3,144,128]{2,1,0:T(8,128)S(1)}, u32[]{:S(2)}, u32[]{:S(2)}) collective-permute-start(f32[3,144,128]{2,1,0:T(8,128)S(1)} %get-tuple-element.32), channel_id=1, source_target_pairs={{0,16},{16,32},{32,48},{48,64},{64,80},{80,96},{96,112},{112,128},... | collective-permute-start | bytes 663560 | tf_op jit(solution)/shard_map/ppermute | solution.py:23
  82.8 31.6 %collective-permute-start.8 = (f32[3,144,128]{2,1,0:T(8,128)S(1)}, f32[3,144,128]{2,1,0:T(8,128)S(1)}, u32[]{:S(2)}, u32[]{:S(2)}) collective-permute-start(f32[3,144,128]{2,1,0:T(8,128)S(1)} %get-tuple-element.30), channel_id=1, source_target_pairs={{0,16},{16,32},{32,48},{48,64},{64,80},{80,96},{96,112},{112,128},... | collective-permute-start | bytes 663560 | tf_op jit(solution)/shard_map/ppermute | solution.py:23
  98.3 16.1 %collective-permute-start.10 = (f32[3,144,128]{2,1,0:T(8,128)S(1)}, f32[3,144,128]{2,1,0:T(8,128)S(1)}, u32[]{:S(2)}, u32[]{:S(2)}) collective-permute-start(f32[3,144,128]{2,1,0:T(8,128)S(1)} %onward.1), channel_id=1, source_target_pairs={{0,1},{1,2},{2,3},{3,4},{4,5},{5,6},{6,7},{7,8},{8,9},{9,10},{10,1... | collective-permute-start | bytes 663560 | tf_op jit(solution)/shard_map/ppermute | solution.py:25

commit v7 on v4

--- a/solution.py
+++ b/solution.py
@@ -159,9 +159,9 @@
         rest[k] = held[f, 0:CAPACITY, :]
 
 
-def update_kernel(home, east, north, far, coords, rest, new_x, new_v, total):
+def update_kernel(home, east, north, coords, rest, new_x, new_v, total):
     for d in range(3):
-        force = home[d] + east[d] + north[d] + far[d]
+        force = home[d] + east[d] + north[d]
         fresh = rest[d] + TSTEP * rest[3] * force
         total[d] = force
         new_v[d] = fresh
@@ -356,18 +356,17 @@
         compiler_params=PARAMS,
         name="pair",
     )(tiles.reshape(18, 128, 2).transpose(0, 2, 1).reshape(-1), coords, east, north, near, far)
-    from_near = sent(on_corner, 1, 0, 0)
-    from_far = sent(on_corner, 1, 1, 1)
+    from_corner = passed_along(on_corner, 1, 0)
     from_east = passed_along(on_east, 1, 0)
-    from_north = passed_along(on_north + from_near, 0, 1)
+    from_north = passed_along(on_north + from_corner, 0, 1)
     out = pl.pallas_call(
         update_kernel,
         out_shape=(planes(3),) * 3,
-        in_specs=[VM] * 6,
+        in_specs=[VM] * 5,
         out_specs=(VM,) * 3,
         compiler_params=PARAMS,
         name="update",
-    )(on_home, from_east, from_north, from_far, coords, rest)
+    )(on_home, from_east, from_north, coords, rest)
     return tuple(value.reshape(3, 1, 1, CAPACITY * BLOCK) for value in out)
 
 

time: 112 us -> 112 us (level)
    ppermute x4, starting transfers between devices: 8.23 us -> 15.4 us  [passed_along(): lax.ppermute(value, 'gy', [(s, (s + step_y) % ny) for s in range(ny)])]
    ppermute x4 -> x5, starting transfers between devices: 13.2 us -> 9.07 us  [passed_along(): lax.ppermute(value, 'gx', [(s, (s + step_x) % nx) for s in range(nx)])]
    ppermute x4, waiting for transfers between devices: 13.2 us -> 16.9 us  [passed_along(): lax.ppermute(value, 'gy', [(s, (s + step_y) % ny) for s in range(ny)])]
    ppermute x4 -> x5, waiting for transfers between devices: 8.31 us -> 5.38 us  [passed_along(): lax.ppermute(value, 'gx', [(s, (s + step_x) % nx) for s in range(nx)])]
    ppermute x2 -> x1, starting transfers between devices: 3.48 us -> 1.28 us  [sent(): lax.ppermute(value, 'gx', [(s, (s + step_x) % nx) for s in range(nx) if s...]
    ppermute x2 -> x1, starting transfers between devices: 4.07 us -> 2.88 us  [sent(): return lax.ppermute(value, ('gx', 'gy'), pairs)]
    ppermute x2 -> x1, waiting for transfers between devices: 3.38 us -> 3.38 us  [sent(): return lax.ppermute(value, ('gx', 'gy'), pairs)]
  transfers between devices with their start and end apart: 12 -> 11, of which waited for: 6 -> 6; matrix products, arithmetic and copies ran while one was open for 0% -> 0% of each run, Pallas kernels for 3% -> 3%
where the time goes in v7:
time: 112 us; the launch traced here: 110 us
  Pallas kernels  54.1 us (48%)
  starting transfers between devices  28.7 us (26%)
  waiting for transfers between devices  25.7 us (23%)
  local copies, waits for them, and re-layouts  1.17 us (1%)
    pallas_call x1, Pallas kernels, body(): pl.pallas_call(pair_kernel, out_shape=(planes(3),) * 4, in_specs=[SM] + [...  45.9 us
    ppermute x4, waiting for transfers between devices, passed_along(): lax.ppermute(value, 'gy', [(s, (s + step_y) % ny) for s in range(ny)])  16.9 us
    ppermute x4, starting transfers between devices, passed_along(): lax.ppermute(value, 'gy', [(s, (s + step_y) % ny) for s in range(ny)])  15.4 us
    ppermute x5, starting transfers between devices, passed_along(): lax.ppermute(value, 'gx', [(s, (s + step_x) % nx) for s in range(nx)])  9.07 us
    ppermute x5, waiting for transfers between devices, passed_along(): lax.ppermute(value, 'gx', [(s, (s + step_x) % nx) for s in range(nx)])  5.38 us
    ppermute x1, waiting for transfers between devices, sent(): return lax.ppermute(value, ('gx', 'gy'), pairs)  3.38 us
    pallas_call x1, Pallas kernels, body(): pl.pallas_call(stay_kernel, out_shape=(planes(10), jax.ShapeDtypeStruct((...  3.07 us
    ppermute x1, starting transfers between devices, sent(): return lax.ppermute(value, ('gx', 'gy'), pairs)  2.88 us
  transfers between devices with their start and end apart: 11, of which 6 were waited for; matrix products, arithmetic and copies ran while one was open for 0% of the time, Pallas kernels for 3%

profile of v7, /device:TPU:96, one launch (start us, length us, event | category | flops | bytes accessed | tf_op | source)
XLA Modules:
  0.0 110.4 jit_solution(5758304273008529855)
XLA Ops:
  0.6 2.8 %pack.1 = (f32[3,24,128]{2,1,0:T(8,128)}, f32[3,24,128]{2,1,0:T(8,128)}, f32[2,24,128]{2,1,0:T(8,128)}) custom-call(s32[128]{0:T(128)} %bitcast.28, f32[3,128,128]{2,1,0:T(8,128)} %bitcast.15, f32[3,128,128]{2,1,0:T(8,128)} %bitcast.17, f32[128,128]{1,0:T(8,128)} %bitcast.19, f32[128,128]{1,0:T(8,128)} %bitcast.21, f32[128,128]{1,0:T(8,128)} %bitcast.23, ...), custom_call_target="tpu_custom_call" | custom-call | tf_op jit(solution)/shard_map/pack/pallas_call | solution.py:305
  3.5 0.3 collective-permute-start
  3.7 0.0 copy-start.1
  3.7 3.7 %collective-permute-start.1 = (f32[3,24,128]{2,1,0:T(8,128)}, f32[3,24,128]{2,1,0:T(8,128)S(1)}, u32[]{:S(2)}, u32[]{:S(2)}) collective-permute-start(f32[3,24,128]{2,1,0:T(8,128)} %get-tuple-element.22), channel_id=1, source_target_pairs={{0,240},{16,0},{32,16},{48,32},{64,48},{80,64},{96,80},{112,96},{1... | collective-permute-start | bytes 110600 | tf_op jit(solution)/shard_map/ppermute | solution.py:23
  7.4 3.1 %stay.1 = (f32[10,144,128]{2,1,0:T(8,128)}, s32[1]{0:T(128)}) custom-call(s32[128]{0:T(128)} %bitcast.29, f32[3,128,128]{2,1,0:T(8,128)} %bitcast.16, f32[3,128,128]{2,1,0:T(8,128)} %bitcast.18, f32[128,128]{1,0:T(8,128)} %bitcast.20, f32[128,128]{1,0:T(8,128)} %bitcast.22, f32[128,128]{1,0:T(8,128)} %bitcast.24, f32[128,128]{1,0:T(8,128)} %bitcast.26), custom_call_target="tpu_custom_call" | custom-call | bytes 6000000 | tf_op jit(solution)/shard_map/stay/pallas_call | solution.py:317
  10.5 0.0 collective-permute-done.left.refs_0_
  10.5 0.0 collective-permute-done.1.right.refs_1_
  10.5 0.0 copy-done.1
  10.5 0.6 turn.1
  11.1 3.6 %collective-permute-start.2 = (f32[3,24,128]{2,1,0:T(8,128)S(1)}, f32[3,24,128]{2,1,0:T(8,128)S(1)}, u32[]{:S(2)}, u32[]{:S(2)}) collective-permute-start(f32[3,24,128]{2,1,0:T(8,128)S(1)} %get-tuple-element.24), channel_id=1, source_target_pairs={{0,1},{1,2},{2,3},{3,4},{4,5},{5,6},{6,7},{7,8},{8,9},{9,10},{10,1... | collective-permute-start | bytes 110600 | tf_op jit(solution)/shard_map/ppermute | solution.py:25
  14.7 0.9 collective-permute-start.3
  15.6 2.0 %collective-permute-done.2.refs_2_ = f32[3,24,128]{2,1,0:T(8,128)S(1)} collective-permute-done((f32[3,24,128]{2,1,0:T(8,128)S(1)}, f32[3,24,128]{2,1,0:T(8,128)S(1)}, u32[]{:S(2)}, u32[]{:S(2)}) %collective-permute-start.2) | collective-permute-done | bytes 36896 | tf_op jit(solution)/shard_map/ppermute | solution.py:25
  17.6 2.6 %collective-permute-done.3.refs_3_ = f32[3,24,128]{2,1,0:T(8,128)S(1)} collective-permute-done((f32[3,24,128]{2,1,0:T(8,128)S(1)}, f32[3,24,128]{2,1,0:T(8,128)S(1)}, u32[]{:S(2)}, u32[]{:S(2)}) %collective-permute-start.3) | collective-permute-done | bytes 36896 | tf_op jit(solution)/shard_map/ppermute | solution.py:25
  20.1 1.1 %copy-done = f32[10,144,128]{2,1,0:T(8,128)S(1)} copy-done((f32[10,144,128]{2,1,0:T(8,128)S(1)}, f32[10,144,128]{2,1,0:T(8,128)}, u32[]{:S(2)}) %copy-start) | copy-done | bytes 737304
  21.3 0.8 arrive.1
  22.0 1.9 %collective-permute-start.5 = (f32[6,144,128]{2,1,0:T(8,128)S(1)}, f32[6,144,128]{2,1,0:T(8,128)S(1)}, u32[]{:S(2)}, u32[]{:S(2)}) collective-permute-start(f32[6,144,128]{2,1,0:T(8,128)S(1)} %get-tuple-element.26.home.coords), channel_id=1, source_target_pairs={{0,15},{1,0},{2,1},{3,2},{4,3},{5,4},{6,5},{7,6},{8,7},{9,8},{10,9... | collective-permute-start | bytes 1327112 | tf_op jit(solution)/shard_map/ppermute | solution.py:25
  23.9 2.9 %collective-permute-start.7 = (f32[6,144,128]{2,1,0:T(8,128)S(1)}, f32[6,144,128]{2,1,0:T(8,128)S(1)}, u32[]{:S(2)}, u32[]{:S(2)}) collective-permute-start(f32[6,144,128]{2,1,0:T(8,128)S(1)} %get-tuple-element.26.home.coords), channel_id=1, source_target_pairs={{0,255},{1,240},{2,241},{3,242},{4,243},{5,244},{6,245},{7,246},{8... | collective-permute-start | bytes 1327112 | tf_op jit(solution)/shard_map/ppermute | solution.py:47
  26.8 0.1 collective-permute-start.4
  26.9 8.9 %collective-permute-done.5.north = f32[6,144,128]{2,1,0:T(8,128)S(1)} collective-permute-done((f32[6,144,128]{2,1,0:T(8,128)S(1)}, f32[6,144,128]{2,1,0:T(8,128)S(1)}, u32[]{:S(2)}, u32[]{:S(2)}) %collective-permute-start.5) | collective-permute-done | bytes 442400 | tf_op jit(solution)/shard_map/ppermute | solution.py:25
  35.8 1.3 %collective-permute-start.6 = (f32[6,144,128]{2,1,0:T(8,128)S(1)}, f32[6,144,128]{2,1,0:T(8,128)S(1)}, u32[]{:S(2)}, u32[]{:S(2)}) collective-permute-start(f32[6,144,128]{2,1,0:T(8,128)S(1)} %collective-permute-done.5.north), channel_id=1, source_target_pairs={{16,0},{48,32},{80,64},{112,96},{144,128},{176,160},{208,192},{240... | collective-permute-start | bytes 1327112 | tf_op jit(solution)/shard_map/ppermute | solution.py:40
  37.1 0.0 copy-done.2
  37.2 3.4 %collective-permute-done.7.far = f32[6,144,128]{2,1,0:T(8,128)S(1)} collective-permute-done((f32[6,144,128]{2,1,0:T(8,128)S(1)}, f32[6,144,128]{2,1,0:T(8,128)S(1)}, u32[]{:S(2)}, u32[]{:S(2)}) %collective-permute-start.7) | collective-permute-done | bytes 442400 | tf_op jit(solution)/shard_map/ppermute | solution.py:47
  40.6 0.0 collective-permute-done.4.east
  40.6 0.0 collective-permute-done.6.near
  40.6 45.9 %pair.1 = (f32[3,144,128]{2,1,0:T(8,128)S(1)}, f32[3,144,128]{2,1,0:T(8,128)S(1)}, f32[3,144,128]{2,1,0:T(8,128)S(1)}, f32[3,144,128]{2,1,0:T(8,128)S(1)}) custom-call(s32[4608]{0:T(1024)S(1)} %reshape.43.tiles, f32[6,144,128]{2,1,0:T(8,128)S(1)} %get-tuple-element.26.home.coords, f32[6,144,128]{2,1,0:T(8,128)S(1)} %collective-permute-done.4.east, ...), custom_call_target="tpu_custom_call" | custom-call | tf_op jit(solution)/shard_map/pair/pallas_call | solution.py:350
  86.5 0.3 collective-permute-start.9
  86.8 4.7 %collective-permute-start.8 = (f32[3,144,128]{2,1,0:T(8,128)S(1)}, f32[3,144,128]{2,1,0:T(8,128)S(1)}, u32[]{:S(2)}, u32[]{:S(2)}) collective-permute-start(f32[3,144,128]{2,1,0:T(8,128)S(1)} %get-tuple-element.28), channel_id=1, source_target_pairs={{0,16},{16,32},{32,48},{48,64},{64,80},{80,96},{96,112},{112,128},... | collective-permute-start | bytes 663560 | tf_op jit(solution)/shard_map/ppermute | solution.py:23
  91.6 5.4 %collective-permute-done.9 = f32[3,144,128]{2,1,0:T(8,128)S(1)} collective-permute-done((f32[3,144,128]{2,1,0:T(8,128)S(1)}, f32[3,144,128]{2,1,0:T(8,128)S(1)}, u32[]{:S(2)}, u32[]{:S(2)}) %collective-permute-start.9) | collective-permute-done | bytes 221216 | tf_op jit(solution)/shard_map/ppermute | solution.py:23
  97.0 9.0 %collective-permute-start.10 = (f32[3,144,128]{2,1,0:T(8,128)S(1)}, f32[3,144,128]{2,1,0:T(8,128)S(1)}, u32[]{:S(2)}, u32[]{:S(2)}) collective-permute-start(f32[3,144,128]{2,1,0:T(8,128)S(1)} %add.3), channel_id=1, source_target_pairs={{0,1},{1,2},{2,3},{3,4},{4,5},{5,6},{6,7},{7,8},{8,9},{9,10},{10,1... | collective-permute-start | bytes 663560 | tf_op jit(solution)/shard_map/ppermute | solution.py:25
  106.0 0.0 collective-permute-done.8.east
  106.0 3.4 %collective-permute-done.10.north = f32[3,144,128]{2,1,0:T(8,128)S(1)} collective-permute-done((f32[3,144,128]{2,1,0:T(8,128)S(1)}, f32[3,144,128]{2,1,0:T(8,128)S(1)}, u32[]{:S(2)}, u32[]{:S(2)}) %collective-permute-start.10) | collective-permute-done | bytes 221216 | tf_op jit(solution)/shard_map/ppermute | solution.py:25
  109.5 0.9 update.1
  (6 shorter events, 0.1 us)
Async XLA Ops:
  3.5 7.0 %collective-permute-start = (f32[3,24,128]{2,1,0:T(8,128)}, f32[3,24,128]{2,1,0:T(8,128)S(1)}, u32[]{:S(2)}, u32[]{:S(2)}) collective-permute-start(f32[3,24,128]{2,1,0:T(8,128)} %get-tuple-element.21), channel_id=1, source_target_pairs={{0,16},{16,32},{32,48},{48,64},{64,80},{80,96},{96,112},{112,128},... | collective-permute-start | bytes 110600 | tf_op jit(solution)/shard_map/ppermute | solution.py:23
  3.7 6.8 %copy-start.1 = (f32[2,24,128]{2,1,0:T(8,128)S(1)}, f32[2,24,128]{2,1,0:T(8,128)}, u32[]{:S(2)}) copy-start(f32[2,24,128]{2,1,0:T(8,128)} %get-tuple-element.23.own) | copy-start | bytes 73732
  3.7 6.8 %collective-permute-start.1 = (f32[3,24,128]{2,1,0:T(8,128)}, f32[3,24,128]{2,1,0:T(8,128)S(1)}, u32[]{:S(2)}, u32[]{:S(2)}) collective-permute-start(f32[3,24,128]{2,1,0:T(8,128)} %get-tuple-element.22), channel_id=1, source_target_pairs={{0,240},{16,0},{32,16},{48,32},{64,48},{80,64},{96,80},{112,96},{1... | collective-permute-start | bytes 110600 | tf_op jit(solution)/shard_map/ppermute | solution.py:23
  11.1 6.5 %collective-permute-start.2 = (f32[3,24,128]{2,1,0:T(8,128)S(1)}, f32[3,24,128]{2,1,0:T(8,128)S(1)}, u32[]{:S(2)}, u32[]{:S(2)}) collective-permute-start(f32[3,24,128]{2,1,0:T(8,128)S(1)} %get-tuple-element.24), channel_id=1, source_target_pairs={{0,1},{1,2},{2,3},{3,4},{4,5},{5,6},{6,7},{7,8},{8,9},{9,10},{10,1... | collective-permute-start | bytes 110600 | tf_op jit(solution)/shard_map/ppermute | solution.py:25
  14.7 5.5 %collective-permute-start.3 = (f32[3,24,128]{2,1,0:T(8,128)S(1)}, f32[3,24,128]{2,1,0:T(8,128)S(1)}, u32[]{:S(2)}, u32[]{:S(2)}) collective-permute-start(f32[3,24,128]{2,1,0:T(8,128)S(1)} %get-tuple-element.25), channel_id=1, source_target_pairs={{0,15},{1,0},{2,1},{3,2},{4,3},{5,4},{6,5},{7,6},{8,7},{9,8},{10,9... | collective-permute-start | bytes 110600 | tf_op jit(solution)/shard_map/ppermute | solution.py:25
  20.1 1.1 %copy-start = (f32[10,144,128]{2,1,0:T(8,128)S(1)}, f32[10,144,128]{2,1,0:T(8,128)}, u32[]{:S(2)}) copy-start(f32[10,144,128]{2,1,0:T(8,128)} %get-tuple-element.20.stay) | copy-start | bytes 2211844
  21.3 15.8 %copy-start.2 = (s32[1,1,2304,2]{2,3,1,0:T(2,128)S(1)}, s32[1,1,2304,2]{2,3,1,0:T(2,128)}, u32[]{:S(2)}) copy-start(s32[1,1,2304,2]{2,3,1,0:T(2,128)} %param.15) | copy-start | bytes 55300
  22.0 13.8 %collective-permute-start.5 = (f32[6,144,128]{2,1,0:T(8,128)S(1)}, f32[6,144,128]{2,1,0:T(8,128)S(1)}, u32[]{:S(2)}, u32[]{:S(2)}) collective-permute-start(f32[6,144,128]{2,1,0:T(8,128)S(1)} %get-tuple-element.26.home.coords), channel_id=1, source_target_pairs={{0,15},{1,0},{2,1},{3,2},{4,3},{5,4},{6,5},{7,6},{8,7},{9,8},{10,9... | collective-permute-start | bytes 1327112 | tf_op jit(solution)/shard_map/ppermute | solution.py:25
  23.9 16.6 %collective-permute-start.7 = (f32[6,144,128]{2,1,0:T(8,128)S(1)}, f32[6,144,128]{2,1,0:T(8,128)S(1)}, u32[]{:S(2)}, u32[]{:S(2)}) collective-permute-start(f32[6,144,128]{2,1,0:T(8,128)S(1)} %get-tuple-element.26.home.coords), channel_id=1, source_target_pairs={{0,255},{1,240},{2,241},{3,242},{4,243},{5,244},{6,245},{7,246},{8... | collective-permute-start | bytes 1327112 | tf_op jit(solution)/shard_map/ppermute | solution.py:47
  26.8 13.8 %collective-permute-start.4 = (f32[6,144,128]{2,1,0:T(8,128)S(1)}, f32[6,144,128]{2,1,0:T(8,128)S(1)}, u32[]{:S(2)}, u32[]{:S(2)}) collective-permute-start(f32[6,144,128]{2,1,0:T(8,128)S(1)} %get-tuple-element.26.home.coords), channel_id=1, source_target_pairs={{0,240},{16,0},{32,16},{48,32},{64,48},{80,64},{96,80},{112,96},{1... | collective-permute-start | bytes 1327112 | tf_op jit(solution)/shard_map/ppermute | solution.py:23
  35.8 4.7 %collective-permute-start.6 = (f32[6,144,128]{2,1,0:T(8,128)S(1)}, f32[6,144,128]{2,1,0:T(8,128)S(1)}, u32[]{:S(2)}, u32[]{:S(2)}) collective-permute-start(f32[6,144,128]{2,1,0:T(8,128)S(1)} %collective-permute-done.5.north), channel_id=1, source_target_pairs={{16,0},{48,32},{80,64},{112,96},{144,128},{176,160},{208,192},{240... | collective-permute-start | bytes 1327112 | tf_op jit(solution)/shard_map/ppermute | solution.py:40
  86.5 10.4 %collective-permute-start.9 = (f32[3,144,128]{2,1,0:T(8,128)S(1)}, f32[3,144,128]{2,1,0:T(8,128)S(1)}, u32[]{:S(2)}, u32[]{:S(2)}) collective-permute-start(f32[3,144,128]{2,1,0:T(8,128)S(1)} %get-tuple-element.30), channel_id=1, source_target_pairs={{0,16},{16,32},{32,48},{48,64},{64,80},{80,96},{96,112},{112,128},... | collective-permute-start | bytes 663560 | tf_op jit(solution)/shard_map/ppermute | solution.py:23
  86.8 19.2 %collective-permute-start.8 = (f32[3,144,128]{2,1,0:T(8,128)S(1)}, f32[3,144,128]{2,1,0:T(8,128)S(1)}, u32[]{:S(2)}, u32[]{:S(2)}) collective-permute-start(f32[3,144,128]{2,1,0:T(8,128)S(1)} %get-tuple-element.28), channel_id=1, source_target_pairs={{0,16},{16,32},{32,48},{48,64},{64,80},{80,96},{96,112},{112,128},... | collective-permute-start | bytes 663560 | tf_op jit(solution)/shard_map/ppermute | solution.py:23
  97.0 12.5 %collective-permute-start.10 = (f32[3,144,128]{2,1,0:T(8,128)S(1)}, f32[3,144,128]{2,1,0:T(8,128)S(1)}, u32[]{:S(2)}, u32[]{:S(2)}) collective-permute-start(f32[3,144,128]{2,1,0:T(8,128)S(1)} %add.3), channel_id=1, source_target_pairs={{0,1},{1,2},{2,3},{3,4},{4,5},{5,6},{6,7},{7,8},{8,9},{9,10},{10,1... | collective-permute-start | bytes 663560 | tf_op jit(solution)/shard_map/ppermute | solution.py:25

commit v8 on v3

--- a/solution.py
+++ b/solution.py
@@ -267,6 +267,7 @@
 SM = pl.BlockSpec(memory_space=pltpu.SMEM)
 HBM = pl.BlockSpec(memory_space=pltpu.HBM)
 PARAMS = pltpu.CompilerParams(vmem_limit_bytes=48 * 1024 * 1024)
+STAY = pltpu.CompilerParams(vmem_limit_bytes=50 * 1024 * 1024)
 WIDE = pltpu.CompilerParams(vmem_limit_bytes=56 * 1024 * 1024)
 
 
@@ -307,7 +308,7 @@
         in_specs=[HBM] * 7,
         out_specs=(VM, SM),
         scratch_shapes=held + [pltpu.SemaphoreType.DMA((7,))],
-        compiler_params=WIDE,
+        compiler_params=STAY,
         cost_estimate=pl.CostEstimate(flops=0, bytes_accessed=6_000_000, transcendentals=0),
         name="stay",
     )(*inputs)

time: 111 us -> 110 us (level)
  transfers between devices with their start and end apart: 10 -> 10, of which waited for: 6 -> 6; matrix products, arithmetic and copies ran while one was open for 0% -> 0% of each run, Pallas kernels for 3% -> 2%
where the time goes in v8:
time: 110 us; the launch traced here: 109 us
  Pallas kernels  53.9 us (49%)
  waiting for transfers between devices  35 us (32%)
  starting transfers between devices  19 us (17%)
    pallas_call x1, Pallas kernels, body(): pl.pallas_call(pair_kernel, out_shape=(planes(3),) * 4, in_specs=[SM] + [...  45.9 us
    ppermute x4, waiting for transfers between devices, passed_along(): lax.ppermute(value, 'gy', [(s, (s + step_y) % ny) for s in range(ny)])  21.7 us
    ppermute x4, starting transfers between devices, passed_along(): lax.ppermute(value, 'gy', [(s, (s + step_y) % ny) for s in range(ny)])  13.5 us
    ppermute x6, waiting for transfers between devices, passed_along(): lax.ppermute(value, 'gx', [(s, (s + step_x) % nx) for s in range(nx)])  13.3 us
    ppermute x6, starting transfers between devices, passed_along(): lax.ppermute(value, 'gx', [(s, (s + step_x) % nx) for s in range(nx)])  5.57 us
    pallas_call x1, Pallas kernels, body(): pl.pallas_call(pack_kernel, out_shape=(planes(3, 24), planes(3, 24), plan...  3.21 us
    pallas_call x1, Pallas kernels, body(): pl.pallas_call(stay_kernel, out_shape=(planes(10), jax.ShapeDtypeStruct((...  2.43 us
  transfers between devices with their start and end apart: 10, of which 6 were waited for; matrix products, arithmetic and copies ran while one was open for 0% of the time, Pallas kernels for 2%

profile of v8, /device:TPU:96, one launch (start us, length us, event | category | flops | bytes accessed | tf_op | source)
XLA Modules:
  0.0 109.0 jit_solution(9232828258256670873)
XLA Ops:
  0.7 3.2 %pack.1 = (f32[3,24,128]{2,1,0:T(8,128)}, f32[3,24,128]{2,1,0:T(8,128)}, f32[2,24,128]{2,1,0:T(8,128)}) custom-call(s32[128]{0:T(128)} %bitcast.27, f32[3,128,128]{2,1,0:T(8,128)} %bitcast.15, f32[3,128,128]{2,1,0:T(8,128)} %bitcast.17, f32[128,128]{1,0:T(8,128)} %bitcast.19, f32[128,128]{1,0:T(8,128)} %bitcast.21, f32[128,128]{1,0:T(8,128)} %bitcast.23, ...), custom_call_target="tpu_custom_call" | custom-call | tf_op jit(solution)/shard_map/pack/pallas_call | solution.py:293
  3.9 0.0 copy-start.7
  3.9 0.1 collective-permute-start
  4.0 0.0 copy-start.6
  4.0 3.8 %collective-permute-start.1 = (f32[3,24,128]{2,1,0:T(8,128)}, f32[3,24,128]{2,1,0:T(8,128)S(1)}, u32[]{:S(2)}, u32[]{:S(2)}) collective-permute-start(f32[3,24,128]{2,1,0:T(8,128)} %get-tuple-element.22), channel_id=1, source_target_pairs={{0,240},{16,0},{32,16},{48,32},{64,48},{80,64},{96,80},{112,96},{1... | collective-permute-start | bytes 110600 | tf_op jit(solution)/shard_map/ppermute | solution.py:23
  7.9 0.0 copy-done
  7.9 0.0 copy-done.4
  7.9 0.0 copy-done.5
  7.9 0.0 copy-done.7
  7.9 2.4 %stay.1 = (f32[10,144,128]{2,1,0:T(8,128)S(1)}, s32[1]{0:T(128)}) custom-call(s32[128]{0:T(128)S(1)} %bitcast.28, f32[3,128,128]{2,1,0:T(8,128)S(1)} %bitcast.16, f32[3,128,128]{2,1,0:T(8,128)S(1)} %bitcast.18, f32[128,128]{1,0:T(8,128)S(1)} %bitcast.20, f32[128,128]{1,0:T(8,128)S(1)} %bitcast.22, f32[128,128]{1,0:T(8,128)S(1)} %bitcast.24, ...), custom_call_target="tpu_custom_call" | custom-call | bytes 6000000 | tf_op jit(solution)/shard_map/stay/pallas_call | solution.py:305
  10.3 0.0 collective-permute-done.left.refs_0_
  10.3 0.0 collective-permute-done.1.right.refs_1_
  10.4 0.6 turn.1
  11.0 3.2 %collective-permute-start.2 = (f32[3,24,128]{2,1,0:T(8,128)S(1)}, f32[3,24,128]{2,1,0:T(8,128)S(1)}, u32[]{:S(2)}, u32[]{:S(2)}) collective-permute-start(f32[3,24,128]{2,1,0:T(8,128)S(1)} %get-tuple-element.24), channel_id=1, source_target_pairs={{0,1},{1,2},{2,3},{3,4},{4,5},{5,6},{6,7},{7,8},{8,9},{9,10},{10,1... | collective-permute-start | bytes 110600 | tf_op jit(solution)/shard_map/ppermute | solution.py:25
  14.2 1.3 %collective-permute-start.3 = (f32[3,24,128]{2,1,0:T(8,128)S(1)}, f32[3,24,128]{2,1,0:T(8,128)S(1)}, u32[]{:S(2)}, u32[]{:S(2)}) collective-permute-start(f32[3,24,128]{2,1,0:T(8,128)S(1)} %get-tuple-element.25), channel_id=1, source_target_pairs={{0,15},{1,0},{2,1},{3,2},{4,3},{5,4},{6,5},{7,6},{8,7},{9,8},{10,9... | collective-permute-start | bytes 110600 | tf_op jit(solution)/shard_map/ppermute | solution.py:25
  15.5 2.0 %collective-permute-done.2.refs_2_ = f32[3,24,128]{2,1,0:T(8,128)S(1)} collective-permute-done((f32[3,24,128]{2,1,0:T(8,128)S(1)}, f32[3,24,128]{2,1,0:T(8,128)S(1)}, u32[]{:S(2)}, u32[]{:S(2)}) %collective-permute-start.2) | collective-permute-done | bytes 36896 | tf_op jit(solution)/shard_map/ppermute | solution.py:25
  17.5 2.1 %collective-permute-done.3.refs_3_ = f32[3,24,128]{2,1,0:T(8,128)S(1)} collective-permute-done((f32[3,24,128]{2,1,0:T(8,128)S(1)}, f32[3,24,128]{2,1,0:T(8,128)S(1)}, u32[]{:S(2)}, u32[]{:S(2)}) %collective-permute-start.3) | collective-permute-done | bytes 36896 | tf_op jit(solution)/shard_map/ppermute | solution.py:25
  19.6 0.8 arrive.1
  20.5 2.3 %collective-permute-start.5 = (f32[6,144,128]{2,1,0:T(8,128)S(1)}, f32[6,144,128]{2,1,0:T(8,128)S(1)}, u32[]{:S(2)}, u32[]{:S(2)}) collective-permute-start(f32[6,144,128]{2,1,0:T(8,128)S(1)} %get-tuple-element.26.home.coords), channel_id=1, source_target_pairs={{0,15},{1,0},{2,1},{3,2},{4,3},{5,4},{6,5},{7,6},{8,7},{9,8},{10,9... | collective-permute-start | bytes 1327112 | tf_op jit(solution)/shard_map/ppermute | solution.py:25
  22.8 1.5 %collective-permute-start.4 = (f32[6,144,128]{2,1,0:T(8,128)S(1)}, f32[6,144,128]{2,1,0:T(8,128)S(1)}, u32[]{:S(2)}, u32[]{:S(2)}) collective-permute-start(f32[6,144,128]{2,1,0:T(8,128)S(1)} %get-tuple-element.26.home.coords), channel_id=1, source_target_pairs={{0,240},{16,0},{32,16},{48,32},{64,48},{80,64},{96,80},{112,96},{1... | collective-permute-start | bytes 1327112 | tf_op jit(solution)/shard_map/ppermute | solution.py:23
  24.3 14.2 %collective-permute-done.5.north = f32[6,144,128]{2,1,0:T(8,128)S(1)} collective-permute-done((f32[6,144,128]{2,1,0:T(8,128)S(1)}, f32[6,144,128]{2,1,0:T(8,128)S(1)}, u32[]{:S(2)}, u32[]{:S(2)}) %collective-permute-start.5) | collective-permute-done | bytes 442400 | tf_op jit(solution)/shard_map/ppermute | solution.py:25
  38.4 0.0 collective-permute-start.6
  38.5 0.0 collective-permute-done.4.east
  38.5 5.7 %collective-permute-done.6.corner = f32[6,144,128]{2,1,0:T(8,128)S(1)} collective-permute-done((f32[6,144,128]{2,1,0:T(8,128)S(1)}, f32[6,144,128]{2,1,0:T(8,128)S(1)}, u32[]{:S(2)}, u32[]{:S(2)}) %collective-permute-start.6) | collective-permute-done | bytes 442400 | tf_op jit(solution)/shard_map/ppermute | solution.py:23
  44.3 45.9 %pair.1 = (f32[3,144,128]{2,1,0:T(8,128)S(1)}, f32[3,144,128]{2,1,0:T(8,128)S(1)}, f32[3,144,128]{2,1,0:T(8,128)S(1)}, f32[3,144,128]{2,1,0:T(8,128)S(1)}) custom-call(s32[4608]{0:T(1024)S(1)} %reshape.43.tiles, f32[6,144,128]{2,1,0:T(8,128)S(1)} %get-tuple-element.26.home.coords, f32[6,144,128]{2,1,0:T(8,128)S(1)} %collective-permute-done.4.east, ...), custom_call_target="tpu_custom_call" | custom-call | tf_op jit(solution)/shard_map/pair/pallas_call | solution.py:337
  90.2 0.1 collective-permute-start.8
  90.3 0.1 collective-permute-start.7
  90.4 7.5 %collective-permute-done.8 = f32[3,144,128]{2,1,0:T(8,128)S(1)} collective-permute-done((f32[3,144,128]{2,1,0:T(8,128)S(1)}, f32[3,144,128]{2,1,0:T(8,128)S(1)}, u32[]{:S(2)}, u32[]{:S(2)}) %collective-permute-start.8) | collective-permute-done | bytes 221216 | tf_op jit(solution)/shard_map/ppermute | solution.py:23
  98.0 6.6 %collective-permute-start.9 = (f32[3,144,128]{2,1,0:T(8,128)S(1)}, f32[3,144,128]{2,1,0:T(8,128)S(1)}, u32[]{:S(2)}, u32[]{:S(2)}) collective-permute-start(f32[3,144,128]{2,1,0:T(8,128)S(1)} %add.3), channel_id=1, source_target_pairs={{0,1},{1,2},{2,3},{3,4},{4,5},{5,6},{6,7},{7,8},{8,9},{9,10},{10,1... | collective-permute-start | bytes 663560 | tf_op jit(solution)/shard_map/ppermute | solution.py:25
  104.6 0.0 collective-permute-done.7.east
  104.6 3.4 %collective-permute-done.9.north = f32[3,144,128]{2,1,0:T(8,128)S(1)} collective-permute-done((f32[3,144,128]{2,1,0:T(8,128)S(1)}, f32[3,144,128]{2,1,0:T(8,128)S(1)}, u32[]{:S(2)}, u32[]{:S(2)}) %collective-permute-start.9) | collective-permute-done | bytes 221216 | tf_op jit(solution)/shard_map/ppermute | solution.py:25
  108.1 0.9 update.1
  (16 shorter events, 0.1 us)
Async XLA Ops:
  0.6 7.2 %copy-start = (f32[3,1,1,16384]{3,2,1,0:T(1,128)S(1)}, f32[3,1,1,16384]{3,2,1,0:T(1,128)}, u32[]{:S(2)}) copy-start(f32[3,1,1,16384]{3,2,1,0:T(1,128)} %param.8) | copy-start | bytes 589828
  0.6 7.2 %copy-start.1 = (f32[3,1,1,16384]{3,2,1,0:T(1,128)S(1)}, f32[3,1,1,16384]{3,2,1,0:T(1,128)}, u32[]{:S(2)}) copy-start(f32[3,1,1,16384]{3,2,1,0:T(1,128)} %param.9) | copy-start | bytes 589828
  0.7 7.2 %copy-start.2 = (f32[1,1,16384]{2,1,0:T(1,128)S(1)}, f32[1,1,16384]{2,1,0:T(1,128)}, u32[]{:S(2)}) copy-start(f32[1,1,16384]{2,1,0:T(1,128)} %param.10) | copy-start | bytes 196612
  0.7 7.2 %copy-start.3 = (f32[1,1,16384]{2,1,0:T(1,128)S(1)}, f32[1,1,16384]{2,1,0:T(1,128)}, u32[]{:S(2)}) copy-start(f32[1,1,16384]{2,1,0:T(1,128)} %param.11) | copy-start | bytes 196612
  0.7 7.2 %copy-start.4 = (f32[1,1,16384]{2,1,0:T(1,128)S(1)}, f32[1,1,16384]{2,1,0:T(1,128)}, u32[]{:S(2)}) copy-start(f32[1,1,16384]{2,1,0:T(1,128)} %param.12) | copy-start | bytes 196612
  0.7 7.2 %copy-start.5 = (f32[1,1,16384]{2,1,0:T(1,128)S(1)}, f32[1,1,16384]{2,1,0:T(1,128)}, u32[]{:S(2)}) copy-start(f32[1,1,16384]{2,1,0:T(1,128)} %param.13) | copy-start | bytes 196612
  3.9 4.0 %copy-start.7 = (s32[1,1,128]{2,1,0:T(1,128)S(1)}, s32[1,1,128]{2,1,0:T(1,128)}, u32[]{:S(2)}) copy-start(s32[1,1,128]{2,1,0:T(1,128)} %param.14) | copy-start | bytes 1540
  3.9 6.4 %collective-permute-start = (f32[3,24,128]{2,1,0:T(8,128)}, f32[3,24,128]{2,1,0:T(8,128)S(1)}, u32[]{:S(2)}, u32[]{:S(2)}) collective-permute-start(f32[3,24,128]{2,1,0:T(8,128)} %get-tuple-element.21), channel_id=1, source_target_pairs={{0,16},{16,32},{32,48},{48,64},{64,80},{80,96},{96,112},{112,128},... | collective-permute-start | bytes 110600 | tf_op jit(solution)/shard_map/ppermute | solution.py:23
  4.0 6.3 %copy-start.6 = (f32[2,24,128]{2,1,0:T(8,128)S(1)}, f32[2,24,128]{2,1,0:T(8,128)}, u32[]{:S(2)}) copy-start(f32[2,24,128]{2,1,0:T(8,128)} %get-tuple-element.23.own) | copy-start | bytes 73732
  4.0 6.3 %collective-permute-start.1 = (f32[3,24,128]{2,1,0:T(8,128)}, f32[3,24,128]{2,1,0:T(8,128)S(1)}, u32[]{:S(2)}, u32[]{:S(2)}) collective-permute-start(f32[3,24,128]{2,1,0:T(8,128)} %get-tuple-element.22), channel_id=1, source_target_pairs={{0,240},{16,0},{32,16},{48,32},{64,48},{80,64},{96,80},{112,96},{1... | collective-permute-start | bytes 110600 | tf_op jit(solution)/shard_map/ppermute | solution.py:23
  11.0 6.5 %collective-permute-start.2 = (f32[3,24,128]{2,1,0:T(8,128)S(1)}, f32[3,24,128]{2,1,0:T(8,128)S(1)}, u32[]{:S(2)}, u32[]{:S(2)}) collective-permute-start(f32[3,24,128]{2,1,0:T(8,128)S(1)} %get-tuple-element.24), channel_id=1, source_target_pairs={{0,1},{1,2},{2,3},{3,4},{4,5},{5,6},{6,7},{7,8},{8,9},{9,10},{10,1... | collective-permute-start | bytes 110600 | tf_op jit(solution)/shard_map/ppermute | solution.py:25
  14.2 5.5 %collective-permute-start.3 = (f32[3,24,128]{2,1,0:T(8,128)S(1)}, f32[3,24,128]{2,1,0:T(8,128)S(1)}, u32[]{:S(2)}, u32[]{:S(2)}) collective-permute-start(f32[3,24,128]{2,1,0:T(8,128)S(1)} %get-tuple-element.25), channel_id=1, source_target_pairs={{0,15},{1,0},{2,1},{3,2},{4,3},{5,4},{6,5},{7,6},{8,7},{9,8},{10,9... | collective-permute-start | bytes 110600 | tf_op jit(solution)/shard_map/ppermute | solution.py:25
  19.6 18.8 %copy-start.8 = (s32[1,1,2304,2]{2,3,1,0:T(2,128)S(1)}, s32[1,1,2304,2]{2,3,1,0:T(2,128)}, u32[]{:S(2)}) copy-start(s32[1,1,2304,2]{2,3,1,0:T(2,128)} %param.15) | copy-start | bytes 55300
  20.5 18.0 %collective-permute-start.5 = (f32[6,144,128]{2,1,0:T(8,128)S(1)}, f32[6,144,128]{2,1,0:T(8,128)S(1)}, u32[]{:S(2)}, u32[]{:S(2)}) collective-permute-start(f32[6,144,128]{2,1,0:T(8,128)S(1)} %get-tuple-element.26.home.coords), channel_id=1, source_target_pairs={{0,15},{1,0},{2,1},{3,2},{4,3},{5,4},{6,5},{7,6},{8,7},{9,8},{10,9... | collective-permute-start | bytes 1327112 | tf_op jit(solution)/shard_map/ppermute | solution.py:25
  22.8 15.7 %collective-permute-start.4 = (f32[6,144,128]{2,1,0:T(8,128)S(1)}, f32[6,144,128]{2,1,0:T(8,128)S(1)}, u32[]{:S(2)}, u32[]{:S(2)}) collective-permute-start(f32[6,144,128]{2,1,0:T(8,128)S(1)} %get-tuple-element.26.home.coords), channel_id=1, source_target_pairs={{0,240},{16,0},{32,16},{48,32},{64,48},{80,64},{96,80},{112,96},{1... | collective-permute-start | bytes 1327112 | tf_op jit(solution)/shard_map/ppermute | solution.py:23
  38.4 5.8 %collective-permute-start.6 = (f32[6,144,128]{2,1,0:T(8,128)S(1)}, f32[6,144,128]{2,1,0:T(8,128)S(1)}, u32[]{:S(2)}, u32[]{:S(2)}) collective-permute-start(f32[6,144,128]{2,1,0:T(8,128)S(1)} %collective-permute-done.5.north), channel_id=1, source_target_pairs={{0,240},{16,0},{32,16},{48,32},{64,48},{80,64},{96,80},{112,96},{1... | collective-permute-start | bytes 1327112 | tf_op jit(solution)/shard_map/ppermute | solution.py:23
  90.2 7.7 %collective-permute-start.8 = (f32[3,144,128]{2,1,0:T(8,128)S(1)}, f32[3,144,128]{2,1,0:T(8,128)S(1)}, u32[]{:S(2)}, u32[]{:S(2)}) collective-permute-start(f32[3,144,128]{2,1,0:T(8,128)S(1)} %get-tuple-element.30), channel_id=1, source_target_pairs={{0,16},{16,32},{32,48},{48,64},{64,80},{80,96},{96,112},{112,128},... | collective-permute-start | bytes 663560 | tf_op jit(solution)/shard_map/ppermute | solution.py:23
  90.3 14.3 %collective-permute-start.7 = (f32[3,144,128]{2,1,0:T(8,128)S(1)}, f32[3,144,128]{2,1,0:T(8,128)S(1)}, u32[]{:S(2)}, u32[]{:S(2)}) collective-permute-start(f32[3,144,128]{2,1,0:T(8,128)S(1)} %get-tuple-element.28), channel_id=1, source_target_pairs={{0,16},{16,32},{32,48},{48,64},{64,80},{80,96},{96,112},{112,128},... | collective-permute-start | bytes 663560 | tf_op jit(solution)/shard_map/ppermute | solution.py:23
  98.0 10.1 %collective-permute-start.9 = (f32[3,144,128]{2,1,0:T(8,128)S(1)}, f32[3,144,128]{2,1,0:T(8,128)S(1)}, u32[]{:S(2)}, u32[]{:S(2)}) collective-permute-start(f32[3,144,128]{2,1,0:T(8,128)S(1)} %add.3), channel_id=1, source_target_pairs={{0,1},{1,2},{2,3},{3,4},{4,5},{5,6},{6,7},{7,8},{8,9},{9,10},{10,1... | collective-permute-start | bytes 663560 | tf_op jit(solution)/shard_map/ppermute | solution.py:25
